TPU v7x, 32 devices: a whole 2x2x4 slice. The times are simulated.
32 devices in a mesh: ctx: 8 (over z, y), tp: 2 (over x), probe: 2 (over core).
Axes of the slice: x: 2, y: 2, z: 4, core: 2. Of those that a mesh axis runs over, the one named last changes fastest.
Arguments:
- latent: float32 [1024, 3072], P('ctx', 'tp'), may hold values from -6 to 6
- probes: int32 [2, 1024, 3072], P('probe', 'ctx', 'tp'), may hold values from 0 to 1
- modulation: float32 [2, 3, 3072], replicated, may hold values from -3 to 3
- pattern: int32 [8, 8], P('ctx'), may hold values from 0 to 7, as said below
- w_qkv: bfloat16 [3072, 3, 3072], P(None, None, 'tp'), may hold values from -0.109375 to 0.109375
- w_out: bfloat16 [3072, 3072], P('tp'), may hold values from -0.109375 to 0.109375
- w_up: bfloat16 [3072, 6144], P('ctx', 'tp'), may hold values from -0.109375 to 0.109375
- w_down: bfloat16 [6144, 3072], P('tp', 'ctx'), may hold values from -0.078125 to 0.078125
- q_gain: float32 [3072], P('tp'), may hold values from 0.5 to 5.1, as said below
- k_gain: float32 [3072], P('tp'), may hold values from 0.5 to 2
Outputs:
- latent_out: float32 [1024, 3072], P('ctx', 'tp')
- density_change: float32 [1024], P('ctx')
Inputs may be any that keep to these rules, and one draw needn't show every extreme that they name: `pattern`: row q lists key blocks for query block q: its first entry is q; the next entries are distinct blocks other than q up to a count of 1 to 8, after which every entry is q again; row 0 lists 8 distinct blocks. `q_gain`: positive gains.
All inputs are finite; a program needn't handle non-finite values.
Results may differ from a plain program's by a relative error of at most 0.034.
Values may be sent and summed in bfloat16 or wider, within the bound.
No kernel may reach another device: no remote copies, remote signals or barrier semaphores. Data moves between devices by JAX's collectives and lax.ppermute only.
A program may use at most 192 MiB of HBM per device.

v0:
```python
from functools import partial
import math

import jax
import jax.numpy as jnp
from jax import lax
from jax.sharding import PartitionSpec as P

HD = 128
BLK = 128
K_SEL = 8
STEPS = 2


EPS = 1e-06
NEG_BIG = -1e30


def norm_features(rows, tangent, shift, stretch, full_width):
    row_sums = jnp.stack(
        [jnp.sum(rows, 1), jnp.sum(rows * rows, 1), jnp.sum(tangent, 1), jnp.sum(rows * tangent, 1)]
    )
    totals = lax.psum(row_sums, "tp")
    row_mean = totals[0][:, None] / full_width
    row_var = totals[1][:, None] / full_width - row_mean * row_mean
    tan_mean = totals[2][:, None] / full_width
    tan_var = 2.0 * (totals[3][:, None] / full_width - row_mean * tan_mean)
    inv_std = lax.rsqrt(row_var + EPS)
    centred = rows - row_mean
    normed = centred * inv_std
    tan_normed = (
        tangent - tan_mean
    ) * inv_std - 0.5 * centred * inv_std * inv_std * inv_std * tan_var
    normed_act = (normed * (1.0 + stretch) + shift).astype(jnp.bfloat16)
    tangent_act = (tan_normed * (1.0 + stretch)).astype(jnp.bfloat16)
    return (
        lax.all_gather(normed_act, "tp", axis=1, tiled=True),
        lax.all_gather(tangent_act, "tp", axis=1, tiled=True),
    )


def head_rms(projected, tan_projected, head_gain):
    row_count = projected.shape[0]
    heads_local = head_gain.shape[0] // HD
    head_view = projected.reshape(row_count, heads_local, HD)
    tan_view = tan_projected.reshape(row_count, heads_local, HD)
    gain_view = head_gain.reshape(heads_local, HD)
    inv_std = lax.rsqrt(jnp.mean(head_view * head_view, axis=-1, keepdims=True) + EPS)
    tan_inv = -inv_std * inv_std * inv_std * jnp.mean(head_view * tan_view, axis=-1, keepdims=True)
    result = (head_view * inv_std * gain_view).astype(jnp.bfloat16)
    tan_result = ((tan_view * inv_std + head_view * tan_inv) * gain_view).astype(jnp.bfloat16)
    return (result, tan_result)


def empty_carry(heads_local, row_count):
    return (
        jnp.full((heads_local, row_count), NEG_BIG, jnp.float32),
        jnp.zeros((heads_local, row_count), jnp.float32),
        jnp.zeros((heads_local, row_count, HD), jnp.float32),
        jnp.zeros((heads_local, row_count, HD), jnp.float32),
        jnp.zeros((heads_local, row_count), jnp.float32),
    )


def attend(state_carry, query, key_set, allowed):
    running_max, run_total, run_acc, tan_acc, tan_sum = state_carry
    q_rows, dq_rows = query
    k_rows, v_rows, dk_rows, dv_rows = key_set
    score_scale = 1.0 / math.sqrt(q_rows.shape[2])
    scores = (
        jnp.einsum("qhd,khd->hqk", q_rows, k_rows, preferred_element_type=jnp.float32) * score_scale
    )
    tan_scores = (
        jnp.einsum("qhd,khd->hqk", dq_rows, k_rows, preferred_element_type=jnp.float32)
        + jnp.einsum("qhd,khd->hqk", q_rows, dk_rows, preferred_element_type=jnp.float32)
    ) * score_scale
    key_mask = allowed[None, :, :]
    scores = jnp.where(key_mask, scores, NEG_BIG)
    new_max = jnp.maximum(running_max, jnp.max(scores, axis=2))
    weights = jnp.where(key_mask, jnp.exp(scores - new_max[:, :, None]), 0.0)
    values = v_rows.astype(jnp.float32)
    tan_values = dv_rows.astype(jnp.float32)
    weighted_ds = weights * tan_scores
    run_total = jnp.sum(weights, axis=2)
    run_acc = jnp.einsum("hqk,khd->hqd", weights, values, precision=lax.Precision.HIGHEST)
    tan_acc = jnp.einsum(
        "hqk,khd->hqd", weights, tan_values, precision=lax.Precision.HIGHEST
    ) + jnp.einsum("hqk,khd->hqd", weighted_ds, values, precision=lax.Precision.HIGHEST)
    tan_sum = jnp.sum(weighted_ds, axis=2)
    return (new_max, run_total, run_acc, tan_acc, tan_sum)


def finish(state_carry):
    running_max, run_total, run_acc, tan_acc, tan_sum = state_carry
    output = run_acc / run_total[:, :, None]
    tan_output = tan_acc / run_total[:, :, None] - (tan_sum / run_total)[:, :, None] * output
    heads_local, row_count, head_size = output.shape
    output = (
        output.transpose(1, 0, 2).reshape(row_count, heads_local * head_size).astype(jnp.bfloat16)
    )
    tan_output = (
        tan_output.transpose(1, 0, 2)
        .reshape(row_count, heads_local * head_size)
        .astype(jnp.bfloat16)
    )
    return (output, tan_output)


def select_blocks(whole_rows, chosen, block_total, heads_local):
    blocked = whole_rows.reshape(block_total, BLK, heads_local * HD)
    return jnp.take(blocked, chosen, axis=0).reshape(K_SEL * BLK, heads_local, HD)


def listed_attention(q_rows, dq_rows, whole_set, pattern, block_total, heads_local):
    chosen = pattern[0]
    valid_cols = (jnp.arange(K_SEL) == 0) | (chosen != chosen[0])
    allowed = jnp.broadcast_to(jnp.repeat(valid_cols, BLK)[None, :], (BLK, K_SEL * BLK))
    key_set = tuple(
        (select_blocks(member, chosen, block_total, heads_local) for member in whole_set)
    )
    query = (q_rows[0:BLK], dq_rows[0:BLK])
    block_out, block_tan = finish(attend(empty_carry(heads_local, BLK), query, key_set, allowed))
    return (block_out, block_tan)


def local(latent, probes, modulation, pattern, w_qkv, w_out, w_up, w_down, q_gain, k_gain):
    row_count, local_width = latent.shape
    full_width = local_width * lax.axis_size("tp")
    feature_start = lax.axis_index("tp") * local_width
    heads_local = q_gain.shape[0] // HD
    block_total = row_count * lax.axis_size("ctx") // BLK
    step_size = 1.0 / STEPS
    probe_signs = 2.0 * probes[0].astype(jnp.float32) - 1.0
    up_full, down_full = (
        lax.all_gather(w_up, "ctx", axis=0, tiled=True),
        lax.all_gather(w_down, "ctx", axis=1, tiled=True),
    )
    gelu_tanh = partial(jax.nn.gelu, approximate=True)
    change = jnp.zeros((row_count,), jnp.float32)
    for euler_step in range(STEPS):
        mod_local = lax.dynamic_slice_in_dim(modulation[euler_step], feature_start, local_width, 1)
        normed_act, tangent_act = norm_features(
            latent, probe_signs, mod_local[0], mod_local[1], full_width
        )
        stacked = jnp.concatenate([normed_act, tangent_act], axis=0)
        projected = jnp.einsum("rd,dcf->crf", stacked, w_qkv, preferred_element_type=jnp.float32)
        q_rows, dq_rows = head_rms(projected[0, :row_count], projected[0, row_count:], q_gain)
        k_heads, dk_heads = head_rms(projected[1, :row_count], projected[1, row_count:], k_gain)
        k_rows = k_heads.reshape(row_count, heads_local * HD)
        dk_rows = dk_heads.reshape(row_count, heads_local * HD)
        v_rows = projected[2, :row_count].astype(jnp.bfloat16)
        dv_rows = projected[2, row_count:].astype(jnp.bfloat16)
        k_whole, v_whole, dk_whole, dv_whole = (
            lax.all_gather(k_rows, "ctx", axis=0, tiled=True),
            lax.all_gather(v_rows, "ctx", axis=0, tiled=True),
            lax.all_gather(dk_rows, "ctx", axis=0, tiled=True),
            lax.all_gather(dv_rows, "ctx", axis=0, tiled=True),
        )
        attended, tan_attended = listed_attention(
            q_rows,
            dq_rows,
            (k_whole, v_whole, dk_whole, dv_whole),
            pattern,
            block_total,
            heads_local,
        )
        pre_hidden = jnp.dot(stacked, up_full, preferred_element_type=jnp.float32)
        hidden, tan_hidden = jax.jvp(
            gelu_tanh, (pre_hidden[:row_count],), (pre_hidden[row_count:],)
        )
        attn_rows = jnp.concatenate([attended, tan_attended], axis=0)
        mlp_rows = jnp.concatenate(
            [hidden.astype(jnp.bfloat16), tan_hidden.astype(jnp.bfloat16)], axis=0
        )
        partials = jnp.dot(attn_rows, w_out, preferred_element_type=jnp.float32) + jnp.dot(
            mlp_rows, down_full, preferred_element_type=jnp.float32
        )
        summed = lax.psum_scatter(
            partials.astype(jnp.bfloat16), "tp", scatter_dimension=1, tiled=True
        ).astype(jnp.float32)
        speed = mod_local[2] * summed[:row_count]
        tan_speed = mod_local[2] * summed[row_count:]
        change = change + jnp.sum(probe_signs * tan_speed, axis=1)
        latent = latent + step_size * speed
    total_change = lax.psum(change, ("tp", "probe"))
    density_change = -step_size * total_change / (lax.axis_size("probe") * math.sqrt(full_width))
    return (latent, density_change)


def solution(mesh):
    return jax.shard_map(
        local,
        mesh=mesh,
        in_specs=(
            P("ctx", "tp"),
            P("probe", "ctx", "tp"),
            P(),
            P("ctx", None),
            P(None, None, "tp"),
            P("tp", None),
            P("ctx", "tp"),
            P("tp", "ctx"),
            P("tp"),
            P("tp"),
        ),
        out_specs=(P("ctx", "tp"), P("ctx")),
        check_vma=False,
    )
```

profile of v0, /device:TPU:0, one launch (start us, length us, event | category | flops | bytes accessed | tf_op | source)
XLA Modules:
  0.0 1486.4 jit_solution(8071988486946177803)
XLA Ops:
  10.3 5.8 psum.21
  17.9 10.7 all_gather.42
  28.6 9.7 all_gather.43
  38.4 15.6 %fusion.145 = (bf16[3,256,1536]{2,1,0:T(8,128)(2,1)S(1)}, f32[3,256,1536]{2,1,0:T(8,128)}) fusion(bf16[3072,3,1536]{2,0,1:T(8,128)(2,1)} %param.16, bf16[256,3072]{1,0:T(8,128)(2,1)S(1)} %constant_dynamic-update-slice_fusion), kind=kOutput, calls=%fused_computation.245 | convolution fusion | flops 7248936960 | bytes 36962304 | tf_op jit(solution)/shard_map/rd,dcf->crf/dot_general | solution.py:146
  62.2 2.9 fusion.79
  68.1 48.7 %all-gather.27.cloned.1.call-done = bf16[1,1024,1536]{2,1,0:T(8,128)(2,1)} async-done(((bf16[1,128,1536]{2,1,0:T(8,128)(2,1)}), bf16[1,1024,1536]{2,1,0:T(8,128)(2,1)}) %all-gather.27.cloned.1.call-update) | async-done | bytes 3145744 | tf_op jit(solution)/shard_map/all_gather | solution.py:155
  116.8 4.3 gather_fusion.1
  121.1 56.9 %all-gather.29.cloned.1.call-done = bf16[1,1024,1536]{2,1,0:T(8,128)(2,1)} async-done(((bf16[1,128,1536]{2,1,0:T(8,128)(2,1)}), bf16[1,1024,1536]{2,1,0:T(8,128)(2,1)}) %all-gather.29.cloned.1.call-update) | async-done | bytes 3145744 | tf_op jit(solution)/shard_map/all_gather | solution.py:157
  178.1 4.3 gather_fusion.2
  182.4 57.0 %all-gather.17.cloned.1.call-done = bf16[1024,1536]{1,0:T(8,128)(2,1)} async-done(((bf16[128,1536]{1,0:T(8,128)(2,1)}), bf16[1024,1536]{1,0:T(8,128)(2,1)}) %all-gather.17.cloned.1.call-update) | async-done | bytes 3145744 | tf_op jit(solution)/shard_map/all_gather | solution.py:156
  239.4 4.3 gather_fusion.3
  243.7 56.8 %all-gather.15.cloned.1.call-done = bf16[1024,1536]{1,0:T(8,128)(2,1)} async-done(((bf16[128,1536]{1,0:T(8,128)(2,1)}), bf16[1024,1536]{1,0:T(8,128)(2,1)}) %all-gather.15.cloned.1.call-update) | async-done | bytes 3145744 | tf_op jit(solution)/shard_map/all_gather | solution.py:154
  300.5 4.4 gather_fusion
  304.9 8.3 broadcast_select_fusion.6
  313.2 3.8 copy.63
  317.1 3.4 reshape.367
  320.4 5.0 copy.59
  325.4 4.1 reshape.363
  329.6 6.9 reshape.476
  336.5 5.0 copy.62
  341.5 5.8 reshape.365
  347.3 2.8 fusion
  353.6 6.1 fusion.146
  359.8 6.8 fusion.92
  366.6 5.0 fusion.147
  371.6 3.2 fusion.55
  374.9 4.5 fusion.64
  379.4 283.6 %all-gather.19.cloned.1.call-done = bf16[3072,3072]{1,0:T(8,128)(2,1)} async-done(((bf16[384,3072]{1,0:T(8,128)(2,1)}), bf16[3072,3072]{1,0:T(8,128)(2,1)}) %all-gather.19.cloned.1.call-update) | async-done | bytes 18874384 | tf_op jit(solution)/shard_map/all_gather | solution.py:135
  663.0 9.0 fusion.151
  674.3 352.6 %all-gather.21.cloned.1.call-done = bf16[3072,3072]{1,0:T(8,128)(2,1)} async-done(((bf16[3072,384]{1,0:T(8,128)(2,1)}), bf16[3072,3072]{1,0:T(8,128)(2,1)}) %all-gather.21.cloned.1.call-update) | async-done | bytes 18874384 | tf_op jit(solution)/shard_map/all_gather | solution.py:136
  1026.9 10.4 fusion.2
  1037.4 26.1 %reduce-scatter.3.cloned.1.call-done = bf16[256,1536]{1,0:T(8,128)(2,1)} async-done(((bf16[256,3072]{1,0:T(8,128)(2,1)}), bf16[256,1536]{1,0:T(8,128)(2,1)}) %reduce-scatter.3.cloned.1.call-update) | async-done | bytes 786448 | tf_op jit(solution)/shard_map/reduce_scatter | solution.py:178
  1066.0 5.2 psum.22
  1071.7 10.4 all_gather.50
  1082.2 9.5 all_gather.51
  1091.7 15.7 %fusion.148 = (bf16[3,256,1536]{2,1,0:T(8,128)(2,1)S(1)}, f32[3,256,1536]{2,1,0:T(8,128)}) fusion(bf16[3072,3,1536]{2,0,1:T(8,128)(2,1)} %param.16, bf16[256,3072]{1,0:T(8,128)(2,1)S(1)} %constant_dynamic-update-slice_fusion.2), kind=kOutput, calls=%fused_computation.248 | convolution fusion | flops 7248936960 | bytes 36962304 | tf_op jit(solution)/shard_map/rd,dcf->crf/dot_general | solution.py:146
  1108.4 3.1 slice_multiply_fusion.4
  1118.9 9.2 fusion.152
  1130.4 38.5 %all-gather.31.cloned.1.call-done = bf16[1,1024,1536]{2,1,0:T(8,128)(2,1)} async-done(((bf16[1,128,1536]{2,1,0:T(8,128)(2,1)}), bf16[1,1024,1536]{2,1,0:T(8,128)(2,1)}) %all-gather.31.cloned.1.call-update) | async-done | bytes 3145744 | tf_op jit(solution)/shard_map/all_gather | solution.py:155
  1168.9 2.6 gather_fusion.5
  1171.5 58.9 %all-gather.23.cloned.1.call-done = bf16[1024,1536]{1,0:T(8,128)(2,1)} async-done(((bf16[128,1536]{1,0:T(8,128)(2,1)}), bf16[1024,1536]{1,0:T(8,128)(2,1)}) %all-gather.23.cloned.1.call-update) | async-done | bytes 3145744 | tf_op jit(solution)/shard_map/all_gather | solution.py:154
  1230.4 4.3 gather_fusion.4
  1234.8 57.0 %all-gather.33.cloned.1.call-done = bf16[1,1024,1536]{2,1,0:T(8,128)(2,1)} async-done(((bf16[1,128,1536]{2,1,0:T(8,128)(2,1)}), bf16[1,1024,1536]{2,1,0:T(8,128)(2,1)}) %all-gather.33.cloned.1.call-update) | async-done | bytes 3145744 | tf_op jit(solution)/shard_map/all_gather | solution.py:157
  1291.8 4.4 gather_fusion.6
  1296.2 57.2 %all-gather.25.cloned.1.call-done = bf16[1024,1536]{1,0:T(8,128)(2,1)} async-done(((bf16[128,1536]{1,0:T(8,128)(2,1)}), bf16[1024,1536]{1,0:T(8,128)(2,1)}) %all-gather.25.cloned.1.call-update) | async-done | bytes 3145744 | tf_op jit(solution)/shard_map/all_gather | solution.py:156
  1353.3 4.3 gather_fusion.7
  1357.6 7.2 broadcast_select_fusion.2
  1364.8 3.8 copy.80
  1368.6 3.4 reshape.375
  1372.0 5.0 copy.76
  1377.0 4.1 reshape.371
  1381.2 2.7 fusion.1
  1388.0 5.6 fusion.94
  1393.7 3.8 fusion.97
  1397.5 7.0 reshape.477
  1404.5 3.4 copy.79
  1407.9 6.1 reshape.373
  1414.1 9.6 fusion.149
  1423.8 4.8 fusion.150
  1428.7 3.2 fusion.54
  1432.0 2.9 fusion.68
  1434.9 10.7 fusion.3
  1445.6 24.9 %reduce-scatter.5.cloned.1.call-done = bf16[256,1536]{1,0:T(8,128)(2,1)} async-done(((bf16[256,3072]{1,0:T(8,128)(2,1)}), bf16[256,1536]{1,0:T(8,128)(2,1)}) %reduce-scatter.5.cloned.1.call-update) | async-done | bytes 786448 | tf_op jit(solution)/shard_map/reduce_scatter | solution.py:178
  1473.1 5.7 psum.23
  (181 shorter events, 42.7 us)
Async XLA Ops:
  7.2 10.2 copy-start.1
  7.2 10.2 copy-start.18
  7.2 109.6 %all-gather.27.cloned.1.call-start = ((), (), s32[]{:S(2)}) async-start(), calls=%async_computation.10 | async-start | bytes 3538944 | tf_op jit(solution)/shard_map/all_gather | solution.py:155
  38.4 15.6 %copy-start.24 = (bf16[256,3072]{1,0:T(8,128)(2,1)}, bf16[256,3072]{1,0:T(8,128)(2,1)S(1)}, u32[]{:S(2)}) copy-start(bf16[256,3072]{1,0:T(8,128)(2,1)S(1)} %constant_dynamic-update-slice_fusion) | copy-start | bytes 4718596
  55.0 123.1 %all-gather.29.cloned.1.call-start = ((), (), s32[]{:S(2)}) async-start(), calls=%async_computation.11 | async-start | bytes 3538944 | tf_op jit(solution)/shard_map/all_gather | solution.py:157
  55.7 183.7 %all-gather.17.cloned.1.call-start = ((), (), s32[]{:S(2)}) async-start(), calls=%async_computation.3 | async-start | bytes 3538944 | tf_op jit(solution)/shard_map/all_gather | solution.py:156
  59.4 2.8 copy-start.34
  65.2 235.4 %all-gather.15.cloned.1.call-start = ((), (), s32[]{:S(2)}) async-start(), calls=%async_computation.2 | async-start | bytes 3538944 | tf_op jit(solution)/shard_map/all_gather | solution.py:154
  65.7 597.3 %all-gather.19.cloned.1.call-start = ((), (), s32[]{:S(2)}) async-start(), calls=%async_computation.4 | async-start | bytes 21233664 | tf_op jit(solution)/shard_map/all_gather | solution.py:135
  66.3 1.5 copy-start.35
  66.3 960.6 %all-gather.21.cloned.1.call-start = ((), (), s32[]{:S(2)}) async-start(), calls=%async_computation.5 | async-start | bytes 21233664 | tf_op jit(solution)/shard_map/all_gather | solution.py:136
  66.9 996.6 %reduce-scatter.3.cloned.1.call-start = ((), (), s32[]{:S(2)}) async-start(), calls=%async_computation.6 | async-start | bytes 2359296 | tf_op jit(solution)/shard_map/reduce_scatter | solution.py:178
  67.5 53.6 %copy-start.7 = (f32[1,128,1536]{1,2,0:T(8,128)}, f32[1,128,1536]{1,2,0:T(8,128)S(1)}, u32[]{:S(2)}) copy-start(f32[1,128,1536]{1,2,0:T(8,128)S(1)} %copy.56) | copy-start | bytes 2359300
  67.8 53.3 %copy-start.14 = (f32[1,128,1536]{1,2,0:T(8,128)}, f32[1,128,1536]{1,2,0:T(8,128)S(1)}, u32[]{:S(2)}) copy-start(f32[1,128,1536]{1,2,0:T(8,128)S(1)} %copy.64) | copy-start | bytes 2359300
  300.5 4.4 copy-start.13
  341.5 5.8 copy-start.33
  347.3 2.8 copy-start.8
  347.3 2.8 copy-start.15
  351.3 2.3 copy-start.9
  359.8 6.8 copy-start.10
  366.5 8.3 slice-start
  366.6 8.3 slice-start.1
  371.6 3.3 slice-start.2
  374.9 288.1 %copy-start.25 = (bf16[256,3072]{1,0:T(8,128)(2,1)S(1)}, bf16[256,3072]{1,0:T(8,128)(2,1)}, u32[]{:S(2)}) copy-start(bf16[256,3072]{1,0:T(8,128)(2,1)} %copy-done.24) | copy-start | bytes 4718596
  672.0 354.9 %copy-start.29 = (f32[256,3072]{1,0:T(8,128)S(1)}, f32[256,3072]{1,0:T(8,128)}, u32[]{:S(2)}) copy-start(f32[256,3072]{1,0:T(8,128)} %fusion.64) | copy-start | bytes 9437188
  1037.3 27.5 %copy-start.2 = (s32[1,128,1536]{2,1,0:T(8,128)S(1)}, s32[1,128,1536]{2,1,0:T(8,128)}, u32[]{:S(2)}) copy-start(s32[1,128,1536]{2,1,0:T(8,128)} %param.13) | copy-start | bytes 2359300
  1037.3 27.5 %copy-start.19 = (f32[128,1536]{1,0:T(8,128)S(1)}, f32[128,1536]{1,0:T(8,128)}, u32[]{:S(2)}) copy-start(f32[128,1536]{1,0:T(8,128)} %param.12) | copy-start | bytes 2359300
  1037.3 131.6 %all-gather.31.cloned.1.call-start = ((), (), s32[]{:S(2)}) async-start(), calls=%async_computation.12 | async-start | bytes 3538944 | tf_op jit(solution)/shard_map/all_gather | solution.py:155
  1064.8 1.2 copy-start.22
  1066.0 25.6 %copy-start.20 = (f32[128,1536]{1,0:T(8,128)}, f32[128,1536]{1,0:T(8,128)S(1)}, u32[]{:S(2)}) copy-start(f32[128,1536]{1,0:T(8,128)S(1)} %get-tuple-element.23) | copy-start | bytes 2359300
  1091.7 15.7 %copy-start.26 = (bf16[256,3072]{1,0:T(8,128)(2,1)}, bf16[256,3072]{1,0:T(8,128)(2,1)S(1)}, u32[]{:S(2)}) copy-start(bf16[256,3072]{1,0:T(8,128)(2,1)S(1)} %constant_dynamic-update-slice_fusion.2) | copy-start | bytes 4718596
  1108.3 122.1 %all-gather.23.cloned.1.call-start = ((), (), s32[]{:S(2)}) async-start(), calls=%async_computation.7 | async-start | bytes 3538944 | tf_op jit(solution)/shard_map/all_gather | solution.py:154
  1115.4 3.5 copy-start.27
  1115.4 176.4 %all-gather.33.cloned.1.call-start = ((), (), s32[]{:S(2)}) async-start(), calls=%async_computation.13 | async-start | bytes 3538944 | tf_op jit(solution)/shard_map/all_gather | solution.py:157
  1116.0 237.3 %all-gather.25.cloned.1.call-start = ((), (), s32[]{:S(2)}) async-start(), calls=%async_computation.8 | async-start | bytes 3538944 | tf_op jit(solution)/shard_map/all_gather | solution.py:156
  1116.7 353.8 %reduce-scatter.5.cloned.1.call-start = ((), (), s32[]{:S(2)}) async-start(), calls=%async_computation.9 | async-start | bytes 2359296 | tf_op jit(solution)/shard_map/reduce_scatter | solution.py:178
  1117.0 11.0 copy-start.4
  1118.7 9.3 copy-start.16
  1383.9 3.2 copy-start
  1383.9 4.2 copy-start.28
  1388.0 5.6 copy-start.5
  1388.0 5.6 copy-start.17
  1397.5 7.0 copy-start.12
  1407.9 6.1 copy-start.6
  1407.9 15.8 %slice-start.6 = ((s8[6291456]{0:T(1024)(128)(4,1)}), s8[2097152]{0:T(1024)(128)(4,1)S(1)}, s32[]{:S(2)}) async-start(s8[6291456]{0:T(1024)(128)(4,1)} %bitcast.230), calls=%async_computation.20 | async-start | bytes 4194304
  1414.1 9.7 slice-start.7
  1414.1 9.7 copy-start.11
  1423.8 4.9 copy-start.32
  1423.8 8.2 slice-start.3
  1423.8 8.2 slice-start.4
  1428.7 3.3 slice-start.5
  1432.0 2.9 copy-start.30
  1432.0 2.9 copy-start.31
  1445.6 26.2 %copy-start.3 = (s32[1,128,1536]{2,1,0:T(8,128)S(1)}, s32[1,128,1536]{2,1,0:T(8,128)}, u32[]{:S(2)}) copy-start(s32[1,128,1536]{2,1,0:T(8,128)} %param.13) | copy-start | bytes 2359300
  1445.6 26.2 %copy-start.21 = (f32[128,1536]{1,0:T(8,128)S(1)}, f32[128,1536]{1,0:T(8,128)}, u32[]{:S(2)}) copy-start(f32[128,1536]{1,0:T(8,128)} %copy-done.20) | copy-start | bytes 2359300
  1445.6 26.2 %copy-start.23 = (f32[256,1536]{1,0:T(8,128)S(1)}, f32[256,1536]{1,0:T(8,128)}, u32[]{:S(2)}) copy-start(f32[256,1536]{1,0:T(8,128)} %copy-done.22) | copy-start | bytes 4718596
Sparse Core Ops, SparseCore 0:
  55.1 61.6 all-gather.26
  119.0 59.0 all-gather.28
  180.3 59.0 all-gather.16
  241.4 59.0 all-gather.14
  301.9 361.0 all-gather.18
  664.4 362.4 all-gather.20
  1037.5 26.0 reduce-scatter.2
  1108.4 60.3 all-gather.30
  1171.3 59.0 all-gather.22
  1232.7 59.0 all-gather.32
  1294.2 59.0 all-gather.24
  1445.7 24.6 reduce-scatter.4
where the time goes:
time: 1490 us
  waiting for transfers between devices  1120 us (75%)
  matrix products  133 us (9%)
  local copies, waits for them, and re-layouts  113 us (8%)
  blocking collectives  57 us (4%)
  other arithmetic  46.2 us (3%)
  between operations  15.4 us (1%)
    all_gather x1, waiting for transfers between devices, local(): lax.all_gather(w_down, 'ctx', axis=1, tiled=True)  353 us
    all_gather x1, waiting for transfers between devices, local(): lax.all_gather(w_up, 'ctx', axis=0, tiled=True)  284 us
    all_gather x2, waiting for transfers between devices, local(): lax.all_gather(k_rows, 'ctx', axis=0, tiled=True)  116 us
    all_gather x2, waiting for transfers between devices, local(): lax.all_gather(dk_rows, 'ctx', axis=0, tiled=True)  114 us
    all_gather x2, waiting for transfers between devices, local(): lax.all_gather(dv_rows, 'ctx', axis=0, tiled=True)  114 us
    all_gather x2, waiting for transfers between devices, local(): lax.all_gather(v_rows, 'ctx', axis=0, tiled=True)  87.2 us
    reduce_scatter x2, waiting for transfers between devices, local(): lax.psum_scatter(partials.astype(jnp.bfloat16), 'tp', scatter_dimension=1...  50.9 us
    reshape x8, local copies, waits for them, and re-layouts, select_blocks(): jnp.take(blocked, chosen, axis=0).reshape(K_SEL * BLK, heads_local, HD)  40.9 us
  transfers between devices with their start and end apart: 12, of which 12 were waited for; matrix products, arithmetic and copies ran while one was open for 10% of the time, Pallas kernels for 0%

commit v1 on v0

v1 whole, which is shorter than its diff:
```python
import math

import jax
import jax.numpy as jnp
from jax import lax
from jax.sharding import PartitionSpec as P

HD = 128
BLK = 128
STEPS = 2
EPS = 1e-06
NEG_BIG = -1e30
F32 = jnp.float32
BF16 = jnp.bfloat16


def dot(a, b):
    return jnp.dot(a, b, preferred_element_type=F32)


def dot_t(a, b):
    return lax.dot_general(a, b, (((1,), (1,)), ((), ())), preferred_element_type=F32)


def cycle_of(size):
    return list(range(0, size, 2)) + list(range(size - 1, 0, -2))


def ring_shift(x, cycle, shift):
    size = len(cycle)
    pairs = [(cycle[i], cycle[(i + shift) % size]) for i in range(size)]
    return lax.ppermute(x, "ctx", pairs)


def ring_gather(own, cycle, split_axis):
    size = len(cycle)
    reach = size // 2
    slots = [None] * size
    slots[0] = own
    fore = back = own
    for hop in range(1, reach):
        back = ring_shift(back, cycle, 1)
        fore = ring_shift(fore, cycle, -1)
        slots[size - hop] = back
        slots[hop] = fore
    first, second = jnp.split(own, 2, axis=split_axis) if reach == 1 else (None, None)
    first = jnp.split(back, 2, axis=split_axis)[0]
    second = jnp.split(fore, 2, axis=split_axis)[1]
    first = ring_shift(first, cycle, 1)
    second = ring_shift(second, cycle, -1)
    slots[reach] = jnp.concatenate([first, second], axis=split_axis)
    return slots


def ring_reduce(parts, cycle, wire):
    size = len(cycle)
    reach = size // 2
    width = parts[0].shape[1] // 2
    far = parts[reach].astype(wire)
    up = ring_shift(far[:, :width], cycle, 1).astype(F32)
    down = ring_shift(far[:, width:], cycle, -1).astype(F32)
    for hop in range(reach - 1, 0, -1):
        up_part, down_part = parts[hop], parts[size - hop]
        if hop == reach - 1:
            up = jnp.concatenate([up_part[:, :width] + up, up_part[:, width:].astype(F32)], axis=1)
            down = jnp.concatenate([down_part[:, :width].astype(F32), down_part[:, width:] + down], axis=1)
        else:
            up = up_part + up
            down = down_part + down
        up = ring_shift(up.astype(wire), cycle, 1).astype(F32)
        down = ring_shift(down.astype(wire), cycle, -1).astype(F32)
    return parts[0] + up + down


def swap(x, axis):
    return lax.ppermute(x, axis, [(0, 1), (1, 0)])


def join_tp(own, axis):
    if lax.axis_size("tp") == 2:
        other = swap(own, "tp")
        first = lax.axis_index("tp") == 0
        low = jnp.where(first, own, other)
        high = jnp.where(first, other, own)
        return jnp.concatenate([low, high], axis=axis)
    return lax.all_gather(own, "tp", axis=axis, tiled=True)


def sum_tp(own):
    if lax.axis_size("tp") == 2:
        return own.astype(F32) + swap(own, "tp").astype(F32)
    return jnp.sum(lax.all_gather(own, "tp", axis=0, tiled=False).astype(F32), axis=0)


def join_probe(own, axis):
    other = swap(own, "probe")
    first = lax.axis_index("probe") == 0
    return jnp.concatenate([jnp.where(first, own, other), jnp.where(first, other, own)], axis=axis)


def exchange(pieces, cycle):
    size = len(cycle)
    got = [None] * size
    got[0] = pieces[0]
    for shift in sorted(range(1, size), key=lambda s: -min(s, size - s)):
        got[(size - shift) % size] = ring_shift(pieces[shift], cycle, shift)
    return got


def head_parts(raw, index):
    return raw[:, index * HD:(index + 1) * HD]


def head_norm(raw, gain):
    inv = lax.rsqrt(jnp.mean(raw * raw, axis=1, keepdims=True) + EPS)
    return (raw * inv * gain).astype(BF16), inv


def head_norm_tangent(raw, tan, inv, gain):
    tan_inv = -inv * inv * inv * jnp.mean(raw * tan, axis=1, keepdims=True)
    return ((tan * inv + raw * tan_inv) * gain).astype(BF16)


def local(latent, probes, modulation, pattern, w_qkv, w_out, w_up, w_down, q_gain, k_gain):
    ctx_size = lax.axis_size("ctx")
    tp_size = lax.axis_size("tp")
    cycle = cycle_of(ctx_size)
    row_count, local_width = latent.shape
    half = row_count // 2
    full_width = local_width * tp_size
    tokens = row_count * ctx_size
    heads_local = q_gain.shape[0] // HD
    groups = math.gcd(heads_local, ctx_size)
    heads_own = heads_local // groups
    head_width = heads_own * HD
    query_rows = groups * row_count
    unit_total = w_up.shape[1]
    units = unit_total // ctx_size
    step_size = 1.0 / STEPS
    score_scale = 1.0 / math.sqrt(HD)

    ctx_index = lax.axis_index("ctx")
    probe_index = lax.axis_index("probe")
    tp_index = lax.axis_index("tp")
    cycle_arr = jnp.array(cycle, jnp.int32)
    place = jnp.array([cycle.index(i) for i in range(ctx_size)], jnp.int32)
    ring_index = place[ctx_index]
    slot_owner = cycle_arr[(ring_index + jnp.arange(ctx_size)) % ctx_size]
    owner_slot = (place - ring_index) % ctx_size
    group = ring_index % groups

    lat_half = lax.dynamic_slice_in_dim(latent, probe_index * half, half, 0)
    rows = join_tp(lat_half, 1)

    up_half = lax.dynamic_slice_in_dim(w_up, probe_index * (w_up.shape[0] // 2), w_up.shape[0] // 2, 0)
    up_pieces = [
        lax.dynamic_slice_in_dim(up_half, slot_owner[k] * units, units, 1) for k in range(ctx_size)
    ]
    up_got = jnp.stack(exchange(up_pieces, cycle))[owner_slot]
    up_other = swap(up_got, "probe")
    first = probe_index == 0
    up_own = jnp.stack([jnp.where(first, up_got, up_other), jnp.where(first, up_other, up_got)], axis=1)
    up_own = up_own.reshape(full_width, units)

    down_pieces = [
        lax.dynamic_slice_in_dim(w_down, slot_owner[k] * units + probe_index * (units // 2), units // 2, 0)
        for k in range(ctx_size)
    ]
    down_got = jnp.stack(exchange(down_pieces, cycle))[owner_slot]
    down_got = down_got.transpose(1, 0, 2).reshape(units // 2, full_width)
    down_own = join_probe(down_got, 0)

    qkv_own = lax.dynamic_slice_in_dim(w_qkv, group * head_width, head_width, 2)
    q_weight, k_weight, v_weight = (qkv_own[:, part] for part in range(3))
    out_own = lax.dynamic_slice_in_dim(w_out, group * head_width, head_width, 0)
    q_gain_own = lax.dynamic_slice_in_dim(q_gain, group * head_width, head_width, 0)[None]
    k_gain_own = lax.dynamic_slice_in_dim(k_gain, group * head_width, head_width, 0)[None]

    signs_local = (2 * probes[0] - 1).astype(BF16)
    signs_local = signs_local.reshape(2, half, local_width)
    signs_local = jnp.where(first, signs_local, signs_local[::-1]).reshape(row_count, local_width)
    sign_slots = ring_gather(signs_local, cycle, 1)
    signs = join_tp(jnp.concatenate(sign_slots, axis=0), 1)
    own_signs = signs[:half].astype(F32)
    other_signs = swap(signs[half:row_count], "probe").astype(F32)
    own_mean = jnp.mean(own_signs, axis=1)
    other_mean = jnp.mean(other_signs, axis=1)

    lists = lax.all_gather(pattern, "ctx", axis=0, tiled=True)
    listed = jnp.any(lists[slot_owner[:groups]][:, :, None] == slot_owner[None, None, :], axis=1)
    allowed = jnp.repeat(jnp.repeat(listed, row_count, axis=0), row_count, axis=1)

    estimate = jnp.zeros((tokens,), F32)
    for step in range(STEPS):
        mod = modulation[step]
        shift, stretch, gate = mod[0][None], 1.0 + mod[1][None], mod[2][None]

        row_mean = jnp.mean(rows, axis=1, keepdims=True)
        row_var = jnp.mean(rows * rows, axis=1, keepdims=True) - row_mean * row_mean
        inv_std = lax.rsqrt(row_var + EPS)
        normed_own = ((rows - row_mean) * inv_std * stretch + shift).astype(BF16)
        slots = ring_gather(normed_own, cycle, 1)
        normed = jnp.concatenate(
            [piece for slot in slots for piece in (slot, swap(slot, "probe"))], axis=0
        )
        q_raw = dot(normed[:query_rows], q_weight)
        k_raw = dot(normed, k_weight)
        v_raw = dot(normed, v_weight)

        stretch_bf = stretch.astype(BF16)
        scaled = signs * stretch_bf
        gated = (signs.astype(F32) * gate).astype(BF16)
        q_sign = dot(scaled[:query_rows], q_weight)
        k_sign = dot(scaled, k_weight)
        v_sign = dot(scaled, v_weight)
        up_sign = dot(scaled, up_own)
        down_back = dot_t(gated, down_own)
        out_back = dot_t(gated[:query_rows], out_own)
        pair = jnp.concatenate([stretch_bf, shift.astype(BF16), jnp.zeros((14, full_width), BF16)], axis=0)
        q_pair, k_pair, v_pair, up_pair = (dot(pair, w) for w in (q_weight, k_weight, v_weight, up_own))

        flat_mean, flat_inv = row_mean[:, 0], inv_std[:, 0]
        scalars = [flat_inv]
        for sign_rows, sign_mean in ((own_signs, own_mean), (other_signs, other_mean)):
            tan_var = 2.0 * (jnp.mean(rows * sign_rows, axis=1) - flat_mean * sign_mean)
            scalars += [flat_inv * sign_mean, 0.5 * tan_var * flat_inv * flat_inv]
        own_scalars = jnp.stack(scalars[:3], axis=1)
        cross_scalars = jnp.stack([scalars[0]] + scalars[3:], axis=1)
        block_scalars = jnp.concatenate([own_scalars, swap(cross_scalars, "probe")], axis=0)
        gathered = lax.all_gather(block_scalars, "ctx", axis=0, tiled=False)
        gathered = gathered[slot_owner].reshape(tokens, 3)
        t_inv, t_mean, t_var = (gathered[:, i:i + 1] for i in range(3))

        def tangent(raw, sign, consts, count):
            return (
                t_inv[:count] * sign - t_mean[:count] * consts[0:1] - t_var[:count] * (raw - consts[1:2])
            )

        dq_raw = tangent(q_raw, q_sign, q_pair, query_rows)
        dk_raw = tangent(k_raw, k_sign, k_pair, tokens)
        dv_raw = tangent(v_raw, v_sign, v_pair, tokens)

        attended_heads = []
        attn_estimate = jnp.zeros((query_rows,), F32)
        for head in range(heads_own):
            q_head, k_head, v_head = (head_parts(raw, head) for raw in (q_raw, k_raw, v_raw))
            q_gain_head, k_gain_head = head_parts(q_gain_own, head), head_parts(k_gain_own, head)
            q_n, q_inv = head_norm(q_head, q_gain_head)
            k_n, k_inv = head_norm(k_head, k_gain_head)
            v_n = v_head.astype(BF16)
            scores = dot_t(q_n, k_n) * score_scale
            scores = jnp.where(allowed, scores, NEG_BIG)
            top = jnp.max(scores, axis=1, keepdims=True)
            weights = jnp.where(allowed, jnp.exp(scores - top), 0.0)
            inv_total = 1.0 / jnp.sum(weights, axis=1, keepdims=True)
            weights_bf = weights.astype(BF16)
            attended = dot(weights_bf, v_n) * inv_total
            attended_heads.append(attended.astype(BF16))

            dq_n = head_norm_tangent(q_head, head_parts(dq_raw, head), q_inv, q_gain_head)
            dk_n = head_norm_tangent(k_head, head_parts(dk_raw, head), k_inv, k_gain_head)
            dv_n = head_parts(dv_raw, head).astype(BF16)
            tan_scores = dot_t(
                jnp.concatenate([dq_n, q_n], axis=1), jnp.concatenate([k_n, dk_n], axis=1)
            ) * score_scale
            weighted = weights * tan_scores
            tan_sum = jnp.sum(weighted, axis=1, keepdims=True) * inv_total
            tan_out = (dot(weights_bf, dv_n) + dot(weighted.astype(BF16), v_n)) * inv_total - tan_sum * attended
            attn_estimate = attn_estimate + jnp.sum(tan_out * head_parts(out_back, head), axis=1)

        attended = jnp.concatenate(attended_heads, axis=1)
        attended = attended.reshape(groups, 2, half, head_width)[:, 0].reshape(groups * half, head_width)

        pre_hidden = dot(normed, up_own)
        pre_own = pre_hidden.reshape(ctx_size, 2, half, units)[:, 0].reshape(ctx_size * half, units)
        hidden = jax.nn.gelu(pre_own, approximate=True).astype(BF16)
        near = dot(attended, out_own) + dot(hidden[:groups * half], down_own)
        parts = [near[k * half:(k + 1) * half] for k in range(groups)]
        if groups < ctx_size:
            far = dot(hidden[groups * half:], down_own)
            parts += [far[k * half:(k + 1) * half] for k in range(ctx_size - groups)]
        branch = sum_tp(ring_reduce(parts, cycle, BF16).astype(BF16))
        rows = rows + step_size * (gate * branch)

        dpre = tangent(pre_hidden, up_sign, up_pair, tokens)
        _, dhidden = jax.jvp(lambda u: jax.nn.gelu(u, approximate=True), (pre_hidden,), (dpre,))
        estimate = estimate + jnp.sum(dhidden * down_back, axis=1)
        estimate = estimate + jnp.pad(attn_estimate, (0, tokens - query_rows))

    lat_cols = lax.dynamic_slice_in_dim(rows, tp_index * local_width, local_width, 1)
    latent_out = join_probe(lat_cols, 0)

    by_slot = estimate.reshape(ctx_size, 2, half)
    by_slot = jnp.where(first, by_slot, by_slot[:, ::-1]).reshape(ctx_size, row_count)
    by_slot = jnp.concatenate([by_slot, jnp.zeros_like(by_slot)], axis=1)
    own_estimate = ring_reduce([by_slot[k:k + 1] for k in range(ctx_size)], cycle, F32)[:, :row_count]
    own_estimate = own_estimate + swap(own_estimate, "probe")
    own_estimate = sum_tp(own_estimate)[0]
    density_change = -step_size * own_estimate / (2 * math.sqrt(full_width))
    return (latent_out, density_change)


def solution(mesh):
    return jax.shard_map(
        local,
        mesh=mesh,
        in_specs=(
            P("ctx", "tp"),
            P("probe", "ctx", "tp"),
            P(),
            P("ctx", None),
            P(None, None, "tp"),
            P("tp", None),
            P("ctx", "tp"),
            P("tp", "ctx"),
            P("tp"),
            P("tp"),
        ),
        out_specs=(P("ctx", "tp"), P("ctx")),
        check_vma=False,
    )
```

time: 1490 us -> 685 us (0.46)
  waiting for transfers between devices: 1120 us -> 214 us
  starting transfers between devices: 0.77 us -> 80.4 us
  matrix products: 133 us -> 165 us
  local copies, waits for them, and re-layouts: 113 us -> 87 us
    all_gather x10 -> x0, waiting for transfers between devices: 1070 us -> none  [the longest x1 353 us: local(): lax.all_gather(w_down, 'ctx', axis=1, tiled=True)]
    ppermute x0 -> x90, waiting for transfers between devices: none -> 214 us  [the longest x62 156 us: ring_shift(): return lax.ppermute(x, 'ctx', pairs)]
    ppermute x0 -> x90, starting transfers between devices: none -> 80.4 us  [the longest x62 74.1 us: ring_shift(): return lax.ppermute(x, 'ctx', pairs)]
    reduce_scatter x2 -> x0, waiting for transfers between devices: 50.9 us -> none  [local(): lax.psum_scatter(partials.astype(jnp.bfloat16), 'tp', scatter_dimension=1...]
    unnamed x90 -> x350, local copies, waits for them, and re-layouts: 2.96 us -> 43.8 us
    reshape x8 -> x3, local copies, waits for them, and re-layouts: 40.9 us -> 0.35 us  [the longest x1 0.19 us: local(): down_got = down_got.transpose(1, 0, 2).reshape(units // 2, full_width)]
    dot_general x20 -> x64, matrix products: 133 us -> 165 us  [the longest x48 132 us: dot(): return jnp.dot(a, b, preferred_element_type=F32)]
    all_gather x4 -> x3, blocking collectives: 40.3 us -> 71 us  [the longest x2 52.5 us: local(): gathered = lax.all_gather(block_scalars, 'ctx', axis=0, tiled=False)]
  transfers between devices with their start and end apart: 12 -> 90, of which waited for: 12 -> 47; matrix products, arithmetic and copies ran while one was open for 10% -> 43% of each run, Pallas kernels for 0% -> 0%
where the time goes in v1:
time: 685 us; the launch traced here: 675 us
  waiting for transfers between devices  214 us (31%)
  matrix products  165 us (24%)
  local copies, waits for them, and re-layouts  87 us (13%)
  starting transfers between devices  80.4 us (12%)
  blocking collectives  71 us (10%)
  other arithmetic  47 us (7%)
  between operations  10.5 us (2%)
    ppermute x62, waiting for transfers between devices, ring_shift(): return lax.ppermute(x, 'ctx', pairs)  156 us
    dot_general x48, matrix products, dot(): return jnp.dot(a, b, preferred_element_type=F32)  132 us
    ppermute x62, starting transfers between devices, ring_shift(): return lax.ppermute(x, 'ctx', pairs)  74.1 us
    ppermute x28, waiting for transfers between devices, swap(): return lax.ppermute(x, axis, [(0, 1), (1, 0)])  57.7 us
    all_gather x2, blocking collectives, local(): gathered = lax.all_gather(block_scalars, 'ctx', axis=0, tiled=False)  52.5 us
    unnamed x350, local copies, waits for them, and re-layouts  43.8 us
    dot_general x16, matrix products, dot_t(): lax.dot_general(a, b, (((1,), (1,)), ((), ())), preferred_element_type=F32)  33.5 us
    all_gather x1, blocking collectives, local(): lists = lax.all_gather(pattern, 'ctx', axis=0, tiled=True)  18.6 us
  transfers between devices with their start and end apart: 90, of which 47 were waited for; matrix products, arithmetic and copies ran while one was open for 43% of the time, Pallas kernels for 0%

profile of v1, /device:TPU:0, one launch (start us, length us, event | category | flops | bytes accessed | tf_op | source)
XLA Modules:
  0.0 675.4 jit_solution(3454637323212552185)
XLA Ops:
  2.1 3.1 collective-permute-start.71
  42.2 18.6 %all-gather.2 = s32[8,1,8]{2,1,0:T(1,128)S(1)} all-gather(s32[1,1,8]{2,1,0:T(1,128)S(1)} %bitcast.456), channel_id=1, replica_groups=mesh['ctx'=8,'tp'=2,'probe'=2] {'ctx'}, dimensions={0}, use_global_device_ids=true | all-gather | bytes 288 | tf_op jit(solution)/shard_map/all_gather | solution.py:189
  73.9 7.0 %collective-permute-done.18 = bf16[192,384]{1,0:T(8,128)(2,1)S(1)} collective-permute-done((bf16[192,384]{1,0:T(8,128)(2,1)S(1)}, bf16[192,384]{1,0:T(8,128)(2,1)S(1)}, u32[]{:S(2)}, u32[]{:S(2)}) %collective-permute-start.18) | collective-permute-done | bytes 147488 | tf_op jit(solution)/shard_map/ppermute | solution.py:32
  81.5 6.7 collective-permute-done.19
  89.5 6.7 collective-permute-done.20
  98.9 4.7 collective-permute-done.21
  104.3 6.1 collective-permute-done.22
  111.5 4.0 collective-permute-done.23
  118.9 3.1 collective-permute-done.25
  122.0 3.2 collective-permute-start.26
  126.1 6.0 collective-permute-done.26
  132.1 3.0 collective-permute-start.27
  135.8 2.8 collective-permute-start.69
  139.8 2.7 collective-permute-start.29
  142.5 3.7 collective-permute-done.72
  151.3 3.2 collective-permute-done.73
  154.6 2.9 collective-permute-start.74
  163.4 3.0 collective-permute-done.75
  170.1 3.2 collective-permute-start.30
  173.3 6.9 %collective-permute-done.30 = bf16[192,384]{1,0:T(8,128)(2,1)S(1)} collective-permute-done((bf16[192,384]{1,0:T(8,128)(2,1)S(1)}, bf16[192,384]{1,0:T(8,128)(2,1)S(1)}, u32[]{:S(2)}, u32[]{:S(2)}) %collective-permute-start.30) | collective-permute-done | bytes 147488 | tf_op jit(solution)/shard_map/ppermute | solution.py:32
  180.3 5.1 collective-permute-done.31
  193.2 47.1 %collective-permute-done.76 = bf16[1024,1536]{1,0:T(8,128)(2,1)} collective-permute-done((bf16[1024,1536]{1,0:T(8,128)(2,1)}, bf16[1024,1536]{1,0:T(8,128)(2,1)}, u32[]{:S(2)}, u32[]{:S(2)}) %collective-permute-start.76) | collective-permute-done | bytes 3145760 | tf_op jit(solution)/shard_map/ppermute | solution.py:76
  243.4 3.3 broadcast_multiply_fusion
  246.7 7.3 %fusion.89 = f32[1024,384]{0,1:T(8,128)} fusion(bf16[1024,3072]{1,0:T(8,128)(2,1)S(1)} %get-tuple-element.78, bf16[3072,3,1536]{2,0,1:T(8,128)(2,1)} %param.16, s32[]{:T(128)S(6)} %add.782, s32[]{:T(128)S(6)} %select_n.257), kind=kOutput, calls=%fused_computation.155 | convolution fusion | flops 2415919104 | bytes 10223624 | tf_op jit(solution)/shard_map/dot_general | solution.py:18
  254.0 3.8 fusion.359
  257.8 5.5 fusion.91
  263.2 3.8 fusion.358
  269.7 4.0 fusion.6
  273.7 3.8 fusion.307
  277.5 3.9 fusion.306
  281.4 4.1 fusion.2
  292.4 26.5 %all-gather = f32[1024,3]{0,1:T(4,128)S(1)} all-gather(f32[128,3]{0,1:T(4,128)S(1)} %pad_maximum_fusion.14), channel_id=2, replica_groups=mesh['ctx'=8,'tp'=2,'probe'=2] {'ctx'}, dimensions={0}, use_global_device_ids=true | all-gather | bytes 13824 | tf_op jit(solution)/shard_map/all_gather | solution.py:230
  326.6 5.4 collective-permute-done.4
  336.1 9.5 %collective-permute-done.10 = bf16[64,3072]{1,0:T(8,128)(2,1)S(1)} collective-permute-done((bf16[64,3072]{1,0:T(8,128)(2,1)S(1)}, bf16[64,3072]{1,0:T(8,128)(2,1)S(1)}, u32[]{:S(2)}, u32[]{:S(2)}) %collective-permute-start.10) | collective-permute-done | bytes 393248 | tf_op jit(solution)/shard_map/ppermute | solution.py:32
  354.5 4.2 fusion.83
  358.8 3.3 multiply_subtract_fusion.3
  364.9 5.7 fusion.87
  370.6 4.6 fusion.355
  375.2 6.5 fusion.338
  381.7 3.0 copy.101
  384.7 3.0 copy.94
  389.2 2.8 fusion.345
  395.0 5.6 multiply_subtract_fusion.1
  428.7 2.7 fusion.48
  438.4 7.4 %collective-permute-done.38 = bf16[64,3072]{1,0:T(8,128)(2,1)S(1)} collective-permute-done((bf16[64,3072]{1,0:T(8,128)(2,1)S(1)}, bf16[64,3072]{1,0:T(8,128)(2,1)S(1)}, u32[]{:S(2)}, u32[]{:S(2)}) %collective-permute-start.38) | collective-permute-done | bytes 393248 | tf_op jit(solution)/shard_map/ppermute | solution.py:32
  448.8 6.8 %collective-permute-done.39 = bf16[64,3072]{1,0:T(8,128)(2,1)S(1)} collective-permute-done((bf16[64,3072]{1,0:T(8,128)(2,1)S(1)}, bf16[64,3072]{1,0:T(8,128)(2,1)S(1)}, u32[]{:S(2)}, u32[]{:S(2)}) %collective-permute-start.39) | collective-permute-done | bytes 393248 | tf_op jit(solution)/shard_map/ppermute | solution.py:32
  460.6 3.8 collective-permute-done.40
  467.9 6.1 collective-permute-done.41
  479.4 26.0 %all-gather.1 = f32[1024,3]{0,1:T(4,128)S(1)} all-gather(f32[128,3]{0,1:T(4,128)S(1)} %pad_maximum_fusion.16), channel_id=3, replica_groups=mesh['ctx'=8,'tp'=2,'probe'=2] {'ctx'}, dimensions={0}, use_global_device_ids=true | all-gather | bytes 13824 | tf_op jit(solution)/shard_map/all_gather | solution.py:230
  512.3 5.7 collective-permute-done.45
  522.0 9.2 %collective-permute-done.51 = bf16[64,3072]{1,0:T(8,128)(2,1)S(1)} collective-permute-done((bf16[64,3072]{1,0:T(8,128)(2,1)S(1)}, bf16[64,3072]{1,0:T(8,128)(2,1)S(1)}, u32[]{:S(2)}, u32[]{:S(2)}) %collective-permute-start.51) | collective-permute-done | bytes 393248 | tf_op jit(solution)/shard_map/ppermute | solution.py:32
  539.4 4.2 fusion.82
  543.7 3.3 multiply_subtract_fusion.2
  550.3 4.7 fusion.357
  555.0 5.5 fusion.86
  560.4 6.5 fusion.346
  566.9 3.0 copy.109
  569.9 7.0 %multiply_subtract_fusion = f32[1024,384]{0,1:T(8,128)S(1)} fusion(f32[1024,384]{0,1:T(8,128)} %fusion.86, bf16[1024,3072]{1,0:T(8,128)(2,1)} %copy-done.15, bf16[3072,3,1536]{2,0,1:T(8,128)(2,1)} %param.16, s32[]{:T(128)S(6)} %add.781, s32[]{:T(128)S(6)} %select_n.257, f32[384]{0:T(512)S(1)} %copy-done.132, f32[384]{0:T(512)S(1)} %copy-done.131, ...), kind=kOutput, calls=%fused_computation.88 | convolution fusion | flops 2418278400 | bytes 11811848 | tf_op jit(solution)/shard_map/dot_general | solution.py:18
  578.5 3.0 copy.102
  622.2 4.1 collective-permute-done.62
  629.3 7.8 %collective-permute-done.63 = bf16[64,3072]{1,0:T(8,128)(2,1)S(1)} collective-permute-done((bf16[64,3072]{1,0:T(8,128)(2,1)S(1)}, bf16[64,3072]{1,0:T(8,128)(2,1)S(1)}, u32[]{:S(2)}, u32[]{:S(2)}) %collective-permute-start.63) | collective-permute-done | bytes 393248 | tf_op jit(solution)/shard_map/ppermute | solution.py:32
  639.7 7.2 %collective-permute-done.64 = bf16[64,3072]{1,0:T(8,128)(2,1)S(1)} collective-permute-done((bf16[64,3072]{1,0:T(8,128)(2,1)S(1)}, bf16[64,3072]{1,0:T(8,128)(2,1)S(1)}, u32[]{:S(2)}, u32[]{:S(2)}) %collective-permute-start.64) | collective-permute-done | bytes 393248 | tf_op jit(solution)/shard_map/ppermute | solution.py:32
  652.3 3.9 collective-permute-done.80
  670.6 3.0 collective-permute-done.89
  (712 shorter events, 261.9 us)
Async XLA Ops:
  2.1 133.0 %collective-permute-start.71 = (bf16[128,1536]{1,0:T(8,128)(2,1)S(1)}, bf16[128,1536]{1,0:T(8,128)(2,1)S(1)}, u32[]{:S(2)}, u32[]{:S(2)}) collective-permute-start(bf16[128,1536]{1,0:T(8,128)(2,1)S(1)} %bitcast.410), channel_id=1, source_target_pairs={{0,8},{8,16},{16,24},{24,28},{28,20},{20,12},{12,4},{4,0},{1,9},{9... | collective-permute-start | bytes 1179656 | tf_op jit(solution)/shard_map/ppermute | solution.py:32
  5.1 130.6 %collective-permute-start.68 = (bf16[128,1536]{1,0:T(8,128)(2,1)S(1)}, bf16[128,1536]{1,0:T(8,128)(2,1)S(1)}, u32[]{:S(2)}, u32[]{:S(2)}) collective-permute-start(bf16[128,1536]{1,0:T(8,128)(2,1)S(1)} %bitcast.411), channel_id=1, source_target_pairs={{0,4},{8,0},{16,8},{24,16},{28,24},{20,28},{12,20},{4,12},{1,5},{9... | collective-permute-start | bytes 1179656 | tf_op jit(solution)/shard_map/ppermute | solution.py:32
  5.7 644.1 %collective-permute-start.84 = (f32[1,128]{1,0:T(1,128)}, f32[1,128]{1,0:T(1,128)}, u32[]{:S(2)}, u32[]{:S(2)}) collective-permute-start(f32[1,128]{1,0:T(1,128)} %slice.658), channel_id=1, source_target_pairs={{0,4},{8,0},{16,8},{24,16},{28,24},{20,28},{12,20},{4,12},{1,5},{9... | collective-permute-start | bytes 1544 | tf_op jit(solution)/shard_map/ppermute | solution.py:32
  8.4 178.3 %collective-permute-start = (f32[64,1536]{1,0:T(8,128)}, f32[64,1536]{1,0:T(8,128)}, u32[]{:S(2)}, u32[]{:S(2)}) collective-permute-start(f32[64,1536]{1,0:T(8,128)} %constant_dynamic-slice_fusion.7), channel_id=1, source_target_pairs={{0,2},{2,0},{1,3},{3,1},{4,6},{6,4},{5,7},{7,5},{8,10},{10,8},{9,1... | collective-permute-start | bytes 1179656 | tf_op jit(solution)/shard_map/ppermute | solution.py:76
  19.0 53.2 %collective-permute-start.17 = (bf16[192,384]{1,0:T(8,128)(2,1)S(1)}, bf16[192,384]{1,0:T(8,128)(2,1)}, u32[]{:S(2)}, u32[]{:S(2)}) collective-permute-start(bf16[192,384]{1,0:T(8,128)(2,1)S(1)} %get-tuple-element.104), channel_id=1, source_target_pairs={{0,4},{8,0},{16,8},{24,16},{28,24},{20,28},{12,20},{4,12},{1,5},{9... | collective-permute-start | bytes 442376 | tf_op jit(solution)/shard_map/ppermute | solution.py:32
  72.3 8.6 %collective-permute-start.18 = (bf16[192,384]{1,0:T(8,128)(2,1)S(1)}, bf16[192,384]{1,0:T(8,128)(2,1)S(1)}, u32[]{:S(2)}, u32[]{:S(2)}) collective-permute-start(bf16[192,384]{1,0:T(8,128)(2,1)S(1)} %get-tuple-element.103), channel_id=1, source_target_pairs={{0,12},{8,4},{16,0},{24,8},{28,16},{20,24},{12,28},{4,20},{1,13},{... | collective-permute-start | bytes 442376 | tf_op jit(solution)/shard_map/ppermute | solution.py:32
  80.9 7.4 %collective-permute-start.19 = (bf16[192,384]{1,0:T(8,128)(2,1)S(1)}, bf16[192,384]{1,0:T(8,128)(2,1)S(1)}, u32[]{:S(2)}, u32[]{:S(2)}) collective-permute-start(bf16[192,384]{1,0:T(8,128)(2,1)S(1)} %get-tuple-element.102), channel_id=1, source_target_pairs={{0,20},{8,12},{16,4},{24,0},{28,8},{20,16},{12,24},{4,28},{1,21},{... | collective-permute-start | bytes 442376 | tf_op jit(solution)/shard_map/ppermute | solution.py:32
  88.3 7.9 %collective-permute-start.20 = (bf16[192,384]{1,0:T(8,128)(2,1)S(1)}, bf16[192,384]{1,0:T(8,128)(2,1)S(1)}, u32[]{:S(2)}, u32[]{:S(2)}) collective-permute-start(bf16[192,384]{1,0:T(8,128)(2,1)S(1)} %get-tuple-element.101), channel_id=1, source_target_pairs={{0,28},{8,20},{16,12},{24,4},{28,0},{20,8},{12,16},{4,24},{1,29},{... | collective-permute-start | bytes 442376 | tf_op jit(solution)/shard_map/ppermute | solution.py:32
  122.0 10.2 %collective-permute-start.26 = (bf16[192,384]{1,0:T(8,128)(2,1)}, bf16[192,384]{1,0:T(8,128)(2,1)S(1)}, u32[]{:S(2)}, u32[]{:S(2)}) collective-permute-start(bf16[192,384]{1,0:T(8,128)(2,1)} %get-tuple-element.94), channel_id=1, source_target_pairs={{0,12},{8,4},{16,0},{24,8},{28,16},{20,24},{12,28},{4,20},{1,13},{... | collective-permute-start | bytes 442376 | tf_op jit(solution)/shard_map/ppermute | solution.py:32
  132.1 7.7 %collective-permute-start.27 = (bf16[192,384]{1,0:T(8,128)(2,1)}, bf16[192,384]{1,0:T(8,128)(2,1)S(1)}, u32[]{:S(2)}, u32[]{:S(2)}) collective-permute-start(bf16[192,384]{1,0:T(8,128)(2,1)} %get-tuple-element.93), channel_id=1, source_target_pairs={{0,20},{8,12},{16,4},{24,0},{28,8},{20,16},{12,24},{4,28},{1,21},{... | collective-permute-start | bytes 442376 | tf_op jit(solution)/shard_map/ppermute | solution.py:32
  135.1 11.2 %collective-permute-start.72 = (bf16[128,1536]{1,0:T(8,128)(2,1)S(1)}, bf16[128,1536]{1,0:T(8,128)(2,1)S(1)}, u32[]{:S(2)}, u32[]{:S(2)}) collective-permute-start(bf16[128,1536]{1,0:T(8,128)(2,1)S(1)} %collective-permute-done.71), channel_id=1, source_target_pairs={{0,8},{8,16},{16,24},{24,28},{28,20},{20,12},{12,4},{4,0},{1,9},{9... | collective-permute-start | bytes 1179656 | tf_op jit(solution)/shard_map/ppermute | solution.py:32
  135.8 13.0 %collective-permute-start.69 = (bf16[128,1536]{1,0:T(8,128)(2,1)S(1)}, bf16[128,1536]{1,0:T(8,128)(2,1)S(1)}, u32[]{:S(2)}, u32[]{:S(2)}) collective-permute-start(bf16[128,1536]{1,0:T(8,128)(2,1)S(1)} %collective-permute-done.68), channel_id=1, source_target_pairs={{0,4},{8,0},{16,8},{24,16},{28,24},{20,28},{12,20},{4,12},{1,5},{9... | collective-permute-start | bytes 1179656 | tf_op jit(solution)/shard_map/ppermute | solution.py:32
  139.8 30.3 %collective-permute-start.29 = (bf16[192,384]{1,0:T(8,128)(2,1)}, bf16[192,384]{1,0:T(8,128)(2,1)S(1)}, u32[]{:S(2)}, u32[]{:S(2)}) collective-permute-start(bf16[192,384]{1,0:T(8,128)(2,1)} %get-tuple-element.91), channel_id=1, source_target_pairs={{0,24},{8,28},{16,20},{24,12},{28,4},{20,0},{12,8},{4,16},{1,25},{... | collective-permute-start | bytes 442376 | tf_op jit(solution)/shard_map/ppermute | solution.py:32
  146.2 8.3 %collective-permute-start.73 = (bf16[128,1536]{1,0:T(8,128)(2,1)S(1)}, bf16[128,1536]{1,0:T(8,128)(2,1)S(1)}, u32[]{:S(2)}, u32[]{:S(2)}) collective-permute-start(bf16[128,1536]{1,0:T(8,128)(2,1)S(1)} %collective-permute-done.72), channel_id=1, source_target_pairs={{0,8},{8,16},{16,24},{24,28},{28,20},{20,12},{12,4},{4,0},{1,9},{9... | collective-permute-start | bytes 1179656 | tf_op jit(solution)/shard_map/ppermute | solution.py:32
  148.8 9.4 %collective-permute-start.70 = (bf16[128,1536]{1,0:T(8,128)(2,1)S(1)}, bf16[128,1536]{1,0:T(8,128)(2,1)S(1)}, u32[]{:S(2)}, u32[]{:S(2)}) collective-permute-start(bf16[128,1536]{1,0:T(8,128)(2,1)S(1)} %collective-permute-done.69), channel_id=1, source_target_pairs={{0,4},{8,0},{16,8},{24,16},{28,24},{20,28},{12,20},{4,12},{1,5},{9... | collective-permute-start | bytes 1179656 | tf_op jit(solution)/shard_map/ppermute | solution.py:32
  158.2 8.2 %collective-permute-start.75 = (bf16[128,768]{1,0:T(8,128)(2,1)S(1)}, bf16[128,768]{1,0:T(8,128)(2,1)S(1)}, u32[]{:S(2)}, u32[]{:S(2)}) collective-permute-start(bf16[128,768]{1,0:T(8,128)(2,1)S(1)} %split.29), channel_id=1, source_target_pairs={{0,4},{8,0},{16,8},{24,16},{28,24},{20,28},{12,20},{4,12},{1,5},{9... | collective-permute-start | bytes 589832 | tf_op jit(solution)/shard_map/ppermute | solution.py:32
  161.6 8.0 %collective-permute-start.28 = (bf16[192,384]{1,0:T(8,128)(2,1)S(1)}, bf16[192,384]{1,0:T(8,128)(2,1)S(1)}, u32[]{:S(2)}, u32[]{:S(2)}) collective-permute-start(bf16[192,384]{1,0:T(8,128)(2,1)S(1)} %copy-done.67), channel_id=1, source_target_pairs={{0,28},{8,20},{16,12},{24,4},{28,0},{20,8},{12,16},{4,24},{1,29},{... | collective-permute-start | bytes 442376 | tf_op jit(solution)/shard_map/ppermute | solution.py:32
  166.4 22.3 %collective-permute-start.24 = (bf16[8,192,384]{2,1,0:T(8,128)(2,1)S(1)}, bf16[8,192,384]{2,1,0:T(8,128)(2,1)}, u32[]{:S(2)}, u32[]{:S(2)}) collective-permute-start(bf16[8,192,384]{2,1,0:T(8,128)(2,1)S(1)} %gather_fusion.2), channel_id=1, source_target_pairs={{0,1},{1,0},{2,3},{3,2},{4,5},{5,4},{6,7},{7,6},{8,9},{9,8},{10,11... | collective-permute-start | bytes 3538952 | tf_op jit(solution)/shard_map/ppermute | solution.py:76
  169.5 70.8 %collective-permute-start.76 = (bf16[1024,1536]{1,0:T(8,128)(2,1)}, bf16[1024,1536]{1,0:T(8,128)(2,1)}, u32[]{:S(2)}, u32[]{:S(2)}) collective-permute-start(bf16[1024,1536]{1,0:T(8,128)(2,1)} %constant_dynamic-update-slice_fusion.64), channel_id=1, source_target_pairs={{0,2},{2,0},{1,3},{3,1},{4,6},{6,4},{5,7},{7,5},{8,10},{10,8},{9,1... | collective-permute-start | bytes 9437192 | tf_op jit(solution)/shard_map/ppermute | solution.py:76
  170.1 10.2 %collective-permute-start.30 = (bf16[192,384]{1,0:T(8,128)(2,1)S(1)}, bf16[192,384]{1,0:T(8,128)(2,1)S(1)}, u32[]{:S(2)}, u32[]{:S(2)}) collective-permute-start(bf16[192,384]{1,0:T(8,128)(2,1)S(1)} %copy-done.66), channel_id=1, source_target_pairs={{0,16},{8,24},{16,28},{24,20},{28,12},{20,4},{12,0},{4,8},{1,17},{... | collective-permute-start | bytes 442376 | tf_op jit(solution)/shard_map/ppermute | solution.py:32
  267.0 18.5 %collective-permute-start.77 = (bf16[64,3072]{1,0:T(8,128)(2,1)S(1)}, bf16[64,3072]{1,0:T(8,128)(2,1)S(1)}, u32[]{:S(2)}, u32[]{:S(2)}) collective-permute-start(bf16[64,3072]{1,0:T(8,128)(2,1)S(1)} %fusion.167), channel_id=1, source_target_pairs={{0,1},{1,0},{2,3},{3,2},{4,5},{5,4},{6,7},{7,6},{8,9},{9,8},{10,11... | collective-permute-start | bytes 1179656 | tf_op jit(solution)/shard_map/ppermute | solution.py:76
  287.9 32.3 %collective-permute-start.8 = (bf16[64,3072]{1,0:T(8,128)(2,1)}, bf16[64,3072]{1,0:T(8,128)(2,1)}, u32[]{:S(2)}, u32[]{:S(2)}) collective-permute-start(bf16[64,3072]{1,0:T(8,128)(2,1)} %get-tuple-element.70), channel_id=1, source_target_pairs={{0,8},{8,16},{16,24},{24,28},{28,20},{20,12},{12,4},{4,0},{1,9},{9... | collective-permute-start | bytes 1179656 | tf_op jit(solution)/shard_map/ppermute | solution.py:32
  289.9 30.6 %collective-permute-start.2 = (bf16[64,3072]{1,0:T(8,128)(2,1)}, bf16[64,3072]{1,0:T(8,128)(2,1)}, u32[]{:S(2)}, u32[]{:S(2)}) collective-permute-start(bf16[64,3072]{1,0:T(8,128)(2,1)} %get-tuple-element.70), channel_id=1, source_target_pairs={{0,4},{8,0},{16,8},{24,16},{28,24},{20,28},{12,20},{4,12},{1,5},{9... | collective-permute-start | bytes 1179656 | tf_op jit(solution)/shard_map/ppermute | solution.py:32
  289.9 32.6 %collective-permute-start.1 = (bf16[64,3072]{1,0:T(8,128)(2,1)}, bf16[64,3072]{1,0:T(8,128)(2,1)}, u32[]{:S(2)}, u32[]{:S(2)}) collective-permute-start(bf16[64,3072]{1,0:T(8,128)(2,1)} %get-tuple-element.70), channel_id=1, source_target_pairs={{0,1},{1,0},{2,3},{3,2},{4,5},{5,4},{6,7},{7,6},{8,9},{9,8},{10,11... | collective-permute-start | bytes 1179656 | tf_op jit(solution)/shard_map/ppermute | solution.py:76
  320.2 44.7 %collective-permute-start.16 = (bf16[64,3072]{1,0:T(8,128)(2,1)}, bf16[64,3072]{1,0:T(8,128)(2,1)S(1)}, u32[]{:S(2)}, u32[]{:S(2)}) collective-permute-start(bf16[64,3072]{1,0:T(8,128)(2,1)} %collective-permute-done.8), channel_id=1, source_target_pairs={{0,1},{1,0},{2,3},{3,2},{4,5},{5,4},{6,7},{7,6},{8,9},{9,8},{10,11... | collective-permute-start | bytes 1179656 | tf_op jit(solution)/shard_map/ppermute | solution.py:76
  320.2 13.9 %collective-permute-start.9 = (bf16[64,3072]{1,0:T(8,128)(2,1)}, bf16[64,3072]{1,0:T(8,128)(2,1)S(1)}, u32[]{:S(2)}, u32[]{:S(2)}) collective-permute-start(bf16[64,3072]{1,0:T(8,128)(2,1)} %collective-permute-done.8), channel_id=1, source_target_pairs={{0,8},{8,16},{16,24},{24,28},{28,20},{20,12},{12,4},{4,0},{1,9},{9... | collective-permute-start | bytes 1179656 | tf_op jit(solution)/shard_map/ppermute | solution.py:32
  320.5 11.4 %collective-permute-start.4 = (bf16[64,3072]{1,0:T(8,128)(2,1)}, bf16[64,3072]{1,0:T(8,128)(2,1)S(1)}, u32[]{:S(2)}, u32[]{:S(2)}) collective-permute-start(bf16[64,3072]{1,0:T(8,128)(2,1)} %collective-permute-done.2), channel_id=1, source_target_pairs={{0,4},{8,0},{16,8},{24,16},{28,24},{20,28},{12,20},{4,12},{1,5},{9... | collective-permute-start | bytes 1179656 | tf_op jit(solution)/shard_map/ppermute | solution.py:32
  322.5 11.6 %collective-permute-start.3 = (bf16[64,3072]{1,0:T(8,128)(2,1)}, bf16[64,3072]{1,0:T(8,128)(2,1)S(1)}, u32[]{:S(2)}, u32[]{:S(2)}) collective-permute-start(bf16[64,3072]{1,0:T(8,128)(2,1)} %collective-permute-done.2), channel_id=1, source_target_pairs={{0,1},{1,0},{2,3},{3,2},{4,5},{5,4},{6,7},{7,6},{8,9},{9,8},{10,11... | collective-permute-start | bytes 1179656 | tf_op jit(solution)/shard_map/ppermute | solution.py:76
  331.9 14.0 %collective-permute-start.6 = (bf16[64,3072]{1,0:T(8,128)(2,1)S(1)}, bf16[64,3072]{1,0:T(8,128)(2,1)S(1)}, u32[]{:S(2)}, u32[]{:S(2)}) collective-permute-start(bf16[64,3072]{1,0:T(8,128)(2,1)S(1)} %collective-permute-done.4), channel_id=1, source_target_pairs={{0,4},{8,0},{16,8},{24,16},{28,24},{20,28},{12,20},{4,12},{1,5},{9... | collective-permute-start | bytes 1179656 | tf_op jit(solution)/shard_map/ppermute | solution.py:32
  334.1 14.2 %collective-permute-start.5 = (bf16[64,3072]{1,0:T(8,128)(2,1)S(1)}, bf16[64,3072]{1,0:T(8,128)(2,1)S(1)}, u32[]{:S(2)}, u32[]{:S(2)}) collective-permute-start(bf16[64,3072]{1,0:T(8,128)(2,1)S(1)} %collective-permute-done.4), channel_id=1, source_target_pairs={{0,1},{1,0},{2,3},{3,2},{4,5},{5,4},{6,7},{7,6},{8,9},{9,8},{10,11... | collective-permute-start | bytes 1179656 | tf_op jit(solution)/shard_map/ppermute | solution.py:76
  334.1 11.5 %collective-permute-start.10 = (bf16[64,3072]{1,0:T(8,128)(2,1)S(1)}, bf16[64,3072]{1,0:T(8,128)(2,1)S(1)}, u32[]{:S(2)}, u32[]{:S(2)}) collective-permute-start(bf16[64,3072]{1,0:T(8,128)(2,1)S(1)} %collective-permute-done.9), channel_id=1, source_target_pairs={{0,8},{8,16},{16,24},{24,28},{28,20},{20,12},{12,4},{4,0},{1,9},{9... | collective-permute-start | bytes 1179656 | tf_op jit(solution)/shard_map/ppermute | solution.py:32
  352.2 11.6 %collective-permute-start.15 = (bf16[64,3072]{1,0:T(8,128)(2,1)S(1)}, bf16[64,3072]{1,0:T(8,128)(2,1)S(1)}, u32[]{:S(2)}, u32[]{:S(2)}) collective-permute-start(bf16[64,3072]{1,0:T(8,128)(2,1)S(1)} %collective-permute-done.9), channel_id=1, source_target_pairs={{0,1},{1,0},{2,3},{3,2},{4,5},{5,4},{6,7},{7,6},{8,9},{9,8},{10,11... | collective-permute-start | bytes 1179656 | tf_op jit(solution)/shard_map/ppermute | solution.py:76
  352.9 10.8 %collective-permute-start.14 = (bf16[64,3072]{1,0:T(8,128)(2,1)S(1)}, bf16[64,3072]{1,0:T(8,128)(2,1)S(1)}, u32[]{:S(2)}, u32[]{:S(2)}) collective-permute-start(bf16[64,3072]{1,0:T(8,128)(2,1)S(1)} %collective-permute-done.10), channel_id=1, source_target_pairs={{0,1},{1,0},{2,3},{3,2},{4,5},{5,4},{6,7},{7,6},{8,9},{9,8},{10,11... | collective-permute-start | bytes 1179656 | tf_op jit(solution)/shard_map/ppermute | solution.py:76
  353.0 10.6 %collective-permute-start.13 = (bf16[64,3072]{1,0:T(8,128)(2,1)S(1)}, bf16[64,3072]{1,0:T(8,128)(2,1)S(1)}, u32[]{:S(2)}, u32[]{:S(2)}) collective-permute-start(bf16[64,3072]{1,0:T(8,128)(2,1)S(1)} %pad_maximum_fusion.5), channel_id=1, source_target_pairs={{0,1},{1,0},{2,3},{3,2},{4,5},{5,4},{6,7},{7,6},{8,9},{9,8},{10,11... | collective-permute-start | bytes 1179656 | tf_op jit(solution)/shard_map/ppermute | solution.py:76
  392.9 44.0 %collective-permute-start.33 = (bf16[64,1536]{1,0:T(8,128)(2,1)}, bf16[64,1536]{1,0:T(8,128)(2,1)}, u32[]{:S(2)}, u32[]{:S(2)}) collective-permute-start(bf16[64,1536]{1,0:T(8,128)(2,1)} %get-tuple-element.121), channel_id=1, source_target_pairs={{0,8},{8,16},{16,24},{24,28},{28,20},{20,12},{12,4},{4,0},{1,9},{9... | collective-permute-start | bytes 589832 | tf_op jit(solution)/shard_map/ppermute | solution.py:32
  393.6 40.5 %collective-permute-start.37 = (bf16[64,1536]{1,0:T(8,128)(2,1)}, bf16[64,1536]{1,0:T(8,128)(2,1)}, u32[]{:S(2)}, u32[]{:S(2)}) collective-permute-start(bf16[64,1536]{1,0:T(8,128)(2,1)} %get-tuple-element.122), channel_id=1, source_target_pairs={{0,4},{8,0},{16,8},{24,16},{28,24},{20,28},{12,20},{4,12},{1,5},{9... | collective-permute-start | bytes 589832 | tf_op jit(solution)/shard_map/ppermute | solution.py:32
  435.3 10.5 %collective-permute-start.38 = (bf16[64,3072]{1,0:T(8,128)(2,1)S(1)}, bf16[64,3072]{1,0:T(8,128)(2,1)S(1)}, u32[]{:S(2)}, u32[]{:S(2)}) collective-permute-start(bf16[64,3072]{1,0:T(8,128)(2,1)S(1)} %pad_maximum_fusion.8), channel_id=1, source_target_pairs={{0,4},{8,0},{16,8},{24,16},{28,24},{20,28},{12,20},{4,12},{1,5},{9... | collective-permute-start | bytes 1179656 | tf_op jit(solution)/shard_map/ppermute | solution.py:32
  437.9 10.2 %collective-permute-start.34 = (bf16[64,3072]{1,0:T(8,128)(2,1)S(1)}, bf16[64,3072]{1,0:T(8,128)(2,1)S(1)}, u32[]{:S(2)}, u32[]{:S(2)}) collective-permute-start(bf16[64,3072]{1,0:T(8,128)(2,1)S(1)} %pad_maximum_fusion.7), channel_id=1, source_target_pairs={{0,8},{8,16},{16,24},{24,28},{28,20},{20,12},{12,4},{4,0},{1,9},{9... | collective-permute-start | bytes 1179656 | tf_op jit(solution)/shard_map/ppermute | solution.py:32
  446.0 9.6 %collective-permute-start.39 = (bf16[64,3072]{1,0:T(8,128)(2,1)S(1)}, bf16[64,3072]{1,0:T(8,128)(2,1)S(1)}, u32[]{:S(2)}, u32[]{:S(2)}) collective-permute-start(bf16[64,3072]{1,0:T(8,128)(2,1)S(1)} %fusion.120), channel_id=1, source_target_pairs={{0,4},{8,0},{16,8},{24,16},{28,24},{20,28},{12,20},{4,12},{1,5},{9... | collective-permute-start | bytes 1179656 | tf_op jit(solution)/shard_map/ppermute | solution.py:32
  448.2 9.3 %collective-permute-start.35 = (bf16[64,3072]{1,0:T(8,128)(2,1)S(1)}, bf16[64,3072]{1,0:T(8,128)(2,1)S(1)}, u32[]{:S(2)}, u32[]{:S(2)}) collective-permute-start(bf16[64,3072]{1,0:T(8,128)(2,1)S(1)} %fusion.122), channel_id=1, source_target_pairs={{0,8},{8,16},{16,24},{24,28},{28,20},{20,12},{12,4},{4,0},{1,9},{9... | collective-permute-start | bytes 1179656 | tf_op jit(solution)/shard_map/ppermute | solution.py:32
  455.7 8.7 %collective-permute-start.40 = (bf16[64,3072]{1,0:T(8,128)(2,1)S(1)}, bf16[64,3072]{1,0:T(8,128)(2,1)S(1)}, u32[]{:S(2)}, u32[]{:S(2)}) collective-permute-start(bf16[64,3072]{1,0:T(8,128)(2,1)S(1)} %fusion.121), channel_id=1, source_target_pairs={{0,4},{8,0},{16,8},{24,16},{28,24},{20,28},{12,20},{4,12},{1,5},{9... | collective-permute-start | bytes 1179656 | tf_op jit(solution)/shard_map/ppermute | solution.py:32
  457.7 8.4 %collective-permute-start.36 = (bf16[64,3072]{1,0:T(8,128)(2,1)S(1)}, bf16[64,3072]{1,0:T(8,128)(2,1)S(1)}, u32[]{:S(2)}, u32[]{:S(2)}) collective-permute-start(bf16[64,3072]{1,0:T(8,128)(2,1)S(1)} %fusion.123), channel_id=1, source_target_pairs={{0,8},{8,16},{16,24},{24,28},{28,20},{20,12},{12,4},{4,0},{1,9},{9... | collective-permute-start | bytes 1179656 | tf_op jit(solution)/shard_map/ppermute | solution.py:32
  466.2 7.8 %collective-permute-start.41 = (bf16[64,3072]{1,0:T(8,128)(2,1)S(1)}, bf16[64,3072]{1,0:T(8,128)(2,1)S(1)}, u32[]{:S(2)}, u32[]{:S(2)}) collective-permute-start(bf16[64,3072]{1,0:T(8,128)(2,1)S(1)} %fusion.125), channel_id=1, source_target_pairs={{0,2},{2,0},{1,3},{3,1},{4,6},{6,4},{5,7},{7,5},{8,10},{10,8},{9,1... | collective-permute-start | bytes 1179656 | tf_op jit(solution)/shard_map/ppermute | solution.py:76
  475.6 30.5 %collective-permute-start.49 = (bf16[64,3072]{1,0:T(8,128)(2,1)S(1)}, bf16[64,3072]{1,0:T(8,128)(2,1)S(1)}, u32[]{:S(2)}, u32[]{:S(2)}) collective-permute-start(bf16[64,3072]{1,0:T(8,128)(2,1)S(1)} %get-tuple-element.64), channel_id=1, source_target_pairs={{0,8},{8,16},{16,24},{24,28},{28,20},{20,12},{12,4},{4,0},{1,9},{9... | collective-permute-start | bytes 1179656 | tf_op jit(solution)/shard_map/ppermute | solution.py:32
  476.0 30.5 %collective-permute-start.43 = (bf16[64,3072]{1,0:T(8,128)(2,1)S(1)}, bf16[64,3072]{1,0:T(8,128)(2,1)}, u32[]{:S(2)}, u32[]{:S(2)}) collective-permute-start(bf16[64,3072]{1,0:T(8,128)(2,1)S(1)} %get-tuple-element.64), channel_id=1, source_target_pairs={{0,4},{8,0},{16,8},{24,16},{28,24},{20,28},{12,20},{4,12},{1,5},{9... | collective-permute-start | bytes 1179656 | tf_op jit(solution)/shard_map/ppermute | solution.py:32
  477.6 30.7 %collective-permute-start.42 = (bf16[64,3072]{1,0:T(8,128)(2,1)S(1)}, bf16[64,3072]{1,0:T(8,128)(2,1)}, u32[]{:S(2)}, u32[]{:S(2)}) collective-permute-start(bf16[64,3072]{1,0:T(8,128)(2,1)S(1)} %get-tuple-element.64), channel_id=1, source_target_pairs={{0,1},{1,0},{2,3},{3,2},{4,5},{5,4},{6,7},{7,6},{8,9},{9,8},{10,11... | collective-permute-start | bytes 1179656 | tf_op jit(solution)/shard_map/ppermute | solution.py:76
  506.1 42.7 %collective-permute-start.57 = (bf16[64,3072]{1,0:T(8,128)(2,1)S(1)}, bf16[64,3072]{1,0:T(8,128)(2,1)S(1)}, u32[]{:S(2)}, u32[]{:S(2)}) collective-permute-start(bf16[64,3072]{1,0:T(8,128)(2,1)S(1)} %collective-permute-done.49), channel_id=1, source_target_pairs={{0,1},{1,0},{2,3},{3,2},{4,5},{5,4},{6,7},{7,6},{8,9},{9,8},{10,11... | collective-permute-start | bytes 1179656 | tf_op jit(solution)/shard_map/ppermute | solution.py:76
  506.2 13.5 %collective-permute-start.50 = (bf16[64,3072]{1,0:T(8,128)(2,1)S(1)}, bf16[64,3072]{1,0:T(8,128)(2,1)S(1)}, u32[]{:S(2)}, u32[]{:S(2)}) collective-permute-start(bf16[64,3072]{1,0:T(8,128)(2,1)S(1)} %collective-permute-done.49), channel_id=1, source_target_pairs={{0,8},{8,16},{16,24},{24,28},{28,20},{20,12},{12,4},{4,0},{1,9},{9... | collective-permute-start | bytes 1179656 | tf_op jit(solution)/shard_map/ppermute | solution.py:32
  506.5 11.4 %collective-permute-start.45 = (bf16[64,3072]{1,0:T(8,128)(2,1)}, bf16[64,3072]{1,0:T(8,128)(2,1)S(1)}, u32[]{:S(2)}, u32[]{:S(2)}) collective-permute-start(bf16[64,3072]{1,0:T(8,128)(2,1)} %collective-permute-done.43), channel_id=1, source_target_pairs={{0,4},{8,0},{16,8},{24,16},{28,24},{20,28},{12,20},{4,12},{1,5},{9... | collective-permute-start | bytes 1179656 | tf_op jit(solution)/shard_map/ppermute | solution.py:32
  508.3 11.4 %collective-permute-start.44 = (bf16[64,3072]{1,0:T(8,128)(2,1)}, bf16[64,3072]{1,0:T(8,128)(2,1)S(1)}, u32[]{:S(2)}, u32[]{:S(2)}) collective-permute-start(bf16[64,3072]{1,0:T(8,128)(2,1)} %collective-permute-done.43), channel_id=1, source_target_pairs={{0,1},{1,0},{2,3},{3,2},{4,5},{5,4},{6,7},{7,6},{8,9},{9,8},{10,11... | collective-permute-start | bytes 1179656 | tf_op jit(solution)/shard_map/ppermute | solution.py:76
  517.9 13.6 %collective-permute-start.47 = (bf16[64,3072]{1,0:T(8,128)(2,1)S(1)}, bf16[64,3072]{1,0:T(8,128)(2,1)S(1)}, u32[]{:S(2)}, u32[]{:S(2)}) collective-permute-start(bf16[64,3072]{1,0:T(8,128)(2,1)S(1)} %collective-permute-done.45), channel_id=1, source_target_pairs={{0,4},{8,0},{16,8},{24,16},{28,24},{20,28},{12,20},{4,12},{1,5},{9... | collective-permute-start | bytes 1179656 | tf_op jit(solution)/shard_map/ppermute | solution.py:32
  519.7 13.7 %collective-permute-start.46 = (bf16[64,3072]{1,0:T(8,128)(2,1)S(1)}, bf16[64,3072]{1,0:T(8,128)(2,1)S(1)}, u32[]{:S(2)}, u32[]{:S(2)}) collective-permute-start(bf16[64,3072]{1,0:T(8,128)(2,1)S(1)} %collective-permute-done.45), channel_id=1, source_target_pairs={{0,1},{1,0},{2,3},{3,2},{4,5},{5,4},{6,7},{7,6},{8,9},{9,8},{10,11... | collective-permute-start | bytes 1179656 | tf_op jit(solution)/shard_map/ppermute | solution.py:76
  519.7 11.5 %collective-permute-start.51 = (bf16[64,3072]{1,0:T(8,128)(2,1)S(1)}, bf16[64,3072]{1,0:T(8,128)(2,1)S(1)}, u32[]{:S(2)}, u32[]{:S(2)}) collective-permute-start(bf16[64,3072]{1,0:T(8,128)(2,1)S(1)} %collective-permute-done.50), channel_id=1, source_target_pairs={{0,8},{8,16},{16,24},{24,28},{28,20},{20,12},{12,4},{4,0},{1,9},{9... | collective-permute-start | bytes 1179656 | tf_op jit(solution)/shard_map/ppermute | solution.py:32
  537.8 11.0 %collective-permute-start.56 = (bf16[64,3072]{1,0:T(8,128)(2,1)S(1)}, bf16[64,3072]{1,0:T(8,128)(2,1)S(1)}, u32[]{:S(2)}, u32[]{:S(2)}) collective-permute-start(bf16[64,3072]{1,0:T(8,128)(2,1)S(1)} %collective-permute-done.50), channel_id=1, source_target_pairs={{0,1},{1,0},{2,3},{3,2},{4,5},{5,4},{6,7},{7,6},{8,9},{9,8},{10,11... | collective-permute-start | bytes 1179656 | tf_op jit(solution)/shard_map/ppermute | solution.py:76
  537.9 10.8 %collective-permute-start.55 = (bf16[64,3072]{1,0:T(8,128)(2,1)S(1)}, bf16[64,3072]{1,0:T(8,128)(2,1)S(1)}, u32[]{:S(2)}, u32[]{:S(2)}) collective-permute-start(bf16[64,3072]{1,0:T(8,128)(2,1)S(1)} %collective-permute-done.51), channel_id=1, source_target_pairs={{0,1},{1,0},{2,3},{3,2},{4,5},{5,4},{6,7},{7,6},{8,9},{9,8},{10,11... | collective-permute-start | bytes 1179656 | tf_op jit(solution)/shard_map/ppermute | solution.py:76
  538.3 10.2 %collective-permute-start.54 = (bf16[64,3072]{1,0:T(8,128)(2,1)S(1)}, bf16[64,3072]{1,0:T(8,128)(2,1)S(1)}, u32[]{:S(2)}, u32[]{:S(2)}) collective-permute-start(bf16[64,3072]{1,0:T(8,128)(2,1)S(1)} %pad_maximum_fusion.9), channel_id=1, source_target_pairs={{0,1},{1,0},{2,3},{3,2},{4,5},{5,4},{6,7},{7,6},{8,9},{9,8},{10,11... | collective-permute-start | bytes 1179656 | tf_op jit(solution)/shard_map/ppermute | solution.py:76
  626.3 10.7 %collective-permute-start.63 = (bf16[64,3072]{1,0:T(8,128)(2,1)S(1)}, bf16[64,3072]{1,0:T(8,128)(2,1)S(1)}, u32[]{:S(2)}, u32[]{:S(2)}) collective-permute-start(bf16[64,3072]{1,0:T(8,128)(2,1)S(1)} %pad_maximum_fusion.12), channel_id=1, source_target_pairs={{0,4},{8,0},{16,8},{24,16},{28,24},{20,28},{12,20},{4,12},{1,5},{9... | collective-permute-start | bytes 1179656 | tf_op jit(solution)/shard_map/ppermute | solution.py:32
  628.5 9.9 %collective-permute-start.59 = (bf16[64,3072]{1,0:T(8,128)(2,1)S(1)}, bf16[64,3072]{1,0:T(8,128)(2,1)S(1)}, u32[]{:S(2)}, u32[]{:S(2)}) collective-permute-start(bf16[64,3072]{1,0:T(8,128)(2,1)S(1)} %pad_maximum_fusion.11), channel_id=1, source_target_pairs={{0,8},{8,16},{16,24},{24,28},{28,20},{20,12},{12,4},{4,0},{1,9},{9... | collective-permute-start | bytes 1179656 | tf_op jit(solution)/shard_map/ppermute | solution.py:32
  637.1 9.8 %collective-permute-start.64 = (bf16[64,3072]{1,0:T(8,128)(2,1)S(1)}, bf16[64,3072]{1,0:T(8,128)(2,1)S(1)}, u32[]{:S(2)}, u32[]{:S(2)}) collective-permute-start(bf16[64,3072]{1,0:T(8,128)(2,1)S(1)} %fusion.114), channel_id=1, source_target_pairs={{0,4},{8,0},{16,8},{24,16},{28,24},{20,28},{12,20},{4,12},{1,5},{9... | collective-permute-start | bytes 1179656 | tf_op jit(solution)/shard_map/ppermute | solution.py:32
  638.5 9.0 %collective-permute-start.60 = (bf16[64,3072]{1,0:T(8,128)(2,1)S(1)}, bf16[64,3072]{1,0:T(8,128)(2,1)S(1)}, u32[]{:S(2)}, u32[]{:S(2)}) collective-permute-start(bf16[64,3072]{1,0:T(8,128)(2,1)S(1)} %fusion.116), channel_id=1, source_target_pairs={{0,8},{8,16},{16,24},{24,28},{28,20},{20,12},{12,4},{4,0},{1,9},{9... | collective-permute-start | bytes 1179656 | tf_op jit(solution)/shard_map/ppermute | solution.py:32
  647.0 10.9 %collective-permute-start.65 = (bf16[64,3072]{1,0:T(8,128)(2,1)S(1)}, bf16[64,3072]{1,0:T(8,128)(2,1)S(1)}, u32[]{:S(2)}, u32[]{:S(2)}) collective-permute-start(bf16[64,3072]{1,0:T(8,128)(2,1)S(1)} %fusion.115), channel_id=1, source_target_pairs={{0,4},{8,0},{16,8},{24,16},{28,24},{20,28},{12,20},{4,12},{1,5},{9... | collective-permute-start | bytes 1179656 | tf_op jit(solution)/shard_map/ppermute | solution.py:32
  647.6 10.4 %collective-permute-start.61 = (bf16[64,3072]{1,0:T(8,128)(2,1)S(1)}, bf16[64,3072]{1,0:T(8,128)(2,1)S(1)}, u32[]{:S(2)}, u32[]{:S(2)}) collective-permute-start(bf16[64,3072]{1,0:T(8,128)(2,1)S(1)} %fusion.117), channel_id=1, source_target_pairs={{0,8},{8,16},{16,24},{24,28},{28,20},{20,12},{12,4},{4,0},{1,9},{9... | collective-permute-start | bytes 1179656 | tf_op jit(solution)/shard_map/ppermute | solution.py:32
  650.5 9.3 %collective-permute-start.85 = (f32[1,256]{1,0:T(1,128)S(1)}, f32[1,256]{1,0:T(1,128)S(1)}, u32[]{:S(2)}, u32[]{:S(2)}) collective-permute-start(f32[1,256]{1,0:T(1,128)S(1)} %pad_maximum_fusion.17), channel_id=1, source_target_pairs={{0,4},{8,0},{16,8},{24,16},{28,24},{20,28},{12,20},{4,12},{1,5},{9... | collective-permute-start | bytes 3080 | tf_op jit(solution)/shard_map/ppermute | solution.py:32
  659.2 7.9 %collective-permute-start.66 = (bf16[64,3072]{1,0:T(8,128)(2,1)S(1)}, bf16[64,3072]{1,0:T(8,128)(2,1)S(1)}, u32[]{:S(2)}, u32[]{:S(2)}) collective-permute-start(bf16[64,3072]{1,0:T(8,128)(2,1)S(1)} %fusion.119), channel_id=1, source_target_pairs={{0,2},{2,0},{1,3},{3,1},{4,6},{6,4},{5,7},{7,5},{8,10},{10,8},{9,1... | collective-permute-start | bytes 1179656 | tf_op jit(solution)/shard_map/ppermute | solution.py:76
  (176 other events, 1278.7 us)

commit v2 on v1

v2 whole, which is shorter than its diff:
```python
import math

import jax
import jax.numpy as jnp
from jax import lax
from jax.experimental import pallas as pl
from jax.experimental.pallas import tpu as pltpu
from jax.sharding import PartitionSpec as P

HD = 128
BLK = 128
STEPS = 2
EPS = 1e-06
NEG_BIG = -1e30
F32 = jnp.float32
BF16 = jnp.bfloat16


def after(value, *others):
    return lax.optimization_barrier((value,) + others)[0]


def dot(a, b):
    return jnp.dot(a, b, preferred_element_type=F32)


def dot_t(a, b):
    return lax.dot_general(a, b, (((1,), (1,)), ((), ())), preferred_element_type=F32)


def cycle_of(size):
    return list(range(0, size, 2)) + list(range(size - 1, 0, -2))


def ring_shift(x, cycle, shift):
    size = len(cycle)
    pairs = [(cycle[i], cycle[(i + shift) % size]) for i in range(size)]
    return lax.ppermute(x, "ctx", pairs)


def ring_gather(own, cycle, split_axis, jobs=()):
    size = len(cycle)
    reach = size // 2
    slots = [None] * size
    slots[0] = own
    fore = back = own
    jobs = list(jobs)
    for hop in range(1, reach):
        new_back = ring_shift(back, cycle, 1)
        new_fore = ring_shift(fore, cycle, -1)
        done = jobs.pop(0)(back) if jobs else []
        slots[size - hop], slots[hop] = new_back, new_fore
        back, fore = after(new_back, *done), after(new_fore, *done)
    first = ring_shift(jnp.split(back, 2, axis=split_axis)[0], cycle, 1)
    second = ring_shift(jnp.split(fore, 2, axis=split_axis)[1], cycle, -1)
    done = jobs.pop(0)(back) if jobs else []
    slots[reach] = after(jnp.concatenate([first, second], axis=split_axis), *done)
    while jobs:
        jobs.pop(0)(slots[reach])
    return slots


def ring_reduce(parts, cycle, wire, jobs=()):
    size = len(cycle)
    reach = size // 2
    width = parts[0].shape[1] // 2
    jobs = list(jobs)
    far = parts[reach].astype(wire)
    up = ring_shift(far[:, :width], cycle, 1)
    down = ring_shift(far[:, width:], cycle, -1)
    done = jobs.pop(0)(far) if jobs else []
    up, down = after(up, *done).astype(F32), after(down, *done).astype(F32)
    for hop in range(reach - 1, 0, -1):
        up_part, down_part = parts[hop], parts[size - hop]
        if hop == reach - 1:
            up = jnp.concatenate([up_part[:, :width] + up, up_part[:, width:].astype(F32)], axis=1)
            down = jnp.concatenate([down_part[:, :width].astype(F32), down_part[:, width:] + down], axis=1)
        else:
            up = up_part + up
            down = down_part + down
        up, down = up.astype(wire), down.astype(wire)
        new_up, new_down = ring_shift(up, cycle, 1), ring_shift(down, cycle, -1)
        done = jobs.pop(0)(up) if jobs else []
        up, down = after(new_up, *done).astype(F32), after(new_down, *done).astype(F32)
    while jobs:
        jobs.pop(0)(up)
    return parts[0] + up + down


def swap(x, axis):
    return lax.ppermute(x, axis, [(0, 1), (1, 0)])


def join_tp(own, axis):
    if lax.axis_size("tp") == 2:
        other = swap(own, "tp")
        first = lax.axis_index("tp") == 0
        low = jnp.where(first, own, other)
        high = jnp.where(first, other, own)
        return jnp.concatenate([low, high], axis=axis)
    return lax.all_gather(own, "tp", axis=axis, tiled=True)


def sum_tp(own):
    if lax.axis_size("tp") == 2:
        return own.astype(F32) + swap(own, "tp").astype(F32)
    return jnp.sum(lax.all_gather(own, "tp", axis=0, tiled=False).astype(F32), axis=0)


def join_probe(own, axis):
    other = swap(own, "probe")
    first = lax.axis_index("probe") == 0
    return jnp.concatenate([jnp.where(first, own, other), jnp.where(first, other, own)], axis=axis)


def assemble(pieces, places, shape, tail, offset):
    count = len(places)

    def kernel(offset_ref, *refs):
        ins, out = refs[:len(pieces)], refs[len(pieces)]
        sems = refs[-1]
        base = offset_ref[0]
        copies = []
        for index, (piece, start, height, row, side) in enumerate(places):
            source = ins[piece]
            width = pieces[piece].shape[1]
            if tail and side != "other":
                width -= tail
                copies.append(
                    pltpu.make_async_copy(
                        source.at[pl.ds(start, height), pl.ds(width, tail)],
                        refs[len(pieces) + 1].at[pl.ds(row, height), :],
                        sems.at[count + index],
                    )
                )
            if side == "all":
                target = out.at[pl.ds(row, height), :]
            else:
                column = pl.multiple_of(base if side == "own" else shape[1] - width - base, 128)
                target = out.at[pl.ds(row, height), pl.ds(column, width)]
            main = source.at[pl.ds(start, height), pl.ds(0, width)]
            copies.append(pltpu.make_async_copy(main, target, sems.at[index]))
        for copy in copies:
            copy.start()
        for copy in copies:
            copy.wait()

    size = pieces[0].dtype.itemsize * shape[0] * (shape[1] + tail)
    shapes = [jax.ShapeDtypeStruct(shape, pieces[0].dtype)]
    if tail:
        shapes.append(jax.ShapeDtypeStruct((shape[0], tail), pieces[0].dtype))
    outs = pl.pallas_call(
        kernel,
        out_shape=shapes,
        in_specs=[pl.BlockSpec(memory_space=pltpu.SMEM)] + [pl.BlockSpec(memory_space=pl.ANY)] * len(pieces),
        out_specs=[pl.BlockSpec(memory_space=pltpu.VMEM)] * len(shapes),
        scratch_shapes=[pltpu.SemaphoreType.DMA((2 * count if tail else count,))],
        compiler_params=pltpu.CompilerParams(vmem_limit_bytes=size + 4 * 1024 * 1024),
        cost_estimate=pl.CostEstimate(flops=0, bytes_accessed=2 * size, transcendentals=0),
    )(offset, *pieces)
    return outs if tail else outs[0]


def place_units(own, twin, probe, which):
    size, _, high, wide = own.shape
    shape = (2 * size * high, wide) if which == 0 else (2 * high, size * wide)

    def kernel(probe_ref, own_ref, twin_ref, out, sems):
        me = probe_ref[0]
        copies = []
        for ref, part in ((own_ref, me), (twin_ref, 1 - me)):
            for c in range(size):
                if which == 0:
                    start = pl.multiple_of((2 * c + part) * high, high)
                    target = out.at[pl.ds(start, high), :]
                else:
                    start = pl.multiple_of(part * high, high)
                    target = out.at[pl.ds(start, high), pl.ds(c * wide, wide)]
                copies.append(pltpu.make_async_copy(ref.at[c, which], target, sems.at[len(copies)]))
        for copy in copies:
            copy.start()
        for copy in copies:
            copy.wait()

    size_bytes = own.dtype.itemsize * shape[0] * shape[1]
    return pl.pallas_call(
        kernel,
        out_shape=jax.ShapeDtypeStruct(shape, own.dtype),
        in_specs=[pl.BlockSpec(memory_space=pltpu.SMEM)] + [pl.BlockSpec(memory_space=pl.ANY)] * 2,
        out_specs=pl.BlockSpec(memory_space=pltpu.VMEM),
        scratch_shapes=[pltpu.SemaphoreType.DMA((2 * size,))],
        compiler_params=pltpu.CompilerParams(vmem_limit_bytes=size_bytes + 4 * 1024 * 1024),
        cost_estimate=pl.CostEstimate(flops=0, bytes_accessed=2 * size_bytes, transcendentals=0),
    )(probe, own, twin)


def sign_products(parts, starts, scale, weights):
    tokens = parts[0].shape[0]
    width = weights[0].shape[0]
    widths = [weight.shape[1] for weight in weights]
    count = len(weights)
    block = 256 if tokens % 256 == 0 else tokens

    def kernel(starts_ref, scale_ref, *refs):
        outs = refs[count + len(parts):]
        totals = [None] * count
        for index, part_ref in enumerate(refs[count:count + len(parts)]):
            span = pl.ds(pl.multiple_of(starts_ref[index], 128), part_ref.shape[1])
            scaled = part_ref[...] * scale_ref[:, span]
            for at in range(count):
                product = dot(scaled, refs[at][span, :])
                totals[at] = product if index == 0 else totals[at] + product
        for total, out_ref in zip(totals, outs):
            out_ref[...] = total.astype(BF16)

    return pl.pallas_call(
        kernel,
        grid=(tokens // block,),
        out_shape=[jax.ShapeDtypeStruct((tokens, columns), BF16) for columns in widths],
        in_specs=[pl.BlockSpec(memory_space=pltpu.SMEM), pl.BlockSpec((1, width), lambda i: (0, 0))]
        + [pl.BlockSpec(weight.shape, lambda i: (0, 0)) for weight in weights]
        + [pl.BlockSpec((block, part.shape[1]), lambda i: (i, 0)) for part in parts],
        out_specs=[pl.BlockSpec((block, columns), lambda i: (i, 0)) for columns in widths],
        compiler_params=pltpu.CompilerParams(vmem_limit_bytes=48 * 1024 * 1024),
        cost_estimate=pl.CostEstimate(
            flops=2 * tokens * width * sum(widths),
            bytes_accessed=2 * (tokens * width + width * sum(widths) + tokens * sum(widths)),
            transcendentals=0,
        ),
    )(starts, scale, *weights, *parts)


def lanes_of(values, count):
    lane = lax.broadcasted_iota(jnp.int32, (values[0].shape[0], count), 1)
    tile = jnp.zeros(lane.shape, F32)
    for index, value in enumerate(values):
        tile = jnp.where(lane == index, value, tile)
    return tile


def row_sums(rows, own_sign, twin_sign):
    total = [jnp.sum(rows, axis=1, keepdims=True), jnp.sum(rows * rows, axis=1, keepdims=True)]
    for sign in (own_sign.astype(F32), twin_sign.astype(F32)):
        total += [jnp.sum(sign, axis=1, keepdims=True), jnp.sum(rows * sign, axis=1, keepdims=True)]
    return total


def partial_sums(rows, own_sign, twin_sign):
    def kernel(rows_ref, own_ref, twin_ref, out_ref):
        out_ref[...] = lanes_of(row_sums(rows_ref[...], own_ref[...], twin_ref[...]), 128)

    return pl.pallas_call(kernel, out_shape=jax.ShapeDtypeStruct((rows.shape[0], 128), F32))(
        rows, own_sign, twin_sign
    )


def write_packet(packet_ref, rows, sums, mod, lists, full_width):
    width = rows.shape[1]
    means = [value / full_width for value in sums]
    inv_std = lax.rsqrt(means[1] - means[0] * means[0] + EPS)
    unit_rows = (rows - means[0]) * inv_std
    packet_ref[:, 0:width] = (unit_rows * (1.0 + mod[1:2]) + mod[0:1]).astype(BF16)
    scalars = [inv_std]
    for index in (2, 4):
        scalars += [means[index], (means[index + 1] - means[0] * means[index]) * inv_std]
    high = [value.astype(BF16).astype(F32) for value in scalars]
    low = [value - part for value, part in zip(scalars, high)]
    tail = lanes_of(high + low, 128) + lists.astype(F32)
    packet_ref[:, width:width + 128] = tail.astype(BF16)


def first_packet(rows, sums_own, sums_other, mod, lists, full_width):
    def kernel(rows_ref, own_ref, other_ref, mod_ref, lists_ref, packet_ref):
        sums = own_ref[...] + other_ref[...]
        sums = [sums[:, i:i + 1] for i in range(6)]
        write_packet(packet_ref, rows_ref[...], sums, mod_ref[...], lists_ref[...], full_width)

    height, width = rows.shape
    return pl.pallas_call(kernel, out_shape=jax.ShapeDtypeStruct((height, width + 128), BF16))(
        rows, sums_own, sums_other, mod, lists
    )


def next_packet(rows, branch_own, branch_other, gate, own_sign, twin_sign, mod, lists, step_size):
    def kernel(rows_ref, own_ref, other_ref, gate_ref, own_sign_ref, twin_sign_ref, mod_ref, lists_ref,
               new_ref, packet_ref):
        branch = own_ref[...].astype(F32) + other_ref[...].astype(F32)
        new = rows_ref[...] + step_size * (gate_ref[...] * branch)
        new_ref[...] = new
        sums = row_sums(new, own_sign_ref[...], twin_sign_ref[...])
        write_packet(packet_ref, new, sums, mod_ref[...], lists_ref[...], new.shape[1])

    height, width = rows.shape
    return pl.pallas_call(
        kernel,
        out_shape=[
            jax.ShapeDtypeStruct((height, width), F32),
            jax.ShapeDtypeStruct((height, width + 128), BF16),
        ],
        compiler_params=pltpu.CompilerParams(vmem_limit_bytes=24 * 1024 * 1024),
    )(rows, branch_own, branch_other, gate, own_sign, twin_sign, mod, lists)


def token_scalars(tails, own_half):
    sums = tails[:, 0:5].astype(F32) + tails[:, 5:10].astype(F32)
    if own_half:
        return sums[:, 0:1], sums[:, 1:2], sums[:, 2:3]
    return sums[:, 0:1], sums[:, 3:4], sums[:, 4:5]


def mlp_tangent(pre_hidden, sign, consts, tails, back):
    tokens, units = sign.shape
    half = tokens // 2
    lanes = HD if units % HD == 0 else units

    def kernel(own_ref, twin_ref, sign_ref, const_ref, own_tail_ref, twin_tail_ref, back_ref, out_ref):
        for part, pre_ref, tail_ref in ((0, own_ref, own_tail_ref), (1, twin_ref, twin_tail_ref)):
            rows = pl.ds(part * half, half)
            inv, mean, cross = token_scalars(tail_ref[...], part == 0)
            pre = pre_ref[...]
            tan = inv * (sign_ref[rows, :].astype(F32) - mean * const_ref[0:1] - cross * (pre - const_ref[1:2]))
            inner = math.sqrt(2.0 / math.pi) * (pre + 0.044715 * (pre * pre * pre))
            bend = jnp.tanh(inner)
            slope = math.sqrt(2.0 / math.pi) * (1.0 + 3.0 * 0.044715 * (pre * pre))
            gelu_slope = 0.5 * (1.0 + bend) + 0.5 * pre * (1.0 - bend * bend) * slope
            product = gelu_slope * tan * back_ref[rows, :].astype(F32)
            out_ref[rows, :] = sum(product[:, i:i + lanes] for i in range(0, units, lanes))

    return pl.pallas_call(
        kernel,
        out_shape=jax.ShapeDtypeStruct((tokens, lanes), F32),
        compiler_params=pltpu.CompilerParams(vmem_limit_bytes=48 * 1024 * 1024),
        cost_estimate=pl.CostEstimate(
            flops=6000 * tokens * units, bytes_accessed=10 * tokens * units, transcendentals=tokens * units
        ),
    )(pre_hidden[0], pre_hidden[1], sign, consts, tails[0], tails[1], back)


def normed_head(raw, gain):
    inv = lax.rsqrt(jnp.mean(raw * raw, axis=1, keepdims=True) + EPS)
    return (raw * inv * gain).astype(BF16), inv


def attention(raw_own, raw_twin, bias, q_gain, k_gain, heads):
    queries, tokens = bias.shape
    half = tokens // 2
    scale = 1.0 / math.sqrt(HD)

    def kernel(q_ref, k_ref, v_ref, k_twin_ref, v_twin_ref, bias_ref, qg_ref, kg_ref, out_ref):
        q_n, _ = normed_head(q_ref[...], qg_ref[...])
        k_n = jnp.concatenate(
            [normed_head(k_ref[...], kg_ref[...])[0], normed_head(k_twin_ref[...], kg_ref[...])[0]], axis=0
        )
        v_n = jnp.concatenate([v_ref[...].astype(BF16), v_twin_ref[...].astype(BF16)], axis=0)
        scores = dot_t(q_n, k_n) * scale + bias_ref[...]
        weights = jnp.exp(scores - jnp.max(scores, axis=1, keepdims=True))
        total = jnp.sum(weights, axis=1, keepdims=True)
        out_ref[...] = (dot(weights.astype(BF16), v_n) / total).astype(BF16)

    def columns(part, height):
        return pl.BlockSpec((height, HD), lambda h: (0, part * heads + h))

    return pl.pallas_call(
        kernel,
        grid=(heads,),
        out_shape=jax.ShapeDtypeStruct((queries, heads * HD), BF16),
        in_specs=[
            columns(0, queries),
            columns(1, half),
            columns(2, half),
            columns(1, half),
            columns(2, half),
            pl.BlockSpec((queries, tokens), lambda h: (0, 0)),
            columns(0, 1),
            columns(0, 1),
        ],
        out_specs=columns(0, queries),
        compiler_params=pltpu.CompilerParams(vmem_limit_bytes=32 * 1024 * 1024),
        cost_estimate=pl.CostEstimate(
            flops=30 * heads * queries * tokens * HD,
            bytes_accessed=12 * heads * tokens * HD + 4 * queries * tokens,
            transcendentals=heads * queries * tokens,
        ),
    )(raw_own, raw_own, raw_own, raw_twin, raw_twin, bias, q_gain, k_gain)


def attention_tangent(
    raw, sign, consts, tails, back, bias, q_gain, k_gain, heads
):
    queries, tokens = bias.shape
    scale = 1.0 / math.sqrt(HD)
    half = tokens // 2

    def kernel(q_ref, k_ref, v_ref, q_twin_ref, k_twin_ref, v_twin_ref, qs_ref, ks_ref, vs_ref, qc_ref, kc_ref,
               vc_ref, tail_ref, tail_twin_ref, back_ref, bias_ref, qg_ref, kg_ref, out_ref):
        head = pl.program_id(0)
        own = token_scalars(tail_ref[...], True)
        twin = token_scalars(tail_twin_ref[...], False)
        every = [jnp.concatenate(pair, axis=0) for pair in zip(own, twin)]

        def tangent(raw_rows, sign_rows, const_ref, columns):
            inv, mean, cross = columns
            return inv * (
                sign_rows.astype(F32) - mean * const_ref[0:1] - cross * (raw_rows - const_ref[1:2])
            )

        def tangent_head(raw_rows, tan, inv, gain):
            tan_inv = -inv * inv * inv * jnp.mean(raw_rows * tan, axis=1, keepdims=True)
            return ((tan * inv + raw_rows * tan_inv) * gain).astype(BF16)

        k_raw = jnp.concatenate([k_ref[...], k_twin_ref[...]], axis=0)
        k_n, k_inv = normed_head(k_raw, kg_ref[...])
        dk_n = tangent_head(k_raw, tangent(k_raw, ks_ref[...], kc_ref, every), k_inv, kg_ref[...])
        keys = jnp.concatenate([k_n, dk_n], axis=1)
        v_raw = jnp.concatenate([v_ref[...], v_twin_ref[...]], axis=0)
        v_n = v_raw.astype(BF16)
        values = jnp.concatenate([v_n, tangent(v_raw, vs_ref[...], vc_ref, every).astype(BF16)], axis=1)
        for part in range(2):
            q_raw = (q_twin_ref if part else q_ref)[...]
            rows = pl.ds(part * half, queries)
            q_n, q_inv = normed_head(q_raw, qg_ref[...])
            columns = [column[:queries] for column in (twin if part else own)]
            dq_n = tangent_head(q_raw, tangent(q_raw, qs_ref[rows, :], qc_ref, columns), q_inv, qg_ref[...])
            scores = dot_t(q_n, k_n) * scale + bias_ref[...]
            weights = jnp.exp(scores - jnp.max(scores, axis=1, keepdims=True))
            inv_total = 1.0 / jnp.sum(weights, axis=1, keepdims=True)
            weighted = weights * (dot_t(jnp.concatenate([dq_n, q_n], axis=1), keys) * scale)
            tan_sum = jnp.sum(weighted, axis=1, keepdims=True) * inv_total
            both = dot(weights.astype(BF16), values) * inv_total
            tan_out = both[:, HD:] + dot(weighted.astype(BF16), v_n) * inv_total - tan_sum * both[:, :HD]
            share = tan_out * back_ref[rows, :].astype(F32)
            span = pl.ds(part * queries, queries)

            @pl.when(head == 0)
            def _():
                out_ref[span, :] = share

            @pl.when(head > 0)
            def _():
                out_ref[span, :] += share

    def columns(part, height):
        return pl.BlockSpec((height, HD), lambda i: (0, part * heads + i))

    def whole(array):
        return pl.BlockSpec(array.shape, lambda i: (0, 0))

    return pl.pallas_call(
        kernel,
        grid=(heads,),
        out_shape=jax.ShapeDtypeStruct((2 * queries, HD), F32),
        in_specs=[columns(0, queries), columns(1, half), columns(2, half)] * 2
        + [columns(i, tokens) for i in range(3)]
        + [columns(i, consts.shape[0]) for i in range(3)]
        + [whole(tails[0]), whole(tails[1]), columns(0, tokens), whole(bias), columns(0, 1), columns(0, 1)],
        out_specs=pl.BlockSpec((2 * queries, HD), lambda i: (0, 0)),
        compiler_params=pltpu.CompilerParams(vmem_limit_bytes=48 * 1024 * 1024),
        cost_estimate=pl.CostEstimate(
            flops=140 * heads * queries * tokens * HD,
            bytes_accessed=32 * heads * tokens * HD + 4 * queries * tokens,
            transcendentals=2 * heads * queries * tokens,
        ),
    )(
        *[raw[0]] * 3, *[raw[1]] * 3, sign, sign, sign, consts, consts, consts, tails[0], tails[1], back, bias,
        q_gain, k_gain,
    )


def local(latent, probes, modulation, pattern, w_qkv, w_out, w_up, w_down, q_gain, k_gain):
    ctx_size = lax.axis_size("ctx")
    tp_size = lax.axis_size("tp")
    cycle = cycle_of(ctx_size)
    row_count, local_width = latent.shape
    half = row_count // 2
    full_width = local_width * tp_size
    tokens = row_count * ctx_size
    heads_local = q_gain.shape[0] // HD
    groups = math.gcd(heads_local, ctx_size)
    heads_own = heads_local // groups
    head_width = heads_own * HD
    queries = groups * half
    unit_total = w_up.shape[1]
    units = unit_total // ctx_size
    list_size = pattern.shape[1]
    step_size = 1.0 / STEPS

    ctx_index = lax.axis_index("ctx")
    probe_index = lax.axis_index("probe")
    tp_index = lax.axis_index("tp")
    first = probe_index == 0
    cycle_arr = jnp.array(cycle, jnp.int32)
    place = jnp.array([cycle.index(i) for i in range(ctx_size)], jnp.int32)
    ring_index = place[ctx_index]
    slot_owner = cycle_arr[(ring_index + jnp.arange(ctx_size)) % ctx_size]
    owner_slot = (place - ring_index) % ctx_size
    group = ring_index % groups
    column_offset = (tp_index * local_width).astype(jnp.int32).reshape(1)

    signs_local = (2 * probes[0] - 1).astype(BF16).reshape(2, half, local_width)
    signs_local = jnp.where(first, signs_local, signs_local[::-1]).reshape(row_count, local_width)
    own_sign, twin_sign = signs_local[:half], swap(signs_local[half:], "probe")
    sign_slots = ring_gather(signs_local, cycle, 1)
    lat_half = lax.dynamic_slice_in_dim(latent, probe_index * half, half, 0)
    rows = join_tp(lat_half, 1)
    places = [
        (k, part * half, half, (part * ctx_size + k) * half, "own") for k in range(ctx_size) for part in range(2)
    ]
    signs = assemble(sign_slots, places, (tokens, local_width), 0, column_offset * 0)
    if tp_size == 2:
        sign_parts = [signs, swap(signs, "tp")]
        sign_starts = jnp.concatenate([column_offset, local_width - column_offset])
        low = tp_index == 0
        block_signs = [
            jnp.concatenate([jnp.where(low, own, other), jnp.where(low, other, own)], axis=1)
            for own, other in ([part[at:at + half] for part in sign_parts] for at in (0, tokens // 2))
        ]
    else:
        sign_parts = [lax.all_gather(signs, "tp", axis=1, tiled=True)]
        sign_starts = column_offset * 0
        block_signs = [sign_parts[0][at:at + half] for at in (0, tokens // 2)]
    own_signs, twin_signs = block_signs[0], swap(block_signs[1], "probe")

    qkv_own = lax.dynamic_slice_in_dim(w_qkv, group * head_width, head_width, 2)
    qkv_own = after(jnp.concatenate([qkv_own[:, part] for part in range(3)], axis=1))
    out_own = lax.dynamic_slice_in_dim(w_out, group * head_width, head_width, 0)
    q_gain_own = lax.dynamic_slice_in_dim(q_gain, group * head_width, head_width, 0)[None]
    k_gain_own = lax.dynamic_slice_in_dim(k_gain, group * head_width, head_width, 0)[None]

    stretches = (1.0 + modulation[:, 1]).astype(BF16)
    gates = modulation[:, 2].astype(BF16)
    lists = jnp.pad(pattern.astype(BF16), ((0, 0), (10, 128 - 10 - list_size)))

    half_tokens = ctx_size * half
    out_turned = out_own.T

    def products(step, back):
        def job(token):
            scale = after((gates if back else stretches)[step][None], token)
            weights = [out_turned, down_turned] if back else [qkv_own, up_own]
            if step == 0:
                made = [early[back]] + list(sign_products(sign_parts, sign_starts, scale, weights[1:]))
            else:
                made = sign_products(sign_parts, sign_starts, scale, weights)
            found[step, back] = made
            return made

        return job

    def head_tangent(step):
        def job(token):
            raw, tails, pre, pairs = kept[step]
            share = attention_tangent(
                (after(raw[0], token), raw[1]), found[step, False][0], pairs[0], tails, found[step, True][0],
                bias, q_gain_own, k_gain_own, heads_own,
            )
            attn_shares.append(share)
            return [share]

        return job

    def unit_tangent(step):
        def job(token):
            raw, tails, pre, pairs = kept[step]
            pre_twin = dot(after(pre[1], token), up_own)
            share = mlp_tangent(
                (pre[0], pre_twin), found[step, False][1], pairs[1], tails, found[step, True][1]
            )
            mlp_shares.append(share)
            return [share]

        return job

    def no_job(token):
        return []

    found = {}
    kept, attn_shares, mlp_shares = [], [], []

    bias = None
    for step in range(STEPS):
        mod = modulation[step]
        shift, stretch, gate = mod[0][None], 1.0 + mod[1][None], mod[2][None]

        if step == 0:
            sums = partial_sums(lat_half, own_sign, twin_sign)
            if tp_size == 2:
                sums_other = swap(sums, "tp")
            else:
                sums_other = lax.psum(sums, "tp") - sums
            packet = first_packet(rows, sums, sums_other, mod, lists, full_width)
            slots = ring_gather(packet, cycle, 0)
            at = slots[0].shape[1] - 128 + 10
            listed = jnp.stack([slots[k][0, at:at + list_size] for k in range(groups)]).astype(jnp.int32)
            listed = jnp.any(listed[:, :, None] == slot_owner[None, None, :], axis=1)
            bias = jnp.where(listed, 0.0, NEG_BIG).astype(F32)
            bias = jnp.tile(jnp.repeat(jnp.repeat(bias, half, axis=0), half, axis=1), (1, 2))
        else:
            rows, packet = next_packet(
                rows, branch, branch_other, last_gate, own_signs, twin_signs, mod, lists, step_size
            )
            jobs = [head_tangent(step - 1), no_job, unit_tangent(step - 1)]
            slots = ring_gather(packet, cycle, 0, jobs)
        places = [(k, 0, half, k * half, "all") for k in range(ctx_size)]
        normed, tails = assemble(slots, places, (half_tokens, full_width), 128, column_offset)

        normed_twin, tails_twin = swap(normed, "probe"), swap(tails, "probe")
        raw_own = dot(normed, qkv_own)
        if step == 0:
            raw_twin = dot(normed_twin, qkv_own)
            attended = attention(raw_own, raw_twin, bias, q_gain_own, k_gain_own, heads_own)

            early = [
                sign_products(sign_parts, sign_starts, after(scales[0][None], attended), [weight])[0]
                for scales, weight in ((stretches, qkv_own), (gates, out_turned))
            ]
            up_late, down_late = after(w_up, slots[ctx_size // 2], signs), after(w_down, slots[ctx_size // 2], signs)
            up_part = lax.dynamic_slice_in_dim(up_late, probe_index * (w_up.shape[0] // 2), w_up.shape[0] // 2, 0)
            up_part = up_part.reshape(-1, ctx_size, units).transpose(1, 0, 2)
            down_part = down_late.reshape(ctx_size, 2, units // 2, w_down.shape[1])
            down_part = lax.dynamic_index_in_dim(down_part, probe_index, 1, keepdims=False)
            fused = up_part.shape == down_part.shape
            if fused:
                got = lax.all_to_all(jnp.stack([up_part, down_part], axis=1), "ctx", 0, 0, tiled=True)
                got = after(got, attended, *early)
                got_twin = swap(got, "probe")
                core = probe_index.astype(jnp.int32).reshape(1)
                up_own = place_units(got, got_twin, core, 0)
                down_own = place_units(got, got_twin, core, 1)
            else:
                got = lax.all_to_all(up_part, "ctx", 0, 0, tiled=True)
                pair = jnp.stack([got, swap(got, "probe")], axis=1)
                up_own = jnp.where(first, pair, pair[:, ::-1]).reshape(full_width, units)
                got = lax.all_to_all(down_part, "ctx", 0, 0, tiled=True)
                down_own = join_probe(got.transpose(1, 0, 2).reshape(units // 2, full_width), 0)
            down_turned = down_own.T

        pre_own = dot(normed, up_own)
        hidden = jax.nn.gelu(pre_own, approximate=True).astype(BF16)
        parts = []
        if groups < ctx_size:
            far = dot(hidden[queries:], down_own)
            parts = [far[k * half:(k + 1) * half] for k in range(ctx_size - groups)]
        if step > 0:
            raw_twin = dot(normed_twin, qkv_own)
            attended = attention(raw_own, raw_twin, bias, q_gain_own, k_gain_own, heads_own)
        near = dot(attended, out_own) + dot(hidden[:queries], down_own)
        parts = [near[k * half:(k + 1) * half] for k in range(groups)] + parts

        pair = jnp.concatenate(
            [stretches[step][None], shift.astype(BF16), jnp.zeros((14, full_width), BF16)], axis=0
        )
        pairs = (dot(pair, qkv_own), dot(pair, up_own))
        kept.append(((raw_own, raw_twin), (tails, tails_twin), (pre_own, normed_twin), pairs))
        if step == 0:
            jobs = [products(0, False), products(0, True), products(1, False), products(1, True)]
        else:
            jobs = [no_job, head_tangent(step), no_job, unit_tangent(step)]
        branch = ring_reduce(parts, cycle, BF16, jobs).astype(BF16)
        if tp_size == 2:
            branch_other = swap(branch, "tp")
        else:
            branch_other = sum_tp(branch) - branch.astype(F32)
        last_gate = gate

    rows = rows + step_size * (last_gate * (branch.astype(F32) + branch_other.astype(F32)))
    estimate = jnp.sum(sum(mlp_shares), axis=1)
    attn_share = jnp.sum(sum(attn_shares), axis=1).reshape(2, queries)
    estimate = estimate + jnp.pad(attn_share, ((0, 0), (0, half_tokens - queries))).reshape(tokens)
    lat_cols = lax.dynamic_slice_in_dim(rows, tp_index * local_width, local_width, 1)
    latent_out = join_probe(lat_cols, 0)

    by_slot = estimate.reshape(2, ctx_size, half)
    by_slot = jnp.where(first, by_slot, by_slot[::-1]).transpose(1, 0, 2).reshape(ctx_size, row_count)
    by_slot = jnp.concatenate([by_slot, jnp.zeros_like(by_slot)], axis=1)
    own_estimate = ring_reduce([by_slot[k:k + 1] for k in range(ctx_size)], cycle, F32)[:, :row_count]
    own_estimate = own_estimate + swap(own_estimate, "probe")
    own_estimate = sum_tp(own_estimate)[0]
    density_change = -step_size * own_estimate / (2 * math.sqrt(full_width))
    return (latent_out, density_change)


def solution(mesh):
    return jax.shard_map(
        local,
        mesh=mesh,
        in_specs=(
            P("ctx", "tp"),
            P("probe", "ctx", "tp"),
            P(),
            P("ctx", None),
            P(None, None, "tp"),
            P("tp", None),
            P("ctx", "tp"),
            P("tp", "ctx"),
            P("tp"),
            P("tp"),
        ),
        out_specs=(P("ctx", "tp"), P("ctx")),
        check_vma=False,
    )
```

time: 685 us -> 429 us (0.63)
  waiting for transfers between devices: 214 us -> 99.6 us
  Pallas kernels: 0 us -> 108 us
  matrix products: 165 us -> 58.1 us
  blocking collectives: 71 us -> 0 us
  local copies, waits for them, and re-layouts: 87 us -> 47.1 us
  starting transfers between devices: 80.4 us -> 66.9 us
  other arithmetic: 47 us -> 37.8 us
    pallas_call x0 -> x20, Pallas kernels: none -> 108 us  [the longest x6 55.3 us: sign_products(): pl.pallas_call(kernel, grid=(tokens // block,), out_shape=[jax.ShapeDtype...]
    ppermute x62 -> x48, waiting for transfers between devices: 156 us -> 61.1 us  [ring_shift(): return lax.ppermute(x, 'ctx', pairs)]
    dot_general x48 -> x18, matrix products: 132 us -> 58.1 us  [dot(): return jnp.dot(a, b, preferred_element_type=F32)]
    all_gather x3 -> x0, blocking collectives: 71 us -> none  [the longest x2 52.5 us: local(): gathered = lax.all_gather(block_scalars, 'ctx', axis=0, tiled=False)]
    dot_general x16 -> x0, matrix products: 33.5 us -> none  [dot_t(): lax.dot_general(a, b, (((1,), (1,)), ((), ())), preferred_element_type=F32)]
    ppermute x62 -> x48, starting transfers between devices: 74.1 us -> 51 us  [ring_shift(): return lax.ppermute(x, 'ctx', pairs)]
    unnamed x350 -> x173, local copies, waits for them, and re-layouts: 43.8 us -> 24.5 us
    ppermute x28 -> x15, waiting for transfers between devices: 57.7 us -> 38.5 us  [swap(): return lax.ppermute(x, axis, [(0, 1), (1, 0)])]
  transfers between devices with their start and end apart: 90 -> 64, of which waited for: 47 -> 29; matrix products, arithmetic and copies ran while one was open for 43% -> 29% of each run, Pallas kernels for 0% -> 25%
where the time goes in v2:
time: 429 us; the launch traced here: 422 us
  Pallas kernels  108 us (25%)
  waiting for transfers between devices  99.6 us (23%)
  starting transfers between devices  66.9 us (16%)
  matrix products  58.1 us (14%)
  local copies, waits for them, and re-layouts  47.1 us (11%)
  other arithmetic  37.8 us (9%)
    ppermute x48, waiting for transfers between devices, ring_shift(): return lax.ppermute(x, 'ctx', pairs)  61.1 us
    dot_general x18, matrix products, dot(): return jnp.dot(a, b, preferred_element_type=F32)  58.1 us
    pallas_call x6, Pallas kernels, sign_products(): pl.pallas_call(kernel, grid=(tokens // block,), out_shape=[jax.ShapeDtype...  55.3 us
    ppermute x48, starting transfers between devices, ring_shift(): return lax.ppermute(x, 'ctx', pairs)  51 us
    ppermute x15, waiting for transfers between devices, swap(): return lax.ppermute(x, axis, [(0, 1), (1, 0)])  38.5 us
    pallas_call x2, Pallas kernels, attention_tangent(): pl.pallas_call(kernel, grid=(heads,), out_shape=jax.ShapeDtypeStruct((2 *...  25.1 us
    unnamed x173, local copies, waits for them, and re-layouts  24.5 us
    convert_element_type x8, other arithmetic, ring_reduce(): up, down = (up.astype(wire), down.astype(wire))  11.1 us
  transfers between devices with their start and end apart: 64, of which 29 were waited for; matrix products, arithmetic and copies ran while one was open for 29% of the time, Pallas kernels for 25%

profile of v2, /device:TPU:0, one launch (start us, length us, event | category | flops | bytes accessed | tf_op | source)
XLA Modules:
  0.0 422.0 jit_solution(10467715859681380033)
XLA Ops:
  1.9 3.0 collective-permute-start
  9.6 2.0 shard_map.131.own_ref
  11.7 2.4 collective-permute-done
  16.8 2.4 shard_map.132.refs_0_
  19.2 1.8 collective-permute-start.3
  26.2 5.6 %collective-permute-done.3.refs_1_ = bf16[64,3200]{1,0:T(8,128)(2,1)S(1)} collective-permute-done((bf16[64,3200]{1,0:T(8,128)(2,1)}, bf16[64,3200]{1,0:T(8,128)(2,1)S(1)}, u32[]{:S(2)}, u32[]{:S(2)}) %collective-permute-start.3) | collective-permute-done | bytes 409632 | tf_op jit(solution)/shard_map/ppermute | solution.py:38
  33.9 3.8 dynamic-slice_bitcast_fusion.2
  37.8 2.5 collective-permute-done.12.refs_1_
  42.3 6.6 %collective-permute-done.4.refs_2_ = bf16[64,3200]{1,0:T(8,128)(2,1)S(1)} collective-permute-done((bf16[64,3200]{1,0:T(8,128)(2,1)S(1)}, bf16[64,3200]{1,0:T(8,128)(2,1)S(1)}, u32[]{:S(2)}, u32[]{:S(2)}) %collective-permute-start.4) | collective-permute-done | bytes 409632 | tf_op jit(solution)/shard_map/ppermute | solution.py:38
  51.0 3.4 pad_maximum_fusion.refs_0_
  54.5 3.0 collective-permute-done.13.refs_2_
  57.5 1.8 collective-permute-start.14
  59.6 6.6 %collective-permute-done.5.refs_3_ = bf16[64,3200]{1,0:T(8,128)(2,1)S(1)} collective-permute-done((bf16[64,3200]{1,0:T(8,128)(2,1)S(1)}, bf16[64,3200]{1,0:T(8,128)(2,1)S(1)}, u32[]{:S(2)}, u32[]{:S(2)}) %collective-permute-start.5) | collective-permute-done | bytes 409632 | tf_op jit(solution)/shard_map/ppermute | solution.py:38
  75.3 1.8 collective-permute-start.19
  85.7 3.1 shard_map.133
  92.2 5.1 %shard_map.135.refs_1_.refs_2_ = bf16[1024,1536]{1,0:T(8,128)(2,1)} custom-call(s32[1]{0:T(128)} %constant.88.clone.1.offset_ref, bf16[128,1536]{1,0:T(8,128)(2,1)S(1)} %bitcast.98, bf16[128,1536]{1,0:T(8,128)(2,1)S(1)} %copy-done.32, bf16[128,1536]{1,0:T(8,128)(2,1)} %collective-permute-done.13.refs_2_, ...), custom_call_target="tpu_custom_call" | custom-call | bytes 6291456 | tf_op jit(solution)/shard_map/pallas_call | solution.py:152
  97.3 1.8 collective-permute-start.20
  101.1 5.7 %all-to-all-start = ((bf16[8,2,192,384]{3,2,1,0:T(8,128)(2,1)}), bf16[8,2,192,384]{3,2,1,0:T(8,128)(2,1)S(1)}, u32[]{:S(2)}, u32[]{:S(2)}) async-start(bf16[8,2,192,384]{3,2,1,0:T(8,128)(2,1)} %pad_maximum_fusion.1), calls=%async_computation | async-start | bytes 4718592 | tf_op jit(solution)/shard_map/all_to_all | solution.py:623
  106.8 3.3 constant_dynamic-slice_fusion.2
  111.7 4.3 %copy.40 = bf16[384,3072]{0,1:T(8,128)(2,1)} copy(bf16[384,3072]{1,0:T(8,128)(2,1)} %constant_dynamic-slice_fusion.2) | data formatting | bytes 4718592
  120.8 8.3 %fusion.63.q_ref.k_ref.v_ref = f32[512,1152]{1,0:T(8,128)S(1)} fusion(bf16[512,3072]{1,0:T(8,128)(2,1)} %get-tuple-element.40, bf16[3072,1152]{1,0:T(8,128)(2,1)} %pad_maximum_fusion.refs_0_), kind=kOutput, calls=%fused_computation.154 | convolution fusion | flops 3623878656 | bytes 12582912 | tf_op jit(solution)/shard_map/dot_general | solution.py:24
  129.2 6.9 %fusion.64.k_twin_ref.v_twin_ref.q_twin_ref = f32[512,1152]{1,0:T(8,128)S(1)} fusion(bf16[512,3072]{1,0:T(8,128)(2,1)} %collective-permute-done.11, bf16[3072,1152]{1,0:T(8,128)(2,1)S(1)} %bitcast.101), kind=kOutput, calls=%fused_computation.155 | convolution fusion | flops 3623878656 | bytes 12582912 | tf_op jit(solution)/shard_map/dot_general | solution.py:24
  136.2 2.9 shard_map.134
  139.1 29.0 %collective-permute-done.20.refs_2_.refs_3_ = bf16[1024,1536]{1,0:T(8,128)(2,1)} collective-permute-done((bf16[1024,1536]{1,0:T(8,128)(2,1)}, bf16[1024,1536]{1,0:T(8,128)(2,1)}, u32[]{:S(2)}, u32[]{:S(2)}) %collective-permute-start.20) | collective-permute-done | bytes 3145760 | tf_op jit(solution)/shard_map/ppermute | solution.py:91
  168.2 5.9 %shard_map.137.back_ref = bf16[1024,384]{1,0:T(8,128)(2,1)S(1)} custom-call(s32[2]{0:T(128)S(1)} %pad_add_fusion.starts_ref, bf16[1,3072]{1,0:T(2,128)(2,1)S(1)} %copy-done.37, bf16[3072,384]{1,0:T(8,128)(2,1)S(1)} %bitcast.88, bf16[1024,1536]{1,0:T(8,128)(2,1)} %shard_map.135.refs_1_.refs_2_, bf16[1024,1536]{1,0:T(8,128)(2,1)} %collective-permute-done.20.refs_2_.refs_3_), custom_call_target="tpu_custom_call" | custom-call | flops 2415919104 | bytes 9437184 | tf_op jit(solution)/shard_map/pallas_call | solution.py:216
  174.9 12.4 %shard_map.136.qs_ref.ks_ref.vs_ref = bf16[1024,1152]{1,0:T(8,128)(2,1)S(1)} custom-call(s32[2]{0:T(128)S(1)} %pad_add_fusion.starts_ref, bf16[1,3072]{1,0:T(2,128)(2,1)S(1)} %copy-done.33, bf16[3072,1152]{1,0:T(8,128)(2,1)} %pad_maximum_fusion.refs_0_, bf16[1024,1536]{1,0:T(8,128)(2,1)} %shard_map.135.refs_1_.refs_2_, ...), custom_call_target="tpu_custom_call" | custom-call | flops 7247757312 | bytes 15728640 | tf_op jit(solution)/shard_map/pallas_call | solution.py:216
  188.8 2.0 collective-permute-start.57
  191.7 2.0 broadcast_select_fusion.1
  194.7 3.6 fusion.65
  198.3 3.2 shard_map.138.refs_0_.refs_1_
  201.6 5.7 %fusion.7 = (bf16[512,384]{1,0:T(8,128)(2,1)}, f32[512,384]{1,0:T(8,128)}) fusion(bf16[512,3072]{1,0:T(8,128)(2,1)} %get-tuple-element.40, bf16[3072,384]{1,0:T(8,128)(2,1)S(1)} %shard_map.138.refs_0_.refs_1_), kind=kOutput, calls=%fused_computation.18 | convolution fusion | flops 1209729024 | bytes 6684672 | tf_op jit(solution)/shard_map/dot_general | solution.py:24
  207.9 2.5 copy.36
  210.3 3.8 fusion.61
  217.3 5.9 %shard_map.140.sign_ref = bf16[1024,384]{1,0:T(8,128)(2,1)S(1)} custom-call(s32[2]{0:T(128)S(1)} %pad_add_fusion.starts_ref, bf16[1,3072]{1,0:T(2,128)(2,1)S(1)} %copy-done.33, bf16[3072,384]{1,0:T(8,128)(2,1)S(1)} %copy-done.3, bf16[1024,1536]{1,0:T(8,128)(2,1)} %shard_map.135.refs_1_.refs_2_, bf16[1024,1536]{1,0:T(8,128)(2,1)} %collective-permute-done.20.refs_2_.refs_3_), custom_call_target="tpu_custom_call" | custom-call | flops 2415919104 | bytes 9437184 | tf_op jit(solution)/shard_map/pallas_call | solution.py:216
  226.6 5.9 %shard_map.141.back_ref = bf16[1024,384]{1,0:T(8,128)(2,1)S(1)} custom-call(s32[2]{0:T(128)S(1)} %pad_add_fusion.starts_ref, bf16[1,3072]{1,0:T(2,128)(2,1)S(1)} %copy-done.37, bf16[3072,384]{1,0:T(8,128)(2,1)S(1)} %bitcast.91, bf16[1024,1536]{1,0:T(8,128)(2,1)} %shard_map.135.refs_1_.refs_2_, bf16[1024,1536]{1,0:T(8,128)(2,1)} %collective-permute-done.20.refs_2_.refs_3_), custom_call_target="tpu_custom_call" | custom-call | flops 2415919104 | bytes 9437184 | tf_op jit(solution)/shard_map/pallas_call | solution.py:216
  232.5 2.8 collective-permute-done.27
  238.7 15.7 %shard_map.142 = (bf16[1024,1152]{1,0:T(8,128)(2,1)S(1)}, bf16[1024,384]{1,0:T(8,128)(2,1)S(1)}) custom-call(s32[2]{0:T(128)S(1)} %pad_add_fusion.starts_ref, bf16[1,3072]{1,0:T(2,128)(2,1)S(1)} %copy-done.36, bf16[3072,1152]{1,0:T(8,128)(2,1)} %pad_maximum_fusion.refs_0_, bf16[3072,384]{1,0:T(8,128)(2,1)S(1)} %copy-done.3, ...), custom_call_target="tpu_custom_call" | custom-call | flops 9663676416 | bytes 18874368 | tf_op jit(solution)/shard_map/pallas_call | solution.py:216
  254.5 1.9 fusion.23
  260.0 9.5 %shard_map.143 = (bf16[1024,384]{1,0:T(8,128)(2,1)S(1)}, bf16[1024,384]{1,0:T(8,128)(2,1)S(1)}) custom-call(s32[2]{0:T(128)S(1)} %pad_add_fusion.starts_ref, bf16[1,3072]{1,0:T(2,128)(2,1)S(1)} %copy-done.38, bf16[3072,384]{1,0:T(8,128)(2,1)S(1)} %bitcast.89, bf16[3072,384]{1,0:T(8,128)(2,1)} %bitcast.90, bf16[1024,1536]{1,0:T(8,128)(2,1)} %shard_map.135.refs_1_.refs_2_, ...), custom_call_target="tpu_custom_call" | custom-call | flops 4831838208 | bytes 12582912 | tf_op jit(solution)/shard_map/pallas_call | solution.py:216
  273.7 4.2 fusion.41.qc_ref.kc_ref.vc_ref
  278.1 2.7 collective-permute-done.30.other_ref
  285.5 12.6 %shard_map.145 = f32[512,128]{1,0:T(8,128)S(1)} custom-call(f32[512,1152]{1,0:T(8,128)S(1)} %copy-done.8, f32[512,1152]{1,0:T(8,128)S(1)} %copy-done.8, f32[512,1152]{1,0:T(8,128)S(1)} %copy-done.8, f32[512,1152]{1,0:T(8,128)} %copy-done.12, f32[512,1152]{1,0:T(8,128)} %copy-done.12, f32[512,1152]{1,0:T(8,128)} %copy-done.12, bf16[1024,1152]{1,0:T(8,128)(2,1)} %copy-done.52, ...), custom_call_target="tpu_custom_call" | custom-call | flops 14092861440 | bytes 13631488 | tf_op jit(solution)/shard_map/pallas_call | solution.py:448
  300.2 4.1 fusion.39.qc_ref.kc_ref.vc_ref
  304.7 3.1 collective-permute-done.34.refs_2_
  309.8 3.7 fusion.66.twin_ref
  315.3 2.3 collective-permute-done.35.refs_3_
  317.5 1.8 collective-permute-start.40
  320.4 3.2 collective-permute-done.40
  325.9 2.8 fusion.15
  331.3 4.3 %fusion.67.q_ref.k_ref.v_ref = f32[512,1152]{1,0:T(8,128)S(1)} fusion(bf16[512,3072]{1,0:T(8,128)(2,1)S(1)} %get-tuple-element.70, bf16[3072,1152]{1,0:T(8,128)(2,1)S(1)} %bitcast.103), kind=kOutput, calls=%fused_computation.158 | convolution fusion | flops 3623878656 | bytes 12582912 | tf_op jit(solution)/shard_map/dot_general | solution.py:24
  337.1 1.9 collective-permute-start.48
  339.0 3.7 collective-permute-done.42
  344.4 4.2 %fusion.68.k_twin_ref.v_twin_ref.q_twin_ref = f32[512,1152]{1,0:T(8,128)S(1)} fusion(bf16[512,3072]{1,0:T(8,128)(2,1)S(1)} %collective-permute-done.41, bf16[3072,1152]{1,0:T(8,128)(2,1)S(1)} %bitcast.103), kind=kOutput, calls=%fused_computation.159 | convolution fusion | flops 3623878656 | bytes 12582912 | tf_op jit(solution)/shard_map/dot_general | solution.py:24
  348.6 2.9 shard_map.148
  355.1 12.6 %shard_map.149 = f32[512,128]{1,0:T(8,128)S(1)} custom-call(f32[512,1152]{1,0:T(8,128)S(1)} %fusion.67.q_ref.k_ref.v_ref, f32[512,1152]{1,0:T(8,128)S(1)} %fusion.67.q_ref.k_ref.v_ref, f32[512,1152]{1,0:T(8,128)S(1)} %fusion.67.q_ref.k_ref.v_ref, f32[512,1152]{1,0:T(8,128)} %copy-done.13, f32[512,1152]{1,0:T(8,128)} %copy-done.13, f32[512,1152]{1,0:T(8,128)} %copy-done.13, ...), custom_call_target="tpu_custom_call" | custom-call | flops 14092861440 | bytes 13631488 | tf_op jit(solution)/shard_map/pallas_call | solution.py:448
  372.9 6.4 %collective-permute-done.49 = bf16[64,3072]{1,0:T(8,128)(2,1)S(1)} collective-permute-done((bf16[64,3072]{1,0:T(8,128)(2,1)S(1)}, bf16[64,3072]{1,0:T(8,128)(2,1)S(1)}, u32[]{:S(2)}, u32[]{:S(2)}) %collective-permute-start.49) | collective-permute-done | bytes 393248 | tf_op jit(solution)/shard_map/ppermute | solution.py:38
  379.3 2.0 fusion.17
  382.9 1.9 fusion.19
  385.6 1.8 fusion.70.twin_ref
  387.5 1.8 shard_map.150
  391.9 2.5 collective-permute-done.53
  395.1 2.9 collective-permute-done.54
  400.1 2.7 collective-permute-start.51
  416.5 3.5 collective-permute-done.62
  (382 shorter events, 122.6 us)
Async XLA Ops:
  1.9 12.2 %collective-permute-start = (f32[64,1536]{1,0:T(8,128)S(1)}, f32[64,1536]{1,0:T(8,128)}, u32[]{:S(2)}, u32[]{:S(2)}) collective-permute-start(f32[64,1536]{1,0:T(8,128)S(1)} %constant_dynamic-slice_fusion.3.rows_ref), channel_id=1, source_target_pairs={{0,2},{2,0},{1,3},{3,1},{4,6},{6,4},{5,7},{7,5},{8,10},{10,8},{9,1... | collective-permute-start | bytes 1179656 | tf_op jit(solution)/shard_map/ppermute | solution.py:91
  7.0 2.0 collective-permute-start.1
  11.6 4.6 %collective-permute-start.2 = (f32[64,128]{1,0:T(8,128)}, f32[64,128]{1,0:T(8,128)S(1)}, u32[]{:S(2)}, u32[]{:S(2)}) collective-permute-start(f32[64,128]{1,0:T(8,128)} %shard_map.131.own_ref), channel_id=1, source_target_pairs={{0,2},{2,0},{1,3},{3,1},{4,6},{6,4},{5,7},{7,5},{8,10},{10,8},{9,1... | collective-permute-start | bytes 98312 | tf_op jit(solution)/shard_map/ppermute | solution.py:91
  19.2 12.6 %collective-permute-start.3 = (bf16[64,3200]{1,0:T(8,128)(2,1)}, bf16[64,3200]{1,0:T(8,128)(2,1)S(1)}, u32[]{:S(2)}, u32[]{:S(2)}) collective-permute-start(bf16[64,3200]{1,0:T(8,128)(2,1)} %shard_map.132.refs_0_), channel_id=1, source_target_pairs={{0,4},{8,0},{16,8},{24,16},{28,24},{20,28},{12,20},{4,12},{1,5},{9... | collective-permute-start | bytes 1228808 | tf_op jit(solution)/shard_map/ppermute | solution.py:38
  20.9 12.7 %collective-permute-start.6 = (bf16[64,3200]{1,0:T(8,128)(2,1)}, bf16[64,3200]{1,0:T(8,128)(2,1)}, u32[]{:S(2)}, u32[]{:S(2)}) collective-permute-start(bf16[64,3200]{1,0:T(8,128)(2,1)} %shard_map.132.refs_0_), channel_id=1, source_target_pairs={{0,8},{8,16},{16,24},{24,28},{28,20},{20,12},{12,4},{4,0},{1,9},{9... | collective-permute-start | bytes 1228808 | tf_op jit(solution)/shard_map/ppermute | solution.py:38
  21.2 19.0 %collective-permute-start.12 = (bf16[128,1536]{1,0:T(8,128)(2,1)S(1)}, bf16[128,1536]{1,0:T(8,128)(2,1)S(1)}, u32[]{:S(2)}, u32[]{:S(2)}) collective-permute-start(bf16[128,1536]{1,0:T(8,128)(2,1)S(1)} %bitcast.96), channel_id=1, source_target_pairs={{0,4},{8,0},{16,8},{24,16},{28,24},{20,28},{12,20},{4,12},{1,5},{9... | collective-permute-start | bytes 1179656 | tf_op jit(solution)/shard_map/ppermute | solution.py:38
  23.0 19.1 %collective-permute-start.15 = (bf16[128,1536]{1,0:T(8,128)(2,1)S(1)}, bf16[128,1536]{1,0:T(8,128)(2,1)}, u32[]{:S(2)}, u32[]{:S(2)}) collective-permute-start(bf16[128,1536]{1,0:T(8,128)(2,1)S(1)} %bitcast.97), channel_id=1, source_target_pairs={{0,8},{8,16},{16,24},{24,28},{28,20},{20,12},{12,4},{4,0},{1,9},{9... | collective-permute-start | bytes 1179656 | tf_op jit(solution)/shard_map/ppermute | solution.py:38
  31.8 17.2 %collective-permute-start.4 = (bf16[64,3200]{1,0:T(8,128)(2,1)S(1)}, bf16[64,3200]{1,0:T(8,128)(2,1)S(1)}, u32[]{:S(2)}, u32[]{:S(2)}) collective-permute-start(bf16[64,3200]{1,0:T(8,128)(2,1)S(1)} %collective-permute-done.3.refs_1_), channel_id=1, source_target_pairs={{0,4},{8,0},{16,8},{24,16},{28,24},{20,28},{12,20},{4,12},{1,5},{9... | collective-permute-start | bytes 1228808 | tf_op jit(solution)/shard_map/ppermute | solution.py:38
  33.7 17.1 %collective-permute-start.7 = (bf16[64,3200]{1,0:T(8,128)(2,1)}, bf16[64,3200]{1,0:T(8,128)(2,1)S(1)}, u32[]{:S(2)}, u32[]{:S(2)}) collective-permute-start(bf16[64,3200]{1,0:T(8,128)(2,1)} %collective-permute-done.6.refs_7_), channel_id=1, source_target_pairs={{0,8},{8,16},{16,24},{24,28},{28,20},{20,12},{12,4},{4,0},{1,9},{9... | collective-permute-start | bytes 1228808 | tf_op jit(solution)/shard_map/ppermute | solution.py:38
  40.2 17.3 %collective-permute-start.13 = (bf16[128,1536]{1,0:T(8,128)(2,1)S(1)}, bf16[128,1536]{1,0:T(8,128)(2,1)}, u32[]{:S(2)}, u32[]{:S(2)}) collective-permute-start(bf16[128,1536]{1,0:T(8,128)(2,1)S(1)} %collective-permute-done.12.refs_1_), channel_id=1, source_target_pairs={{0,4},{8,0},{16,8},{24,16},{28,24},{20,28},{12,20},{4,12},{1,5},{9... | collective-permute-start | bytes 1179656 | tf_op jit(solution)/shard_map/ppermute | solution.py:38
  42.1 17.2 %collective-permute-start.16 = (bf16[128,1536]{1,0:T(8,128)(2,1)}, bf16[128,1536]{1,0:T(8,128)(2,1)}, u32[]{:S(2)}, u32[]{:S(2)}) collective-permute-start(bf16[128,1536]{1,0:T(8,128)(2,1)} %collective-permute-done.15.refs_7_), channel_id=1, source_target_pairs={{0,8},{8,16},{16,24},{24,28},{28,20},{20,12},{12,4},{4,0},{1,9},{9... | collective-permute-start | bytes 1179656 | tf_op jit(solution)/shard_map/ppermute | solution.py:38
  49.0 17.2 %collective-permute-start.5 = (bf16[64,3200]{1,0:T(8,128)(2,1)S(1)}, bf16[64,3200]{1,0:T(8,128)(2,1)S(1)}, u32[]{:S(2)}, u32[]{:S(2)}) collective-permute-start(bf16[64,3200]{1,0:T(8,128)(2,1)S(1)} %collective-permute-done.4.refs_2_), channel_id=1, source_target_pairs={{0,4},{8,0},{16,8},{24,16},{28,24},{20,28},{12,20},{4,12},{1,5},{9... | collective-permute-start | bytes 1228808 | tf_op jit(solution)/shard_map/ppermute | solution.py:38
  50.8 18.7 %collective-permute-start.8 = (bf16[64,3200]{1,0:T(8,128)(2,1)S(1)}, bf16[64,3200]{1,0:T(8,128)(2,1)S(1)}, u32[]{:S(2)}, u32[]{:S(2)}) collective-permute-start(bf16[64,3200]{1,0:T(8,128)(2,1)S(1)} %collective-permute-done.7.refs_6_), channel_id=1, source_target_pairs={{0,8},{8,16},{16,24},{24,28},{28,20},{20,12},{12,4},{4,0},{1,9},{9... | collective-permute-start | bytes 1228808 | tf_op jit(solution)/shard_map/ppermute | solution.py:38
  57.5 17.1 %collective-permute-start.14 = (bf16[128,1536]{1,0:T(8,128)(2,1)}, bf16[128,1536]{1,0:T(8,128)(2,1)S(1)}, u32[]{:S(2)}, u32[]{:S(2)}) collective-permute-start(bf16[128,1536]{1,0:T(8,128)(2,1)} %collective-permute-done.13.refs_2_), channel_id=1, source_target_pairs={{0,4},{8,0},{16,8},{24,16},{28,24},{20,28},{12,20},{4,12},{1,5},{9... | collective-permute-start | bytes 1179656 | tf_op jit(solution)/shard_map/ppermute | solution.py:38
  59.3 17.8 %collective-permute-start.17 = (bf16[128,1536]{1,0:T(8,128)(2,1)}, bf16[128,1536]{1,0:T(8,128)(2,1)}, u32[]{:S(2)}, u32[]{:S(2)}) collective-permute-start(bf16[128,1536]{1,0:T(8,128)(2,1)} %collective-permute-done.16.refs_6_), channel_id=1, source_target_pairs={{0,8},{8,16},{16,24},{24,28},{28,20},{20,12},{12,4},{4,0},{1,9},{9... | collective-permute-start | bytes 1179656 | tf_op jit(solution)/shard_map/ppermute | solution.py:38
  67.7 11.4 %collective-permute-start.10 = (bf16[32,3200]{1,0:T(8,128)(2,1)}, bf16[32,3200]{1,0:T(8,128)(2,1)}, u32[]{:S(2)}, u32[]{:S(2)}) collective-permute-start(bf16[32,3200]{1,0:T(8,128)(2,1)} %split.25), channel_id=1, source_target_pairs={{0,4},{8,0},{16,8},{24,16},{28,24},{20,28},{12,20},{4,12},{1,5},{9... | collective-permute-start | bytes 614408 | tf_op jit(solution)/shard_map/ppermute | solution.py:38
  70.9 8.7 %collective-permute-start.9 = (bf16[32,3200]{1,0:T(8,128)(2,1)}, bf16[32,3200]{1,0:T(8,128)(2,1)}, u32[]{:S(2)}, u32[]{:S(2)}) collective-permute-start(bf16[32,3200]{1,0:T(8,128)(2,1)} %split.24), channel_id=1, source_target_pairs={{0,8},{8,16},{16,24},{24,28},{28,20},{20,12},{12,4},{4,0},{1,9},{9... | collective-permute-start | bytes 614408 | tf_op jit(solution)/shard_map/ppermute | solution.py:38
  75.3 14.8 %collective-permute-start.19 = (bf16[128,768]{1,0:T(8,128)(2,1)}, bf16[128,768]{1,0:T(8,128)(2,1)}, u32[]{:S(2)}, u32[]{:S(2)}) collective-permute-start(bf16[128,768]{1,0:T(8,128)(2,1)} %split.27), channel_id=1, source_target_pairs={{0,4},{8,0},{16,8},{24,16},{28,24},{20,28},{12,20},{4,12},{1,5},{9... | collective-permute-start | bytes 589832 | tf_op jit(solution)/shard_map/ppermute | solution.py:38
  78.7 11.4 %collective-permute-start.18 = (bf16[128,768]{1,0:T(8,128)(2,1)}, bf16[128,768]{1,0:T(8,128)(2,1)}, u32[]{:S(2)}, u32[]{:S(2)}) collective-permute-start(bf16[128,768]{1,0:T(8,128)(2,1)} %split.26), channel_id=1, source_target_pairs={{0,8},{8,16},{16,24},{24,28},{28,20},{20,12},{12,4},{4,0},{1,9},{9... | collective-permute-start | bytes 589832 | tf_op jit(solution)/shard_map/ppermute | solution.py:38
  89.4 39.8 %collective-permute-start.11 = (bf16[512,3072]{1,0:T(8,128)(2,1)}, bf16[512,3072]{1,0:T(8,128)(2,1)}, u32[]{:S(2)}, u32[]{:S(2)}) collective-permute-start(bf16[512,3072]{1,0:T(8,128)(2,1)} %get-tuple-element.40), channel_id=1, source_target_pairs={{0,1},{1,0},{2,3},{3,2},{4,5},{5,4},{6,7},{7,6},{8,9},{9,8},{10,11... | collective-permute-start | bytes 9437192 | tf_op jit(solution)/shard_map/ppermute | solution.py:91
  97.3 70.9 %collective-permute-start.20 = (bf16[1024,1536]{1,0:T(8,128)(2,1)}, bf16[1024,1536]{1,0:T(8,128)(2,1)}, u32[]{:S(2)}, u32[]{:S(2)}) collective-permute-start(bf16[1024,1536]{1,0:T(8,128)(2,1)} %shard_map.135.refs_1_.refs_2_), channel_id=1, source_target_pairs={{0,2},{2,0},{1,3},{3,1},{4,6},{6,4},{5,7},{7,5},{8,10},{10,8},{9,1... | collective-permute-start | bytes 9437192 | tf_op jit(solution)/shard_map/ppermute | solution.py:91
  101.1 87.7 %all-to-all-start = ((bf16[8,2,192,384]{3,2,1,0:T(8,128)(2,1)}), bf16[8,2,192,384]{3,2,1,0:T(8,128)(2,1)S(1)}, u32[]{:S(2)}, u32[]{:S(2)}) async-start(bf16[8,2,192,384]{3,2,1,0:T(8,128)(2,1)} %pad_maximum_fusion.1), calls=%async_computation | async-start | bytes 4718592 | tf_op jit(solution)/shard_map/all_to_all | solution.py:623
  188.8 9.5 %collective-permute-start.21 = (bf16[8,2,192,384]{3,2,1,0:T(8,128)(2,1)S(1)}, bf16[8,2,192,384]{3,2,1,0:T(8,128)(2,1)S(1)}, u32[]{:S(2)}, u32[]{:S(2)}) collective-permute-start(bf16[8,2,192,384]{3,2,1,0:T(8,128)(2,1)S(1)} %all-to-all-done.own_ref), channel_id=1, source_target_pairs={{0,1},{1,0},{2,3},{3,2},{4,5},{5,4},{6,7},{7,6},{8,9},{9,8},{10,11... | collective-permute-start | bytes 7077896 | tf_op jit(solution)/shard_map/ppermute | solution.py:91
  188.8 115.4 %collective-permute-start.57 = (f32[1,128]{1,0:T(1,128)S(1)}, f32[1,128]{1,0:T(1,128)S(1)}, u32[]{:S(2)}, u32[]{:S(2)}) collective-permute-start(f32[1,128]{1,0:T(1,128)S(1)} %slice.333), channel_id=1, source_target_pairs={{0,4},{8,0},{16,8},{24,16},{28,24},{20,28},{12,20},{4,12},{1,5},{9... | collective-permute-start | bytes 1544 | tf_op jit(solution)/shard_map/ppermute | solution.py:38
  194.6 83.6 %collective-permute-start.31 = (bf16[64,3072]{1,0:T(8,128)(2,1)}, bf16[64,3072]{1,0:T(8,128)(2,1)}, u32[]{:S(2)}, u32[]{:S(2)}) collective-permute-start(bf16[64,3072]{1,0:T(8,128)(2,1)} %pad_maximum_fusion.10), channel_id=1, source_target_pairs={{0,1},{1,0},{2,3},{3,2},{4,5},{5,4},{6,7},{7,6},{8,9},{9,8},{10,11... | collective-permute-start | bytes 1179656 | tf_op jit(solution)/shard_map/ppermute | solution.py:91
  215.2 8.0 %collective-permute-start.26 = (bf16[64,1536]{1,0:T(8,128)(2,1)S(1)}, bf16[64,1536]{1,0:T(8,128)(2,1)S(1)}, u32[]{:S(2)}, u32[]{:S(2)}) collective-permute-start(bf16[64,1536]{1,0:T(8,128)(2,1)S(1)} %get-tuple-element.92), channel_id=1, source_target_pairs={{0,4},{8,0},{16,8},{24,16},{28,24},{20,28},{12,20},{4,12},{1,5},{9... | collective-permute-start | bytes 589832 | tf_op jit(solution)/shard_map/ppermute | solution.py:38
  216.8 9.2 %collective-permute-start.22 = (bf16[64,1536]{1,0:T(8,128)(2,1)S(1)}, bf16[64,1536]{1,0:T(8,128)(2,1)S(1)}, u32[]{:S(2)}, u32[]{:S(2)}) collective-permute-start(bf16[64,1536]{1,0:T(8,128)(2,1)S(1)} %get-tuple-element.91), channel_id=1, source_target_pairs={{0,8},{8,16},{16,24},{24,28},{28,20},{20,12},{12,4},{4,0},{1,9},{9... | collective-permute-start | bytes 589832 | tf_op jit(solution)/shard_map/ppermute | solution.py:38
  224.4 10.9 %collective-permute-start.27 = (bf16[64,3072]{1,0:T(8,128)(2,1)S(1)}, bf16[64,3072]{1,0:T(8,128)(2,1)S(1)}, u32[]{:S(2)}, u32[]{:S(2)}) collective-permute-start(bf16[64,3072]{1,0:T(8,128)(2,1)S(1)} %pad_maximum_fusion.8), channel_id=1, source_target_pairs={{0,4},{8,0},{16,8},{24,16},{28,24},{20,28},{12,20},{4,12},{1,5},{9... | collective-permute-start | bytes 1179656 | tf_op jit(solution)/shard_map/ppermute | solution.py:38
  226.1 12.0 %collective-permute-start.23 = (bf16[64,3072]{1,0:T(8,128)(2,1)S(1)}, bf16[64,3072]{1,0:T(8,128)(2,1)S(1)}, u32[]{:S(2)}, u32[]{:S(2)}) collective-permute-start(bf16[64,3072]{1,0:T(8,128)(2,1)S(1)} %pad_maximum_fusion.7), channel_id=1, source_target_pairs={{0,8},{8,16},{16,24},{24,28},{28,20},{20,12},{12,4},{4,0},{1,9},{9... | collective-permute-start | bytes 1179656 | tf_op jit(solution)/shard_map/ppermute | solution.py:38
  236.5 18.0 %collective-permute-start.28 = (bf16[64,3072]{1,0:T(8,128)(2,1)S(1)}, bf16[64,3072]{1,0:T(8,128)(2,1)S(1)}, u32[]{:S(2)}, u32[]{:S(2)}) collective-permute-start(bf16[64,3072]{1,0:T(8,128)(2,1)S(1)} %fusion.22), channel_id=1, source_target_pairs={{0,4},{8,0},{16,8},{24,16},{28,24},{20,28},{12,20},{4,12},{1,5},{9... | collective-permute-start | bytes 1179656 | tf_op jit(solution)/shard_map/ppermute | solution.py:38
  238.2 19.9 %collective-permute-start.24 = (bf16[64,3072]{1,0:T(8,128)(2,1)S(1)}, bf16[64,3072]{1,0:T(8,128)(2,1)S(1)}, u32[]{:S(2)}, u32[]{:S(2)}) collective-permute-start(bf16[64,3072]{1,0:T(8,128)(2,1)S(1)} %fusion.24), channel_id=1, source_target_pairs={{0,8},{8,16},{16,24},{24,28},{28,20},{20,12},{12,4},{4,0},{1,9},{9... | collective-permute-start | bytes 1179656 | tf_op jit(solution)/shard_map/ppermute | solution.py:38
  256.4 14.0 %collective-permute-start.29 = (bf16[64,3072]{1,0:T(8,128)(2,1)S(1)}, bf16[64,3072]{1,0:T(8,128)(2,1)S(1)}, u32[]{:S(2)}, u32[]{:S(2)}) collective-permute-start(bf16[64,3072]{1,0:T(8,128)(2,1)S(1)} %fusion.23), channel_id=1, source_target_pairs={{0,4},{8,0},{16,8},{24,16},{28,24},{20,28},{12,20},{4,12},{1,5},{9... | collective-permute-start | bytes 1179656 | tf_op jit(solution)/shard_map/ppermute | solution.py:38
  259.3 11.1 %collective-permute-start.25 = (bf16[64,3072]{1,0:T(8,128)(2,1)S(1)}, bf16[64,3072]{1,0:T(8,128)(2,1)S(1)}, u32[]{:S(2)}, u32[]{:S(2)}) collective-permute-start(bf16[64,3072]{1,0:T(8,128)(2,1)S(1)} %fusion.25), channel_id=1, source_target_pairs={{0,8},{8,16},{16,24},{24,28},{28,20},{20,12},{12,4},{4,0},{1,9},{9... | collective-permute-start | bytes 1179656 | tf_op jit(solution)/shard_map/ppermute | solution.py:38
  271.9 8.9 %collective-permute-start.30 = (bf16[64,3072]{1,0:T(8,128)(2,1)S(1)}, bf16[64,3072]{1,0:T(8,128)(2,1)S(1)}, u32[]{:S(2)}, u32[]{:S(2)}) collective-permute-start(bf16[64,3072]{1,0:T(8,128)(2,1)S(1)} %fusion.27.own_ref), channel_id=1, source_target_pairs={{0,2},{2,0},{1,3},{3,1},{4,6},{6,4},{5,7},{7,5},{8,10},{10,8},{9,1... | collective-permute-start | bytes 1179656 | tf_op jit(solution)/shard_map/ppermute | solution.py:91
  278.0 7.5 %collective-permute-start.33 = (bf16[512,128]{1,0:T(8,128)(2,1)S(1)}, bf16[512,128]{1,0:T(8,128)(2,1)S(1)}, u32[]{:S(2)}, u32[]{:S(2)}) collective-permute-start(bf16[512,128]{1,0:T(8,128)(2,1)S(1)} %copy-done.41), channel_id=1, source_target_pairs={{0,1},{1,0},{2,3},{3,2},{4,5},{5,4},{6,7},{7,6},{8,9},{9,8},{10,11... | collective-permute-start | bytes 393224 | tf_op jit(solution)/shard_map/ppermute | solution.py:91
  283.5 14.6 %collective-permute-start.32 = (bf16[64,3200]{1,0:T(8,128)(2,1)S(1)}, bf16[64,3200]{1,0:T(8,128)(2,1)S(1)}, u32[]{:S(2)}, u32[]{:S(2)}) collective-permute-start(bf16[64,3200]{1,0:T(8,128)(2,1)S(1)} %get-tuple-element.62.refs_0_), channel_id=1, source_target_pairs={{0,4},{8,0},{16,8},{24,16},{28,24},{20,28},{12,20},{4,12},{1,5},{9... | collective-permute-start | bytes 1228808 | tf_op jit(solution)/shard_map/ppermute | solution.py:38
  285.0 14.7 %collective-permute-start.36 = (bf16[64,3200]{1,0:T(8,128)(2,1)S(1)}, bf16[64,3200]{1,0:T(8,128)(2,1)S(1)}, u32[]{:S(2)}, u32[]{:S(2)}) collective-permute-start(bf16[64,3200]{1,0:T(8,128)(2,1)S(1)} %get-tuple-element.62.refs_0_), channel_id=1, source_target_pairs={{0,8},{8,16},{16,24},{24,28},{28,20},{20,12},{12,4},{4,0},{1,9},{9... | collective-permute-start | bytes 1228808 | tf_op jit(solution)/shard_map/ppermute | solution.py:38
  298.1 9.7 %collective-permute-start.34 = (bf16[64,3200]{1,0:T(8,128)(2,1)S(1)}, bf16[64,3200]{1,0:T(8,128)(2,1)S(1)}, u32[]{:S(2)}, u32[]{:S(2)}) collective-permute-start(bf16[64,3200]{1,0:T(8,128)(2,1)S(1)} %collective-permute-done.32.refs_1_), channel_id=1, source_target_pairs={{0,4},{8,0},{16,8},{24,16},{28,24},{20,28},{12,20},{4,12},{1,5},{9... | collective-permute-start | bytes 1228808 | tf_op jit(solution)/shard_map/ppermute | solution.py:38
  299.7 9.6 %collective-permute-start.37 = (bf16[64,3200]{1,0:T(8,128)(2,1)S(1)}, bf16[64,3200]{1,0:T(8,128)(2,1)S(1)}, u32[]{:S(2)}, u32[]{:S(2)}) collective-permute-start(bf16[64,3200]{1,0:T(8,128)(2,1)S(1)} %collective-permute-done.36.refs_7_), channel_id=1, source_target_pairs={{0,8},{8,16},{16,24},{24,28},{28,20},{20,12},{12,4},{4,0},{1,9},{9... | collective-permute-start | bytes 1228808 | tf_op jit(solution)/shard_map/ppermute | solution.py:38
  307.8 9.8 %collective-permute-start.35 = (bf16[64,3200]{1,0:T(8,128)(2,1)S(1)}, bf16[64,3200]{1,0:T(8,128)(2,1)S(1)}, u32[]{:S(2)}, u32[]{:S(2)}) collective-permute-start(bf16[64,3200]{1,0:T(8,128)(2,1)S(1)} %collective-permute-done.34.refs_2_), channel_id=1, source_target_pairs={{0,4},{8,0},{16,8},{24,16},{28,24},{20,28},{12,20},{4,12},{1,5},{9... | collective-permute-start | bytes 1228808 | tf_op jit(solution)/shard_map/ppermute | solution.py:38
  309.3 10.0 %collective-permute-start.38 = (bf16[64,3200]{1,0:T(8,128)(2,1)S(1)}, bf16[64,3200]{1,0:T(8,128)(2,1)S(1)}, u32[]{:S(2)}, u32[]{:S(2)}) collective-permute-start(bf16[64,3200]{1,0:T(8,128)(2,1)S(1)} %collective-permute-done.37.refs_6_), channel_id=1, source_target_pairs={{0,8},{8,16},{16,24},{24,28},{28,20},{20,12},{12,4},{4,0},{1,9},{9... | collective-permute-start | bytes 1228808 | tf_op jit(solution)/shard_map/ppermute | solution.py:38
  317.5 6.0 %collective-permute-start.40 = (bf16[32,3200]{1,0:T(8,128)(2,1)S(1)}, bf16[32,3200]{1,0:T(8,128)(2,1)S(1)}, u32[]{:S(2)}, u32[]{:S(2)}) collective-permute-start(bf16[32,3200]{1,0:T(8,128)(2,1)S(1)} %split.23), channel_id=1, source_target_pairs={{0,4},{8,0},{16,8},{24,16},{28,24},{20,28},{12,20},{4,12},{1,5},{9... | collective-permute-start | bytes 614408 | tf_op jit(solution)/shard_map/ppermute | solution.py:38
  319.4 5.8 %collective-permute-start.39 = (bf16[32,3200]{1,0:T(8,128)(2,1)S(1)}, bf16[32,3200]{1,0:T(8,128)(2,1)S(1)}, u32[]{:S(2)}, u32[]{:S(2)}) collective-permute-start(bf16[32,3200]{1,0:T(8,128)(2,1)S(1)} %split.22), channel_id=1, source_target_pairs={{0,8},{8,16},{16,24},{24,28},{28,20},{20,12},{12,4},{4,0},{1,9},{9... | collective-permute-start | bytes 614408 | tf_op jit(solution)/shard_map/ppermute | solution.py:38
  325.8 16.9 %collective-permute-start.41 = (bf16[512,3072]{1,0:T(8,128)(2,1)S(1)}, bf16[512,3072]{1,0:T(8,128)(2,1)S(1)}, u32[]{:S(2)}, u32[]{:S(2)}) collective-permute-start(bf16[512,3072]{1,0:T(8,128)(2,1)S(1)} %get-tuple-element.70), channel_id=1, source_target_pairs={{0,1},{1,0},{2,3},{3,2},{4,5},{5,4},{6,7},{7,6},{8,9},{9,8},{10,11... | collective-permute-start | bytes 9437192 | tf_op jit(solution)/shard_map/ppermute | solution.py:91
  329.7 7.4 %collective-permute-start.47 = (bf16[64,1536]{1,0:T(8,128)(2,1)S(1)}, bf16[64,1536]{1,0:T(8,128)(2,1)S(1)}, u32[]{:S(2)}, u32[]{:S(2)}) collective-permute-start(bf16[64,1536]{1,0:T(8,128)(2,1)S(1)} %get-tuple-element.89), channel_id=1, source_target_pairs={{0,4},{8,0},{16,8},{24,16},{28,24},{20,28},{12,20},{4,12},{1,5},{9... | collective-permute-start | bytes 589832 | tf_op jit(solution)/shard_map/ppermute | solution.py:38
  335.6 7.1 %collective-permute-start.42 = (bf16[64,1536]{1,0:T(8,128)(2,1)S(1)}, bf16[64,1536]{1,0:T(8,128)(2,1)S(1)}, u32[]{:S(2)}, u32[]{:S(2)}) collective-permute-start(bf16[64,1536]{1,0:T(8,128)(2,1)S(1)} %get-tuple-element.88), channel_id=1, source_target_pairs={{0,8},{8,16},{16,24},{24,28},{28,20},{20,12},{12,4},{4,0},{1,9},{9... | collective-permute-start | bytes 589832 | tf_op jit(solution)/shard_map/ppermute | solution.py:38
  336.1 19.0 %collective-permute-start.44 = (bf16[512,128]{1,0:T(8,128)(2,1)S(1)}, bf16[512,128]{1,0:T(8,128)(2,1)S(1)}, u32[]{:S(2)}, u32[]{:S(2)}) collective-permute-start(bf16[512,128]{1,0:T(8,128)(2,1)S(1)} %get-tuple-element.72.tail_ref.own_tail_ref), channel_id=1, source_target_pairs={{0,1},{1,0},{2,3},{3,2},{4,5},{5,4},{6,7},{7,6},{8,9},{9,8},{10,11... | collective-permute-start | bytes 393224 | tf_op jit(solution)/shard_map/ppermute | solution.py:91
  337.1 30.6 %collective-permute-start.48 = (bf16[64,3072]{1,0:T(8,128)(2,1)S(1)}, bf16[64,3072]{1,0:T(8,128)(2,1)S(1)}, u32[]{:S(2)}, u32[]{:S(2)}) collective-permute-start(bf16[64,3072]{1,0:T(8,128)(2,1)S(1)} %pad_maximum_fusion.12), channel_id=1, source_target_pairs={{0,4},{8,0},{16,8},{24,16},{28,24},{20,28},{12,20},{4,12},{1,5},{9... | collective-permute-start | bytes 1179656 | tf_op jit(solution)/shard_map/ppermute | solution.py:38
  354.6 16.3 %collective-permute-start.43 = (bf16[64,3072]{1,0:T(8,128)(2,1)}, bf16[64,3072]{1,0:T(8,128)(2,1)}, u32[]{:S(2)}, u32[]{:S(2)}) collective-permute-start(bf16[64,3072]{1,0:T(8,128)(2,1)} %pad_maximum_fusion.11), channel_id=1, source_target_pairs={{0,8},{8,16},{16,24},{24,28},{28,20},{20,12},{12,4},{4,0},{1,9},{9... | collective-permute-start | bytes 1179656 | tf_op jit(solution)/shard_map/ppermute | solution.py:38
  369.1 10.2 %collective-permute-start.49 = (bf16[64,3072]{1,0:T(8,128)(2,1)S(1)}, bf16[64,3072]{1,0:T(8,128)(2,1)S(1)}, u32[]{:S(2)}, u32[]{:S(2)}) collective-permute-start(bf16[64,3072]{1,0:T(8,128)(2,1)S(1)} %fusion.16), channel_id=1, source_target_pairs={{0,4},{8,0},{16,8},{24,16},{28,24},{20,28},{12,20},{4,12},{1,5},{9... | collective-permute-start | bytes 1179656 | tf_op jit(solution)/shard_map/ppermute | solution.py:38
  372.5 10.4 %collective-permute-start.45 = (bf16[64,3072]{1,0:T(8,128)(2,1)S(1)}, bf16[64,3072]{1,0:T(8,128)(2,1)S(1)}, u32[]{:S(2)}, u32[]{:S(2)}) collective-permute-start(bf16[64,3072]{1,0:T(8,128)(2,1)S(1)} %fusion.18), channel_id=1, source_target_pairs={{0,8},{8,16},{16,24},{24,28},{28,20},{20,12},{12,4},{4,0},{1,9},{9... | collective-permute-start | bytes 1179656 | tf_op jit(solution)/shard_map/ppermute | solution.py:38
  381.3 13.7 %collective-permute-start.50 = (bf16[64,3072]{1,0:T(8,128)(2,1)}, bf16[64,3072]{1,0:T(8,128)(2,1)}, u32[]{:S(2)}, u32[]{:S(2)}) collective-permute-start(bf16[64,3072]{1,0:T(8,128)(2,1)} %fusion.17), channel_id=1, source_target_pairs={{0,4},{8,0},{16,8},{24,16},{28,24},{20,28},{12,20},{4,12},{1,5},{9... | collective-permute-start | bytes 1179656 | tf_op jit(solution)/shard_map/ppermute | solution.py:38
  384.8 13.8 %collective-permute-start.46 = (bf16[64,3072]{1,0:T(8,128)(2,1)}, bf16[64,3072]{1,0:T(8,128)(2,1)}, u32[]{:S(2)}, u32[]{:S(2)}) collective-permute-start(bf16[64,3072]{1,0:T(8,128)(2,1)} %fusion.19), channel_id=1, source_target_pairs={{0,8},{8,16},{16,24},{24,28},{28,20},{20,12},{12,4},{4,0},{1,9},{9... | collective-permute-start | bytes 1179656 | tf_op jit(solution)/shard_map/ppermute | solution.py:38
  389.7 4.7 %collective-permute-start.53 = (f32[1,128]{1,0:T(1,128)S(1)}, f32[1,128]{1,0:T(1,128)S(1)}, u32[]{:S(2)}, u32[]{:S(2)}) collective-permute-start(f32[1,128]{1,0:T(1,128)S(1)} %slice.328), channel_id=1, source_target_pairs={{0,8},{8,16},{16,24},{24,28},{28,20},{20,12},{12,4},{4,0},{1,9},{9... | collective-permute-start | bytes 1544 | tf_op jit(solution)/shard_map/ppermute | solution.py:38
  390.3 4.8 %collective-permute-start.58 = (f32[1,256]{1,0:T(1,128)S(1)}, f32[1,256]{1,0:T(1,128)S(1)}, u32[]{:S(2)}, u32[]{:S(2)}) collective-permute-start(f32[1,256]{1,0:T(1,128)S(1)} %pad_maximum_fusion.13), channel_id=1, source_target_pairs={{0,4},{8,0},{16,8},{24,16},{28,24},{20,28},{12,20},{4,12},{1,5},{9... | collective-permute-start | bytes 3080 | tf_op jit(solution)/shard_map/ppermute | solution.py:38
  394.4 3.6 collective-permute-start.54
  400.1 13.4 %collective-permute-start.51 = (bf16[64,3072]{1,0:T(8,128)(2,1)S(1)}, bf16[64,3072]{1,0:T(8,128)(2,1)}, u32[]{:S(2)}, u32[]{:S(2)}) collective-permute-start(bf16[64,3072]{1,0:T(8,128)(2,1)S(1)} %fusion.21), channel_id=1, source_target_pairs={{0,2},{2,0},{1,3},{3,1},{4,6},{6,4},{5,7},{7,5},{8,10},{10,8},{9,1... | collective-permute-start | bytes 1179656 | tf_op jit(solution)/shard_map/ppermute | solution.py:91
  403.4 3.6 collective-permute-start.55
  403.9 3.6 collective-permute-start.59
  408.0 3.8 collective-permute-start.60
  409.6 3.9 collective-permute-start.56
  414.5 6.1 %collective-permute-start.52 = (f32[64,1536]{1,0:T(8,128)S(1)}, f32[64,1536]{1,0:T(8,128)S(1)}, u32[]{:S(2)}, u32[]{:S(2)}) collective-permute-start(f32[64,1536]{1,0:T(8,128)S(1)} %dynamic-slice_add_fusion), channel_id=1, source_target_pairs={{0,1},{1,0},{2,3},{3,2},{4,5},{5,4},{6,7},{7,6},{8,9},{9,8},{10,11... | collective-permute-start | bytes 1179656 | tf_op jit(solution)/shard_map/ppermute | solution.py:91
  415.2 1.3 collective-permute-start.61
  416.5 3.5 collective-permute-start.62
  (84 other events, 770.0 us)

commit v3 on v2

--- a/solution.py
+++ b/solution.py
@@ -55,14 +55,13 @@
     second = ring_shift(jnp.split(fore, 2, axis=split_axis)[1], cycle, -1)
     done = jobs.pop(0)(back) if jobs else []
     slots[reach] = after(jnp.concatenate([first, second], axis=split_axis), *done)
-    while jobs:
-        jobs.pop(0)(slots[reach])
-    return slots
+    return slots[-1:] + slots[:-1]
 
 
 def ring_reduce(parts, cycle, wire, jobs=()):
     size = len(cycle)
     reach = size // 2
+    parts = parts[1:] + parts[:1]
     width = parts[0].shape[1] // 2
     jobs = list(jobs)
     far = parts[reach].astype(wire)
@@ -82,8 +81,6 @@
         new_up, new_down = ring_shift(up, cycle, 1), ring_shift(down, cycle, -1)
         done = jobs.pop(0)(up) if jobs else []
         up, down = after(new_up, *done).astype(F32), after(new_down, *done).astype(F32)
-    while jobs:
-        jobs.pop(0)(up)
     return parts[0] + up + down
 
 
@@ -194,40 +191,105 @@
     )(probe, own, twin)
 
 
-def sign_products(parts, starts, scale, weights):
+def sign_products(parts, starts, scales, weight, columns):
     tokens = parts[0].shape[0]
-    width = weights[0].shape[0]
-    widths = [weight.shape[1] for weight in weights]
-    count = len(weights)
-    block = 256 if tokens % 256 == 0 else tokens
-
-    def kernel(starts_ref, scale_ref, *refs):
-        outs = refs[count + len(parts):]
-        totals = [None] * count
-        for index, part_ref in enumerate(refs[count:count + len(parts)]):
-            span = pl.ds(pl.multiple_of(starts_ref[index], 128), part_ref.shape[1])
-            scaled = part_ref[...] * scale_ref[:, span]
-            for at in range(count):
-                product = dot(scaled, refs[at][span, :])
-                totals[at] = product if index == 0 else totals[at] + product
-        for total, out_ref in zip(totals, outs):
-            out_ref[...] = total.astype(BF16)
-
+    width, total_columns = weight.shape
+    blocks, steps, _ = scales.shape
+    if columns % 128:
+        made = []
+        for step in range(steps):
+            scaled = [(parts, scales[at, step][None], weight[:, at * columns:(at + 1) * columns]) for at in range(blocks)]
+            made.append(jnp.concatenate([dot(signs[0] * scale, own) for signs, scale, own in scaled], axis=1))
+        return jnp.stack(made).astype(BF16)
+
+    def kernel(starts_ref, scale_ref, weight_ref, *refs):
+        out_ref = refs[-1]
+        spans = [
+            pl.ds(pl.multiple_of(starts_ref[index], 128), part.shape[1]) for index, part in enumerate(parts)
+        ]
+        for step in range(steps):
+            total = None
+            for span, part_ref in zip(spans, refs):
+                product = dot(part_ref[...] * scale_ref[0, step:step + 1, span], weight_ref[span, :])
+                total = product if total is None else total + product
+            out_ref[step] = total.astype(BF16)
+
+    flops = 2 * steps * tokens * width * total_columns
     return pl.pallas_call(
         kernel,
-        grid=(tokens // block,),
-        out_shape=[jax.ShapeDtypeStruct((tokens, columns), BF16) for columns in widths],
-        in_specs=[pl.BlockSpec(memory_space=pltpu.SMEM), pl.BlockSpec((1, width), lambda i: (0, 0))]
-        + [pl.BlockSpec(weight.shape, lambda i: (0, 0)) for weight in weights]
-        + [pl.BlockSpec((block, part.shape[1]), lambda i: (i, 0)) for part in parts],
-        out_specs=[pl.BlockSpec((block, columns), lambda i: (i, 0)) for columns in widths],
-        compiler_params=pltpu.CompilerParams(vmem_limit_bytes=48 * 1024 * 1024),
+        grid=(blocks,),
+        out_shape=jax.ShapeDtypeStruct((steps, tokens, total_columns), BF16),
+        in_specs=[
+            pl.BlockSpec(memory_space=pltpu.SMEM),
+            pl.BlockSpec((1, steps, width), lambda i: (i, 0, 0)),
+            pl.BlockSpec((width, columns), lambda i: (0, i)),
+        ]
+        + [pl.BlockSpec(part.shape, lambda i: (0, 0)) for part in parts],
+        out_specs=pl.BlockSpec((steps, tokens, columns), lambda i: (0, 0, i)),
+        compiler_params=pltpu.CompilerParams(vmem_limit_bytes=32 * 1024 * 1024),
         cost_estimate=pl.CostEstimate(
-            flops=2 * tokens * width * sum(widths),
-            bytes_accessed=2 * (tokens * width + width * sum(widths) + tokens * sum(widths)),
+            flops=flops + flops // 2,
+            bytes_accessed=2 * (tokens * width + width * total_columns + steps * tokens * total_columns),
             transcendentals=0,
         ),
-    )(starts, scale, *weights, *parts)
+    )(starts, scales, weight, *parts)
+
+
+def project(rows, weight, columns):
+    tokens, width = rows.shape
+    total_columns = weight.shape[1]
+
+    def kernel(rows_ref, weight_ref, out_ref):
+        out_ref[...] = dot(rows_ref[...], weight_ref[...])
+
+    return pl.pallas_call(
+        kernel,
+        grid=(total_columns // columns,),
+        out_shape=jax.ShapeDtypeStruct((tokens, total_columns), F32),
+        in_specs=[
+            pl.BlockSpec((tokens, width), lambda i: (0, 0)),
+            pl.BlockSpec((width, columns), lambda i: (0, i)),
+        ],
+        out_specs=pl.BlockSpec((tokens, columns), lambda i: (0, i)),
+        compiler_params=pltpu.CompilerParams(vmem_limit_bytes=24 * 1024 * 1024),
+        cost_estimate=pl.CostEstimate(
+            flops=3 * tokens * width * total_columns,
+            bytes_accessed=2 * (tokens * width + width * total_columns) + 4 * tokens * total_columns,
+            transcendentals=0,
+        ),
+    )(rows, weight)
+
+
+def gelu_tanh(pre):
+    inner = math.sqrt(2.0 / math.pi) * (pre + 0.044715 * (pre * pre * pre))
+    return 0.5 * pre * (1.0 + jnp.tanh(inner))
+
+
+def hidden_units(normed, up, down, first_far):
+    tokens, width = normed.shape
+    units = up.shape[1]
+
+    def kernel(normed_ref, up_ref, down_ref, pre_ref, hidden_ref, far_ref):
+        pre = dot(normed_ref[...], up_ref[...])
+        pre_ref[...] = pre
+        hidden = gelu_tanh(pre).astype(BF16)
+        hidden_ref[...] = hidden[:first_far]
+        far_ref[...] = dot(hidden[first_far:], down_ref[...]).astype(BF16)
+
+    return pl.pallas_call(
+        kernel,
+        out_shape=[
+            jax.ShapeDtypeStruct((tokens, units), F32),
+            jax.ShapeDtypeStruct((first_far, units), BF16),
+            jax.ShapeDtypeStruct((tokens - first_far, width), BF16),
+        ],
+        compiler_params=pltpu.CompilerParams(vmem_limit_bytes=28 * 1024 * 1024),
+        cost_estimate=pl.CostEstimate(
+            flops=4 * tokens * width * units,
+            bytes_accessed=2 * (2 * tokens * width + 2 * width * units),
+            transcendentals=tokens * units,
+        ),
+    )(normed, up, down)
 
 
 def lanes_of(values, count):
@@ -308,32 +370,40 @@
     return sums[:, 0:1], sums[:, 3:4], sums[:, 4:5]
 
 
-def mlp_tangent(pre_hidden, sign, consts, tails, back):
-    tokens, units = sign.shape
-    half = tokens // 2
+def mlp_tangent(pre_hidden, signs, step, consts, tails):
+    half, units = pre_hidden[0].shape
+    tokens = 2 * half
     lanes = HD if units % HD == 0 else units
 
-    def kernel(own_ref, twin_ref, sign_ref, const_ref, own_tail_ref, twin_tail_ref, back_ref, out_ref):
-        for part, pre_ref, tail_ref in ((0, own_ref, own_tail_ref), (1, twin_ref, twin_tail_ref)):
-            rows = pl.ds(part * half, half)
+    def kernel(own_ref, twin_ref, own_sign_ref, twin_sign_ref, const_ref, own_tail_ref, twin_tail_ref, out_ref):
+        own = (0, own_ref, own_tail_ref, own_sign_ref)
+        twin = (1, twin_ref, twin_tail_ref, twin_sign_ref)
+        for part, pre_ref, tail_ref, sign_ref in (own, twin):
             inv, mean, cross = token_scalars(tail_ref[...], part == 0)
             pre = pre_ref[...]
-            tan = inv * (sign_ref[rows, :].astype(F32) - mean * const_ref[0:1] - cross * (pre - const_ref[1:2]))
+            tan = inv * (sign_ref[0, :, 0:units].astype(F32) - mean * const_ref[0:1] - cross * (pre - const_ref[1:2]))
             inner = math.sqrt(2.0 / math.pi) * (pre + 0.044715 * (pre * pre * pre))
             bend = jnp.tanh(inner)
             slope = math.sqrt(2.0 / math.pi) * (1.0 + 3.0 * 0.044715 * (pre * pre))
             gelu_slope = 0.5 * (1.0 + bend) + 0.5 * pre * (1.0 - bend * bend) * slope
-            product = gelu_slope * tan * back_ref[rows, :].astype(F32)
-            out_ref[rows, :] = sum(product[:, i:i + lanes] for i in range(0, units, lanes))
-
+            product = gelu_slope * tan * sign_ref[0, :, units:2 * units].astype(F32)
+            out_ref[pl.ds(part * half, half), :] = sum(product[:, i:i + lanes] for i in range(0, units, lanes))
+
+    def whole(array):
+        return pl.BlockSpec(array.shape, lambda i: (0, 0))
+
+    chosen = pl.BlockSpec((1, half, 2 * units), lambda i: (step, 0, 0))
     return pl.pallas_call(
         kernel,
+        grid=(1,),
         out_shape=jax.ShapeDtypeStruct((tokens, lanes), F32),
-        compiler_params=pltpu.CompilerParams(vmem_limit_bytes=48 * 1024 * 1024),
+        in_specs=[whole(pre_hidden[0])] * 2 + [chosen] * 2 + [whole(consts)] + [whole(tails[0])] * 2,
+        out_specs=pl.BlockSpec((tokens, lanes), lambda i: (0, 0)),
+        compiler_params=pltpu.CompilerParams(vmem_limit_bytes=24 * 1024 * 1024),
         cost_estimate=pl.CostEstimate(
             flops=6000 * tokens * units, bytes_accessed=10 * tokens * units, transcendentals=tokens * units
         ),
-    )(pre_hidden[0], pre_hidden[1], sign, consts, tails[0], tails[1], back)
+    )(pre_hidden[0], pre_hidden[1], signs[0], signs[1], consts, tails[0], tails[1])
 
 
 def normed_head(raw, gain):
@@ -375,7 +445,7 @@
             columns(0, 1),
         ],
         out_specs=columns(0, queries),
-        compiler_params=pltpu.CompilerParams(vmem_limit_bytes=32 * 1024 * 1024),
+        compiler_params=pltpu.CompilerParams(vmem_limit_bytes=20 * 1024 * 1024),
         cost_estimate=pl.CostEstimate(
             flops=30 * heads * queries * tokens * HD,
             bytes_accessed=12 * heads * tokens * HD + 4 * queries * tokens,
@@ -385,14 +455,14 @@
 
 
 def attention_tangent(
-    raw, sign, consts, tails, back, bias, q_gain, k_gain, heads
+    raw, signs, step, consts, tails, bias, q_gain, k_gain, heads
 ):
     queries, tokens = bias.shape
     scale = 1.0 / math.sqrt(HD)
     half = tokens // 2
 
-    def kernel(q_ref, k_ref, v_ref, q_twin_ref, k_twin_ref, v_twin_ref, qs_ref, ks_ref, vs_ref, qc_ref, kc_ref,
-               vc_ref, tail_ref, tail_twin_ref, back_ref, bias_ref, qg_ref, kg_ref, out_ref):
+    def kernel(q_ref, k_ref, v_ref, q_twin_ref, k_twin_ref, v_twin_ref, qs_ref, ks_ref, vs_ref, back_ref, qs_twin_ref,
+               ks_twin_ref, vs_twin_ref, back_twin_ref, qc_ref, kc_ref, vc_ref, tail_ref, tail_twin_ref, bias_ref, qg_ref, kg_ref, out_ref):
         head = pl.program_id(0)
         own = token_scalars(tail_ref[...], True)
         twin = token_scalars(tail_twin_ref[...], False)
@@ -409,18 +479,19 @@
             return ((tan * inv + raw_rows * tan_inv) * gain).astype(BF16)
 
         k_raw = jnp.concatenate([k_ref[...], k_twin_ref[...]], axis=0)
+        k_sign = jnp.concatenate([ks_ref[0], ks_twin_ref[0]], axis=0)
+        v_sign = jnp.concatenate([vs_ref[0], vs_twin_ref[0]], axis=0)
         k_n, k_inv = normed_head(k_raw, kg_ref[...])
-        dk_n = tangent_head(k_raw, tangent(k_raw, ks_ref[...], kc_ref, every), k_inv, kg_ref[...])
+        dk_n = tangent_head(k_raw, tangent(k_raw, k_sign, kc_ref, every), k_inv, kg_ref[...])
         keys = jnp.concatenate([k_n, dk_n], axis=1)
         v_raw = jnp.concatenate([v_ref[...], v_twin_ref[...]], axis=0)
         v_n = v_raw.astype(BF16)
-        values = jnp.concatenate([v_n, tangent(v_raw, vs_ref[...], vc_ref, every).astype(BF16)], axis=1)
+        values = jnp.concatenate([v_n, tangent(v_raw, v_sign, vc_ref, every).astype(BF16)], axis=1)
         for part in range(2):
             q_raw = (q_twin_ref if part else q_ref)[...]
-            rows = pl.ds(part * half, queries)
             q_n, q_inv = normed_head(q_raw, qg_ref[...])
             columns = [column[:queries] for column in (twin if part else own)]
-            dq_n = tangent_head(q_raw, tangent(q_raw, qs_ref[rows, :], qc_ref, columns), q_inv, qg_ref[...])
+            dq_n = tangent_head(q_raw, tangent(q_raw, (qs_twin_ref if part else qs_ref)[0], qc_ref, columns), q_inv, qg_ref[...])
             scores = dot_t(q_n, k_n) * scale + bias_ref[...]
             weights = jnp.exp(scores - jnp.max(scores, axis=1, keepdims=True))
             inv_total = 1.0 / jnp.sum(weights, axis=1, keepdims=True)
@@ -428,7 +499,7 @@
             tan_sum = jnp.sum(weighted, axis=1, keepdims=True) * inv_total
             both = dot(weights.astype(BF16), values) * inv_total
             tan_out = both[:, HD:] + dot(weighted.astype(BF16), v_n) * inv_total - tan_sum * both[:, :HD]
-            share = tan_out * back_ref[rows, :].astype(F32)
+            share = tan_out * (back_twin_ref if part else back_ref)[0].astype(F32)
             span = pl.ds(part * queries, queries)
 
             @pl.when(head == 0)
@@ -442,6 +513,9 @@
     def columns(part, height):
         return pl.BlockSpec((height, HD), lambda i: (0, part * heads + i))
 
+    def chosen(part, height):
+        return pl.BlockSpec((1, height, HD), lambda i: (step, 0, part * heads + i))
+
     def whole(array):
         return pl.BlockSpec(array.shape, lambda i: (0, 0))
 
@@ -450,19 +524,19 @@
         grid=(heads,),
         out_shape=jax.ShapeDtypeStruct((2 * queries, HD), F32),
         in_specs=[columns(0, queries), columns(1, half), columns(2, half)] * 2
-        + [columns(i, tokens) for i in range(3)]
+        + [chosen(0, queries), chosen(1, half), chosen(2, half), chosen(3, queries)] * 2
         + [columns(i, consts.shape[0]) for i in range(3)]
-        + [whole(tails[0]), whole(tails[1]), columns(0, tokens), whole(bias), columns(0, 1), columns(0, 1)],
+        + [whole(tails[0]), whole(tails[1]), whole(bias), columns(0, 1), columns(0, 1)],
         out_specs=pl.BlockSpec((2 * queries, HD), lambda i: (0, 0)),
-        compiler_params=pltpu.CompilerParams(vmem_limit_bytes=48 * 1024 * 1024),
+        compiler_params=pltpu.CompilerParams(vmem_limit_bytes=28 * 1024 * 1024),
         cost_estimate=pl.CostEstimate(
             flops=140 * heads * queries * tokens * HD,
             bytes_accessed=32 * heads * tokens * HD + 4 * queries * tokens,
             transcendentals=2 * heads * queries * tokens,
         ),
     )(
-        *[raw[0]] * 3, *[raw[1]] * 3, sign, sign, sign, consts, consts, consts, tails[0], tails[1], back, bias,
-        q_gain, k_gain,
+        *[raw[0]] * 3, *[raw[1]] * 3, *[signs[0]] * 4, *[signs[1]] * 4, consts, consts, consts, tails[0], tails[1],
+        bias, q_gain, k_gain,
     )
 
 
@@ -491,8 +565,8 @@
     cycle_arr = jnp.array(cycle, jnp.int32)
     place = jnp.array([cycle.index(i) for i in range(ctx_size)], jnp.int32)
     ring_index = place[ctx_index]
-    slot_owner = cycle_arr[(ring_index + jnp.arange(ctx_size)) % ctx_size]
-    owner_slot = (place - ring_index) % ctx_size
+    slot_owner = cycle_arr[(ring_index + jnp.arange(-1, ctx_size - 1)) % ctx_size]
+    owner_slot = (place - ring_index + 1) % ctx_size
     group = ring_index % groups
     column_offset = (tp_index * local_width).astype(jnp.int32).reshape(1)
 
@@ -502,22 +576,25 @@
     sign_slots = ring_gather(signs_local, cycle, 1)
     lat_half = lax.dynamic_slice_in_dim(latent, probe_index * half, half, 0)
     rows = join_tp(lat_half, 1)
-    places = [
-        (k, part * half, half, (part * ctx_size + k) * half, "own") for k in range(ctx_size) for part in range(2)
+    sign_own = [
+        assemble(
+            sign_slots, [(k, part * half, half, k * half, "own") for k in range(ctx_size)],
+            (ctx_size * half, local_width), 0, column_offset * 0,
+        )
+        for part in range(2)
     ]
-    signs = assemble(sign_slots, places, (tokens, local_width), 0, column_offset * 0)
     if tp_size == 2:
-        sign_parts = [signs, swap(signs, "tp")]
+        sign_parts = [[own, swap(own, "tp")] for own in sign_own]
         sign_starts = jnp.concatenate([column_offset, local_width - column_offset])
         low = tp_index == 0
         block_signs = [
             jnp.concatenate([jnp.where(low, own, other), jnp.where(low, other, own)], axis=1)
-            for own, other in ([part[at:at + half] for part in sign_parts] for at in (0, tokens // 2))
+            for own, other in ([part[half:row_count] for part in parts] for parts in sign_parts)
         ]
     else:
-        sign_parts = [lax.all_gather(signs, "tp", axis=1, tiled=True)]
+        sign_parts = [[lax.all_gather(own, "tp", axis=1, tiled=True)] for own in sign_own]
         sign_starts = column_offset * 0
-        block_signs = [sign_parts[0][at:at + half] for at in (0, tokens // 2)]
+        block_signs = [parts[0][half:row_count] for parts in sign_parts]
     own_signs, twin_signs = block_signs[0], swap(block_signs[1], "probe")
 
     qkv_own = lax.dynamic_slice_in_dim(w_qkv, group * head_width, head_width, 2)
@@ -531,27 +608,36 @@
     lists = jnp.pad(pattern.astype(BF16), ((0, 0), (10, 128 - 10 - list_size)))
 
     half_tokens = ctx_size * half
-    out_turned = out_own.T
-
-    def products(step, back):
+    mixed = after(jnp.concatenate([qkv_own, out_own.T], axis=1))
+    mixed_scales = jnp.stack([stretches] * 3 + [gates])
+    unit_scales = jnp.stack([stretches, gates])
+    constants = [row for step in range(STEPS) for row in (stretches[step], modulation[step, 0].astype(BF16))]
+    constants = jnp.pad(jnp.stack(constants), ((0, 16 - 2 * STEPS), (0, 0)))
+
+    def constant_rows(weight):
+        rows = dot(constants, weight)
+        return [jnp.pad(rows[2 * step:2 * step + 2], ((0, 6), (0, 0))) for step in range(STEPS)]
+
+    qkv_rows = constant_rows(qkv_own)
+
+    def unit_weights(token):
+        late = after(down_own, token)
+        up_down.append(after(jnp.concatenate([up_own, late.T], axis=1)))
+        return up_down
+
+    def unit_products(part):
         def job(token):
-            scale = after((gates if back else stretches)[step][None], token)
-            weights = [out_turned, down_turned] if back else [qkv_own, up_own]
-            if step == 0:
-                made = [early[back]] + list(sign_products(sign_parts, sign_starts, scale, weights[1:]))
-            else:
-                made = sign_products(sign_parts, sign_starts, scale, weights)
-            found[step, back] = made
-            return made
+            made = sign_products(sign_parts[part], sign_starts, after(unit_scales, token), up_down[0], units)
+            unit_signs.append(made)
+            return [made]
 
         return job
 
     def head_tangent(step):
         def job(token):
-            raw, tails, pre, pairs = kept[step]
+            raw, tails, pre = kept[step]
             share = attention_tangent(
-                (after(raw[0], token), raw[1]), found[step, False][0], pairs[0], tails, found[step, True][0],
-                bias, q_gain_own, k_gain_own, heads_own,
+                (after(raw[0], token), raw[1]), head_signs, step, qkv_rows[step], tails, bias, q_gain_own, k_gain_own, heads_own,
             )
             attn_shares.append(share)
             return [share]
@@ -560,11 +646,9 @@
 
     def unit_tangent(step):
         def job(token):
-            raw, tails, pre, pairs = kept[step]
-            pre_twin = dot(after(pre[1], token), up_own)
-            share = mlp_tangent(
-                (pre[0], pre_twin), found[step, False][1], pairs[1], tails, found[step, True][1]
-            )
+            raw, tails, pre = kept[step]
+            pre_twin = project(after(pre[1], token), up_own, units)
+            share = mlp_tangent((pre[0], pre_twin), unit_signs, step, up_rows[step], tails)
             mlp_shares.append(share)
             return [share]
 
@@ -573,7 +657,7 @@
     def no_job(token):
         return []
 
-    found = {}
+    unit_signs, up_down = [], []
     kept, attn_shares, mlp_shares = [], [], []
 
     bias = None
@@ -588,7 +672,9 @@
             else:
                 sums_other = lax.psum(sums, "tp") - sums
             packet = first_packet(rows, sums, sums_other, mod, lists, full_width)
-            slots = ring_gather(packet, cycle, 0)
+            packet = after(packet, sign_slots[ctx_size // 2 + 1])
+            jobs = [lambda token: sign_own, no_job, no_job, lambda token: sign_parts[0][1:]]
+            slots = ring_gather(packet, cycle, 0, jobs)
             at = slots[0].shape[1] - 128 + 10
             listed = jnp.stack([slots[k][0, at:at + list_size] for k in range(groups)]).astype(jnp.int32)
             listed = jnp.any(listed[:, :, None] == slot_owner[None, None, :], axis=1)
@@ -598,30 +684,29 @@
             rows, packet = next_packet(
                 rows, branch, branch_other, last_gate, own_signs, twin_signs, mod, lists, step_size
             )
-            jobs = [head_tangent(step - 1), no_job, unit_tangent(step - 1)]
+            jobs = [head_tangent(step - 1), unit_products(1), unit_tangent(step - 1)]
             slots = ring_gather(packet, cycle, 0, jobs)
         places = [(k, 0, half, k * half, "all") for k in range(ctx_size)]
         normed, tails = assemble(slots, places, (half_tokens, full_width), 128, column_offset)
 
         normed_twin, tails_twin = swap(normed, "probe"), swap(tails, "probe")
-        raw_own = dot(normed, qkv_own)
         if step == 0:
-            raw_twin = dot(normed_twin, qkv_own)
+            raw_own = project(normed, qkv_own, head_width)
+            raw_twin = project(normed_twin, qkv_own, head_width)
             attended = attention(raw_own, raw_twin, bias, q_gain_own, k_gain_own, heads_own)
 
-            early = [
-                sign_products(sign_parts, sign_starts, after(scales[0][None], attended), [weight])[0]
-                for scales, weight in ((stretches, qkv_own), (gates, out_turned))
+            head_signs = [
+                sign_products(part, sign_starts, after(mixed_scales, attended), mixed, head_width)
+                for part in sign_parts
             ]
-            up_late, down_late = after(w_up, slots[ctx_size // 2], signs), after(w_down, slots[ctx_size // 2], signs)
-            up_part = lax.dynamic_slice_in_dim(up_late, probe_index * (w_up.shape[0] // 2), w_up.shape[0] // 2, 0)
+            up_part = lax.dynamic_slice_in_dim(w_up, probe_index * (w_up.shape[0] // 2), w_up.shape[0] // 2, 0)
             up_part = up_part.reshape(-1, ctx_size, units).transpose(1, 0, 2)
-            down_part = down_late.reshape(ctx_size, 2, units // 2, w_down.shape[1])
+            down_part = w_down.reshape(ctx_size, 2, units // 2, w_down.shape[1])
             down_part = lax.dynamic_index_in_dim(down_part, probe_index, 1, keepdims=False)
             fused = up_part.shape == down_part.shape
             if fused:
-                got = lax.all_to_all(jnp.stack([up_part, down_part], axis=1), "ctx", 0, 0, tiled=True)
-                got = after(got, attended, *early)
+                got = lax.all_to_all(after(after(jnp.stack([up_part, down_part], axis=1)), slots[ctx_size // 2]), "ctx", 0, 0, tiled=True)
+                got = after(got, attended, *head_signs)
                 got_twin = swap(got, "probe")
                 core = probe_index.astype(jnp.int32).reshape(1)
                 up_own = place_units(got, got_twin, core, 0)
@@ -632,47 +717,54 @@
                 up_own = jnp.where(first, pair, pair[:, ::-1]).reshape(full_width, units)
                 got = lax.all_to_all(down_part, "ctx", 0, 0, tiled=True)
                 down_own = join_probe(got.transpose(1, 0, 2).reshape(units // 2, full_width), 0)
-            down_turned = down_own.T
-
-        pre_own = dot(normed, up_own)
-        hidden = jax.nn.gelu(pre_own, approximate=True).astype(BF16)
+            up_rows = constant_rows(up_own)
+
         parts = []
         if groups < ctx_size:
-            far = dot(hidden[queries:], down_own)
+            pre_own, hidden, far = hidden_units(normed, up_own, down_own, queries)
             parts = [far[k * half:(k + 1) * half] for k in range(ctx_size - groups)]
+        else:
+            pre_own = dot(normed, up_own)
+            hidden = gelu_tanh(pre_own).astype(BF16)
         if step > 0:
+            raw_own = dot(normed, qkv_own)
             raw_twin = dot(normed_twin, qkv_own)
             attended = attention(raw_own, raw_twin, bias, q_gain_own, k_gain_own, heads_own)
-        near = dot(attended, out_own) + dot(hidden[:queries], down_own)
+        near = dot(attended, out_own) + dot(hidden, down_own)
         parts = [near[k * half:(k + 1) * half] for k in range(groups)] + parts
 
-        pair = jnp.concatenate(
-            [stretches[step][None], shift.astype(BF16), jnp.zeros((14, full_width), BF16)], axis=0
-        )
-        pairs = (dot(pair, qkv_own), dot(pair, up_own))
-        kept.append(((raw_own, raw_twin), (tails, tails_twin), (pre_own, normed_twin), pairs))
+        kept.append(((raw_own, raw_twin), (tails, tails_twin), (pre_own, normed_twin)))
         if step == 0:
-            jobs = [products(0, False), products(0, True), products(1, False), products(1, True)]
+            jobs = [no_job, unit_weights, unit_products(0)]
         else:
-            jobs = [no_job, head_tangent(step), no_job, unit_tangent(step)]
+            jobs = [lambda token: [raw_own], lambda token: [attended], head_tangent(step), unit_tangent(step)]
         branch = ring_reduce(parts, cycle, BF16, jobs).astype(BF16)
+        if step == STEPS - 1:
+            break
         if tp_size == 2:
             branch_other = swap(branch, "tp")
         else:
             branch_other = sum_tp(branch) - branch.astype(F32)
         last_gate = gate
 
-    rows = rows + step_size * (last_gate * (branch.astype(F32) + branch_other.astype(F32)))
     estimate = jnp.sum(sum(mlp_shares), axis=1)
     attn_share = jnp.sum(sum(attn_shares), axis=1).reshape(2, queries)
     estimate = estimate + jnp.pad(attn_share, ((0, 0), (0, half_tokens - queries))).reshape(tokens)
-    lat_cols = lax.dynamic_slice_in_dim(rows, tp_index * local_width, local_width, 1)
+    def own_columns(array, index):
+        return lax.dynamic_slice_in_dim(array, index * local_width, local_width, 1)
+
+    if tp_size == 2:
+        whole = own_columns(branch, tp_index).astype(F32)
+        whole = whole + swap(own_columns(branch, 1 - tp_index), "tp").astype(F32)
+    else:
+        whole = own_columns(sum_tp(branch), tp_index)
+    lat_cols = own_columns(rows, tp_index) + step_size * (own_columns(gate, tp_index) * whole)
     latent_out = join_probe(lat_cols, 0)
 
     by_slot = estimate.reshape(2, ctx_size, half)
     by_slot = jnp.where(first, by_slot, by_slot[::-1]).transpose(1, 0, 2).reshape(ctx_size, row_count)
-    by_slot = jnp.concatenate([by_slot, jnp.zeros_like(by_slot)], axis=1)
-    own_estimate = ring_reduce([by_slot[k:k + 1] for k in range(ctx_size)], cycle, F32)[:, :row_count]
+    by_owner = by_slot[owner_slot][:, None]
+    own_estimate = jnp.sum(lax.all_to_all(by_owner, "ctx", 0, 0, tiled=True), axis=0)
     own_estimate = own_estimate + swap(own_estimate, "probe")
     own_estimate = sum_tp(own_estimate)[0]
     density_change = -step_size * own_estimate / (2 * math.sqrt(full_width))

time: 429 us -> 393 us (0.916)
  waiting for transfers between devices: 99.6 us -> 57.6 us
  matrix products: 58.1 us -> 21.6 us
  Pallas kernels: 108 us -> 136 us
  local copies, waits for them, and re-layouts: 47.1 us -> 64.7 us
  starting transfers between devices: 66.9 us -> 61.3 us
    dot_general x18 -> x8, matrix products: 58.1 us -> 21.6 us  [dot(): return jnp.dot(a, b, preferred_element_type=F32)]
    ppermute x15 -> x16, waiting for transfers between devices: 38.5 us -> 8.79 us  [swap(): return lax.ppermute(x, axis, [(0, 1), (1, 0)])]
    pallas_call x8 -> x12, Pallas kernels: 58.8 us -> 85.8 us  [the longest x4 51.7 us: sign_products(): pl.pallas_call(kernel, grid=(blocks,), out_shape=jax.ShapeDtypeStruct((st...]
    ppermute x48 -> x40, waiting for transfers between devices: 61.1 us -> 43.1 us  [ring_shift(): return lax.ppermute(x, 'ctx', pairs)]
    unnamed x173 -> x205, local copies, waits for them, and re-layouts: 24.5 us -> 36.2 us
    concatenate x0 -> x2, other arithmetic: none -> 11 us  [the longest x1 8.07 us: local(): mixed = after(jnp.concatenate([qkv_own, out_own.T], axis=1))]
    ppermute x48 -> x40, starting transfers between devices: 51 us -> 42.5 us  [ring_shift(): return lax.ppermute(x, 'ctx', pairs)]
    all_to_all x1 -> x2, waiting for transfers between devices: 0.01 us -> 5.68 us  [the longest x1 5.68 us: local(): lax.all_to_all(by_owner, 'ctx', 0, 0, tiled=True)]
  transfers between devices with their start and end apart: 64 -> 58, of which waited for: 29 -> 20; matrix products, arithmetic and copies ran while one was open for 29% -> 23% of each run, Pallas kernels for 25% -> 32%
where the time goes in v3:
time: 393 us; the launch traced here: 386 us
  Pallas kernels  136 us (35%)
  local copies, waits for them, and re-layouts  64.7 us (16%)
  starting transfers between devices  61.3 us (16%)
  waiting for transfers between devices  57.6 us (15%)
  other arithmetic  40.8 us (10%)
  matrix products  21.6 us (5%)
  between operations  4.36 us (1%)
    pallas_call x4, Pallas kernels, sign_products(): pl.pallas_call(kernel, grid=(blocks,), out_shape=jax.ShapeDtypeStruct((st...  51.7 us
    ppermute x40, waiting for transfers between devices, ring_shift(): return lax.ppermute(x, 'ctx', pairs)  43.1 us
    ppermute x40, starting transfers between devices, ring_shift(): return lax.ppermute(x, 'ctx', pairs)  42.5 us
    unnamed x205, local copies, waits for them, and re-layouts  36.2 us
    pallas_call x2, Pallas kernels, attention_tangent(): pl.pallas_call(kernel, grid=(heads,), out_shape=jax.ShapeDtypeStruct((2 *...  24.3 us
    pallas_call x4, Pallas kernels, project(): pl.pallas_call(kernel, grid=(total_columns // columns,), out_shape=jax.Sh...  22.3 us
    dot_general x8, matrix products, dot(): return jnp.dot(a, b, preferred_element_type=F32)  21.6 us
    pallas_call x4, Pallas kernels, assemble(): pl.pallas_call(kernel, out_shape=shapes, in_specs=[pl.BlockSpec(memory_sp...  10.8 us
  transfers between devices with their start and end apart: 58, of which 20 were waited for; matrix products, arithmetic and copies ran while one was open for 23% of the time, Pallas kernels for 32%

profile of v3, /device:TPU:0, one launch (start us, length us, event | category | flops | bytes accessed | tf_op | source)
XLA Modules:
  0.0 386.0 jit_solution(15589154226535642582)
XLA Ops:
  2.1 3.0 collective-permute-start.7
  5.3 1.8 constant_dynamic-slice_fusion.4.rows_ref
  7.0 1.9 collective-permute-start
  14.3 1.7 collective-permute-start.8
  16.4 6.3 %dynamic-slice_bitcast_fusion.2 = (bf16[3072,384]{1,0:T(8,128)(2,1)}, bf16[3072,384]{1,0:T(8,128)(2,1)}, bf16[3072,384]{1,0:T(8,128)(2,1)}) fusion(bf16[3072,3,1536]{2,0,1:T(8,128)(2,1)} %param.16, s32[]{:T(128)S(6)} %select_n.133, s32[]{:T(128)S(6)} %add.239, s32[]{:T(128)S(6)} %add.240), kind=kLoop, calls=%fused_computation.9 | loop fusion | bytes 14155788 | tf_op jit(solution)/shard_map/squeeze | solution.py:601
  24.6 2.0 shard_map.131.own_ref
  26.6 1.7 collective-permute-start.2
  31.5 6.2 %collective-permute-done.9.refs_4_ = bf16[128,1536]{1,0:T(8,128)(2,1)S(1)} collective-permute-done((bf16[128,1536]{1,0:T(8,128)(2,1)}, bf16[128,1536]{1,0:T(8,128)(2,1)S(1)}, u32[]{:S(2)}, u32[]{:S(2)}) %collective-permute-start.9) | collective-permute-done | bytes 393248 | tf_op jit(solution)/shard_map/ppermute | solution.py:38
  42.1 2.4 shard_map.132.refs_1_
  44.5 2.2 collective-permute-done.6
  49.8 6.3 %pad_maximum_fusion.1.weight_ref = bf16[3072,1152]{1,0:T(8,128)(2,1)} fusion(bf16[3072,384]{1,0:T(8,128)(2,1)} %get-tuple-element.92, bf16[3072,384]{1,0:T(8,128)(2,1)} %get-tuple-element.91, bf16[3072,384]{1,0:T(8,128)(2,1)} %get-tuple-element.90), kind=kLoop, calls=%fused_computation.3 | loop fusion | flops 21233664 | bytes 14155776 | tf_op jit(solution)/shard_map/concatenate | solution.py:601
  56.1 3.3 constant_dynamic-slice_fusion.3
  59.4 4.3 %copy.43 = bf16[384,3072]{0,1:T(8,128)(2,1)} copy(bf16[384,3072]{1,0:T(8,128)(2,1)} %constant_dynamic-slice_fusion.3) | data formatting | bytes 4718592
  65.7 3.4 shard_map.133.refs_0_
  69.7 3.4 shard_map.134.refs_0_
  75.2 8.1 %pad_maximum_fusion.weight_ref = bf16[3072,1536]{1,0:T(8,128)(2,1)} fusion(bf16[3072,384]{1,0:T(8,128)(2,1)S(1)} %bitcast.91, bf16[3072,1152]{1,0:T(8,128)(2,1)} %pad_maximum_fusion.1.weight_ref), kind=kLoop, calls=%fused_computation.2 | loop fusion | flops 18874368 | bytes 18874368 | tf_op jit(solution)/shard_map/concatenate | solution.py:611
  89.6 1.6 pad_maximum_fusion.3
  91.9 5.9 %collective-permute-done.16.refs_6_ = bf16[64,3200]{1,0:T(8,128)(2,1)S(1)} collective-permute-done((bf16[64,3200]{1,0:T(8,128)(2,1)}, bf16[64,3200]{1,0:T(8,128)(2,1)S(1)}, u32[]{:S(2)}, u32[]{:S(2)}) %collective-permute-start.16) | collective-permute-done | bytes 409632 | tf_op jit(solution)/shard_map/ppermute | solution.py:38
  100.7 2.9 collective-permute-done.17
  104.4 3.3 shard_map.135
  112.2 6.1 %all-to-all-start = ((bf16[8,2,192,384]{3,2,1,0:T(8,128)(2,1)}), bf16[8,2,192,384]{3,2,1,0:T(8,128)(2,1)}, u32[]{:S(2)}, u32[]{:S(2)}) async-start(bf16[8,2,192,384]{3,2,1,0:T(8,128)(2,1)} %pad_maximum_fusion.3), calls=%async_computation | async-start | bytes 4718592 | tf_op jit(solution)/shard_map/all_to_all | solution.py:708
  119.4 3.0 copy-done.2
  122.4 7.9 %shard_map.136.q_ref.k_ref.v_ref = f32[512,1152]{1,0:T(8,128)S(1)} custom-call(bf16[512,3072]{1,0:T(8,128)(2,1)} %get-tuple-element.50.rows_ref.normed_ref, bf16[3072,1152]{1,0:T(8,128)(2,1)S(1)} %copy-done.2), custom_call_target="tpu_custom_call" | custom-call | flops 5435817984 | bytes 12582912 | tf_op jit(solution)/shard_map/pallas_call | solution.py:245
  130.3 8.9 %shard_map.137.k_twin_ref.v_twin_ref.q_twin_ref = f32[512,1152]{1,0:T(8,128)S(1)} custom-call(bf16[512,3072]{1,0:T(8,128)(2,1)} %collective-permute-done.20.rows_ref, bf16[3072,1152]{1,0:T(8,128)(2,1)S(1)} %copy-done.2), custom_call_target="tpu_custom_call" | custom-call | flops 5435817984 | bytes 12582912 | tf_op jit(solution)/shard_map/pallas_call | solution.py:245
  139.2 2.9 shard_map.138
  144.2 16.6 %shard_map.139.qs_ref.ks_ref.vs_ref.back_ref = bf16[2,512,1536]{2,1,0:T(8,128)(2,1)S(1)} custom-call(s32[2]{0:T(128)S(1)} %pad_add_fusion.starts_ref, bf16[4,2,3072]{2,1,0:T(2,128)(2,1)S(1)} %pad_maximum_fusion.15.scale_ref, bf16[3072,1536]{1,0:T(8,128)(2,1)S(1)} %bitcast.85, bf16[512,1536]{1,0:T(8,128)(2,1)} %shard_map.133.refs_0_, ...), custom_call_target="tpu_custom_call" | custom-call | flops 14495514624 | bytes 15728640 | tf_op jit(solution)/shard_map/pallas_call | solution.py:218
  160.9 1.7 copy-done.60
  162.6 16.6 %shard_map.140.qs_twin_ref.ks_twin_ref.vs_twin_ref.back_twin_ref = bf16[2,512,1536]{2,1,0:T(8,128)(2,1)S(1)} custom-call(s32[2]{0:T(128)S(1)} %pad_add_fusion.starts_ref, bf16[4,2,3072]{2,1,0:T(2,128)(2,1)S(1)} %pad_maximum_fusion.15.scale_ref, bf16[3072,1536]{1,0:T(8,128)(2,1)S(1)} %bitcast.85, bf16[512,1536]{1,0:T(8,128)(2,1)} %shard_map.134.refs_0_, ...), custom_call_target="tpu_custom_call" | custom-call | flops 14495514624 | bytes 15728640 | tf_op jit(solution)/shard_map/pallas_call | solution.py:218
  179.2 1.7 copy-done.63
  181.7 4.0 %fusion.21 = f32[16,1152]{1,0:T(8,128)S(1)} fusion(bf16[3072,1152]{1,0:T(8,128)(2,1)} %pad_maximum_fusion.1.weight_ref, bf16[1,3072]{1,0:T(2,128)(2,1)S(1)} %get-tuple-element.124, bf16[1,3072]{1,0:T(2,128)(2,1)S(1)} %get-tuple-element.129, bf16[1,3072]{1,0:T(2,128)(2,1)S(1)} %get-tuple-element.123, bf16[1,3072]{1,0:T(2,128)(2,1)S(1)} %get-tuple-element.130), kind=kOutput, calls=%fused_computation.110 | convolution fusion | flops 113885184 | bytes 7176192 | tf_op jit(solution)/shard_map/dot_general | solution.py:24
  188.8 2.3 shard_map.141.up_ref.weight_ref
  191.1 5.5 %shard_map.143 = (f32[512,384]{1,0:T(8,128)S(1)}, bf16[256,384]{1,0:T(8,128)(2,1)S(1)}, bf16[256,3072]{1,0:T(8,128)(2,1)S(1)}) custom-call(bf16[512,3072]{1,0:T(8,128)(2,1)} %get-tuple-element.50.rows_ref.normed_ref, bf16[3072,384]{1,0:T(8,128)(2,1)S(1)} %shard_map.141.up_ref.weight_ref, bf16[384,3072]{1,0:T(8,128)(2,1)S(1)} %shard_map.142.down_ref), custom_call_target="tpu_custom_call" | custom-call | flops 2415919104 | bytes 11010048 | tf_op jit(solution)/shard_map/pallas_call | solution.py:279
  196.8 2.1 collective-permute-start.23
  200.7 2.6 convolution_add_fusion.1
  209.6 2.4 copy.38
  212.1 2.9 pad_maximum_fusion.2.weight_ref
  215.0 4.5 %collective-permute-done.28 = bf16[64,3072]{1,0:T(8,128)(2,1)} collective-permute-done((bf16[64,3072]{1,0:T(8,128)(2,1)}, bf16[64,3072]{1,0:T(8,128)(2,1)}, u32[]{:S(2)}, u32[]{:S(2)}) %collective-permute-start.28) | collective-permute-done | bytes 393248 | tf_op jit(solution)/shard_map/ppermute | solution.py:38
  223.9 9.3 %shard_map.144.own_sign_ref = bf16[2,512,768]{2,1,0:T(8,128)(2,1)S(1)} custom-call(s32[2]{0:T(128)S(1)} %pad_add_fusion.starts_ref, bf16[2,2,3072]{2,1,0:T(2,128)(2,1)S(1)} %pad_maximum_fusion.16.scale_ref, bf16[3072,768]{1,0:T(8,128)(2,1)S(1)} %pad_maximum_fusion.2.weight_ref, bf16[512,1536]{1,0:T(8,128)(2,1)} %shard_map.133.refs_0_, ...), custom_call_target="tpu_custom_call" | custom-call | flops 7247757312 | bytes 9437184 | tf_op jit(solution)/shard_map/pallas_call | solution.py:218
  237.6 4.6 %collective-permute-done.26 = bf16[64,3072]{1,0:T(8,128)(2,1)S(1)} collective-permute-done((bf16[64,3072]{1,0:T(8,128)(2,1)S(1)}, bf16[64,3072]{1,0:T(8,128)(2,1)S(1)}, u32[]{:S(2)}, u32[]{:S(2)}) %collective-permute-start.26) | collective-permute-done | bytes 393248 | tf_op jit(solution)/shard_map/ppermute | solution.py:38
  244.7 6.7 %collective-permute-done.31.other_ref = bf16[64,3072]{1,0:T(8,128)(2,1)S(1)} collective-permute-done((bf16[64,3072]{1,0:T(8,128)(2,1)S(1)}, bf16[64,3072]{1,0:T(8,128)(2,1)S(1)}, u32[]{:S(2)}, u32[]{:S(2)}) %collective-permute-start.31) | collective-permute-done | bytes 393248 | tf_op jit(solution)/shard_map/ppermute | solution.py:88
  254.2 12.3 %shard_map.146 = f32[512,128]{1,0:T(8,128)S(1)} custom-call(f32[512,1152]{1,0:T(8,128)S(1)} %copy-done.11, f32[512,1152]{1,0:T(8,128)S(1)} %copy-done.11, f32[512,1152]{1,0:T(8,128)S(1)} %copy-done.11, f32[512,1152]{1,0:T(8,128)S(1)} %copy-done.13, f32[512,1152]{1,0:T(8,128)S(1)} %copy-done.13, f32[512,1152]{1,0:T(8,128)S(1)} %copy-done.13, ...), custom_call_target="tpu_custom_call" | custom-call | flops 14092861440 | bytes 13631488 | tf_op jit(solution)/shard_map/pallas_call | solution.py:522
  268.7 9.1 %shard_map.147.twin_sign_ref = bf16[2,512,768]{2,1,0:T(8,128)(2,1)S(1)} custom-call(s32[2]{0:T(128)S(1)} %pad_add_fusion.starts_ref, bf16[2,2,3072]{2,1,0:T(2,128)(2,1)S(1)} %pad_maximum_fusion.16.scale_ref, bf16[3072,768]{1,0:T(8,128)(2,1)S(1)} %pad_maximum_fusion.2.weight_ref, bf16[512,1536]{1,0:T(8,128)(2,1)} %shard_map.134.refs_0_, ...), custom_call_target="tpu_custom_call" | custom-call | flops 7247757312 | bytes 9437184 | tf_op jit(solution)/shard_map/pallas_call | solution.py:218
  280.0 3.7 shard_map.148.twin_ref
  283.8 1.8 shard_map.149
  286.4 1.7 collective-permute-done.39.refs_6_
  292.4 2.2 collective-permute-done.40
  294.6 2.2 collective-permute-done.41
  306.0 1.7 copy-done.5
  307.7 1.7 copy-done.8
  309.4 2.8 shard_map.152
  314.3 7.3 %fusion.30.q_ref.k_ref.v_ref = f32[512,1152]{1,0:T(8,128)S(1)} fusion(bf16[512,3072]{1,0:T(8,128)(2,1)S(1)} %get-tuple-element.75.normed_ref, bf16[3072,1152]{1,0:T(8,128)(2,1)} %pad_maximum_fusion.1.weight_ref), kind=kOutput, calls=%fused_computation.117 | convolution fusion | flops 3623878656 | bytes 12582912 | tf_op jit(solution)/shard_map/dot_general | solution.py:24
  324.1 4.3 %fusion.31.k_twin_ref.v_twin_ref.q_twin_ref = f32[512,1152]{1,0:T(8,128)S(1)} fusion(bf16[512,3072]{1,0:T(8,128)(2,1)S(1)} %collective-permute-done.42.rows_ref, bf16[3072,1152]{1,0:T(8,128)(2,1)S(1)} %bitcast.79), kind=kOutput, calls=%fused_computation.118 | convolution fusion | flops 3623878656 | bytes 12582912 | tf_op jit(solution)/shard_map/dot_general | solution.py:24
  328.4 2.9 shard_map.151
  331.3 2.1 collective-permute-done.44
  339.2 12.1 %shard_map.153 = f32[512,128]{1,0:T(8,128)S(1)} custom-call(f32[512,1152]{1,0:T(8,128)S(1)} %fusion.30.q_ref.k_ref.v_ref, f32[512,1152]{1,0:T(8,128)S(1)} %fusion.30.q_ref.k_ref.v_ref, f32[512,1152]{1,0:T(8,128)S(1)} %fusion.30.q_ref.k_ref.v_ref, f32[512,1152]{1,0:T(8,128)S(1)} %fusion.31.k_twin_ref.v_twin_ref.q_twin_ref, ...), custom_call_target="tpu_custom_call" | custom-call | flops 14092861440 | bytes 13631488 | tf_op jit(solution)/shard_map/pallas_call | solution.py:522
  351.6 2.8 fusion.2
  356.4 1.9 copy-done.45
  358.3 1.8 shard_map.154.twin_ref
  360.5 1.8 shard_map.155
  362.6 2.2 collective-permute-done.47
  365.2 1.6 fusion.4
  369.3 3.3 all-to-all-start.1
  373.4 5.7 %all-to-all-done.1 = f32[8,1,128]{2,1,0:T(1,128)S(1)} async-done(((f32[8,1,128]{2,1,0:T(1,128)}), f32[8,1,128]{2,1,0:T(1,128)S(1)}, u32[]{:S(2)}, u32[]{:S(2)}) %all-to-all-start.1) | async-done | bytes 4128 | tf_op jit(solution)/shard_map/all_to_all | solution.py:767
  382.2 2.1 collective-permute-done.55
  (395 shorter events, 106.7 us)
Async XLA Ops:
  0.6 88.8 %copy-start = (bf16[3072,384]{1,0:T(8,128)(2,1)S(1)}, bf16[3072,384]{1,0:T(8,128)(2,1)}, u32[]{:S(2)}) copy-start(bf16[3072,384]{1,0:T(8,128)(2,1)} %param.19) | copy-start | bytes 7077892
  2.1 12.2 %collective-permute-start.7 = (bf16[128,1536]{1,0:T(8,128)(2,1)S(1)}, bf16[128,1536]{1,0:T(8,128)(2,1)S(1)}, u32[]{:S(2)}, u32[]{:S(2)}) collective-permute-start(bf16[128,1536]{1,0:T(8,128)(2,1)S(1)} %bitcast.86), channel_id=1, source_target_pairs={{0,4},{8,0},{16,8},{24,16},{28,24},{20,28},{12,20},{4,12},{1,5},{9... | collective-permute-start | bytes 1179656 | tf_op jit(solution)/shard_map/ppermute | solution.py:38
  5.2 10.9 %collective-permute-start.3 = (bf16[128,1536]{1,0:T(8,128)(2,1)S(1)}, bf16[128,1536]{1,0:T(8,128)(2,1)}, u32[]{:S(2)}, u32[]{:S(2)}) collective-permute-start(bf16[128,1536]{1,0:T(8,128)(2,1)S(1)} %bitcast.87), channel_id=1, source_target_pairs={{0,8},{8,16},{16,24},{24,28},{28,20},{20,12},{12,4},{4,0},{1,9},{9... | collective-permute-start | bytes 1179656 | tf_op jit(solution)/shard_map/ppermute | solution.py:38
  7.0 23.3 %collective-permute-start = (f32[64,1536]{1,0:T(8,128)}, f32[64,1536]{1,0:T(8,128)}, u32[]{:S(2)}, u32[]{:S(2)}) collective-permute-start(f32[64,1536]{1,0:T(8,128)} %constant_dynamic-slice_fusion.4.rows_ref), channel_id=1, source_target_pairs={{0,2},{2,0},{1,3},{3,1},{4,6},{6,4},{5,7},{7,5},{8,10},{10,8},{9,1... | collective-permute-start | bytes 1179656 | tf_op jit(solution)/shard_map/ppermute | solution.py:88
  9.7 14.2 %collective-permute-start.1 = (bf16[64,1536]{1,0:T(8,128)(2,1)}, bf16[64,1536]{1,0:T(8,128)(2,1)S(1)}, u32[]{:S(2)}, u32[]{:S(2)}) collective-permute-start(bf16[64,1536]{1,0:T(8,128)(2,1)} %get-tuple-element.117), channel_id=1, source_target_pairs={{0,1},{1,0},{2,3},{3,2},{4,5},{5,4},{6,7},{7,6},{8,9},{9,8},{10,11... | collective-permute-start | bytes 589832 | tf_op jit(solution)/shard_map/ppermute | solution.py:88
  14.3 14.0 %collective-permute-start.8 = (bf16[128,1536]{1,0:T(8,128)(2,1)S(1)}, bf16[128,1536]{1,0:T(8,128)(2,1)}, u32[]{:S(2)}, u32[]{:S(2)}) collective-permute-start(bf16[128,1536]{1,0:T(8,128)(2,1)S(1)} %collective-permute-done.7.refs_2_), channel_id=1, source_target_pairs={{0,4},{8,0},{16,8},{24,16},{28,24},{20,28},{12,20},{4,12},{1,5},{9... | collective-permute-start | bytes 1179656 | tf_op jit(solution)/shard_map/ppermute | solution.py:38
  16.0 13.8 %collective-permute-start.4 = (bf16[128,1536]{1,0:T(8,128)(2,1)}, bf16[128,1536]{1,0:T(8,128)(2,1)}, u32[]{:S(2)}, u32[]{:S(2)}) collective-permute-start(bf16[128,1536]{1,0:T(8,128)(2,1)} %collective-permute-done.3.refs_0_), channel_id=1, source_target_pairs={{0,8},{8,16},{16,24},{24,28},{28,20},{20,12},{12,4},{4,0},{1,9},{9... | collective-permute-start | bytes 1179656 | tf_op jit(solution)/shard_map/ppermute | solution.py:38
  26.6 15.5 %collective-permute-start.2 = (f32[64,128]{1,0:T(8,128)}, f32[64,128]{1,0:T(8,128)}, u32[]{:S(2)}, u32[]{:S(2)}) collective-permute-start(f32[64,128]{1,0:T(8,128)} %shard_map.131.own_ref), channel_id=1, source_target_pairs={{0,2},{2,0},{1,3},{3,1},{4,6},{6,4},{5,7},{7,5},{8,10},{10,8},{9,1... | collective-permute-start | bytes 98312 | tf_op jit(solution)/shard_map/ppermute | solution.py:88
  28.3 9.5 %collective-permute-start.9 = (bf16[128,1536]{1,0:T(8,128)(2,1)}, bf16[128,1536]{1,0:T(8,128)(2,1)S(1)}, u32[]{:S(2)}, u32[]{:S(2)}) collective-permute-start(bf16[128,1536]{1,0:T(8,128)(2,1)} %collective-permute-done.8.refs_3_), channel_id=1, source_target_pairs={{0,4},{8,0},{16,8},{24,16},{28,24},{20,28},{12,20},{4,12},{1,5},{9... | collective-permute-start | bytes 1179656 | tf_op jit(solution)/shard_map/ppermute | solution.py:38
  29.8 10.1 %collective-permute-start.5 = (bf16[128,1536]{1,0:T(8,128)(2,1)}, bf16[128,1536]{1,0:T(8,128)(2,1)S(1)}, u32[]{:S(2)}, u32[]{:S(2)}) collective-permute-start(bf16[128,1536]{1,0:T(8,128)(2,1)} %collective-permute-done.4.refs_7_), channel_id=1, source_target_pairs={{0,8},{8,16},{16,24},{24,28},{28,20},{20,12},{12,4},{4,0},{1,9},{9... | collective-permute-start | bytes 1179656 | tf_op jit(solution)/shard_map/ppermute | solution.py:38
  38.4 6.1 %collective-permute-start.10 = (bf16[128,768]{1,0:T(8,128)(2,1)}, bf16[128,768]{1,0:T(8,128)(2,1)}, u32[]{:S(2)}, u32[]{:S(2)}) collective-permute-start(bf16[128,768]{1,0:T(8,128)(2,1)} %split.25), channel_id=1, source_target_pairs={{0,4},{8,0},{16,8},{24,16},{28,24},{20,28},{12,20},{4,12},{1,5},{9... | collective-permute-start | bytes 589832 | tf_op jit(solution)/shard_map/ppermute | solution.py:38
  40.7 6.0 %collective-permute-start.6 = (bf16[128,768]{1,0:T(8,128)(2,1)}, bf16[128,768]{1,0:T(8,128)(2,1)}, u32[]{:S(2)}, u32[]{:S(2)}) collective-permute-start(bf16[128,768]{1,0:T(8,128)(2,1)} %split.24), channel_id=1, source_target_pairs={{0,8},{8,16},{16,24},{24,28},{28,20},{20,12},{12,4},{4,0},{1,9},{9... | collective-permute-start | bytes 589832 | tf_op jit(solution)/shard_map/ppermute | solution.py:38
  47.7 25.4 %collective-permute-start.11 = (bf16[64,3200]{1,0:T(8,128)(2,1)}, bf16[64,3200]{1,0:T(8,128)(2,1)}, u32[]{:S(2)}, u32[]{:S(2)}) collective-permute-start(bf16[64,3200]{1,0:T(8,128)(2,1)} %shard_map.132.refs_1_), channel_id=1, source_target_pairs={{0,8},{8,16},{16,24},{24,28},{28,20},{20,12},{12,4},{4,0},{1,9},{9... | collective-permute-start | bytes 1228808 | tf_op jit(solution)/shard_map/ppermute | solution.py:38
  48.3 25.5 %collective-permute-start.12 = (bf16[64,3200]{1,0:T(8,128)(2,1)}, bf16[64,3200]{1,0:T(8,128)(2,1)}, u32[]{:S(2)}, u32[]{:S(2)}) collective-permute-start(bf16[64,3200]{1,0:T(8,128)(2,1)} %shard_map.132.refs_1_), channel_id=1, source_target_pairs={{0,4},{8,0},{16,8},{24,16},{28,24},{20,28},{12,20},{4,12},{1,5},{9... | collective-permute-start | bytes 1228808 | tf_op jit(solution)/shard_map/ppermute | solution.py:38
  69.1 35.3 %collective-permute-start.19 = (bf16[512,1536]{1,0:T(8,128)(2,1)}, bf16[512,1536]{1,0:T(8,128)(2,1)}, u32[]{:S(2)}, u32[]{:S(2)}) collective-permute-start(bf16[512,1536]{1,0:T(8,128)(2,1)} %shard_map.133.refs_0_), channel_id=1, source_target_pairs={{0,2},{2,0},{1,3},{3,1},{4,6},{6,4},{5,7},{7,5},{8,10},{10,8},{9,1... | collective-permute-start | bytes 4718600 | tf_op jit(solution)/shard_map/ppermute | solution.py:88
  73.1 14.3 %collective-permute-start.15 = (bf16[64,3200]{1,0:T(8,128)(2,1)}, bf16[64,3200]{1,0:T(8,128)(2,1)}, u32[]{:S(2)}, u32[]{:S(2)}) collective-permute-start(bf16[64,3200]{1,0:T(8,128)(2,1)} %collective-permute-done.11.refs_0_), channel_id=1, source_target_pairs={{0,8},{8,16},{16,24},{24,28},{28,20},{20,12},{12,4},{4,0},{1,9},{9... | collective-permute-start | bytes 1228808 | tf_op jit(solution)/shard_map/ppermute | solution.py:38
  73.8 14.2 %collective-permute-start.13 = (bf16[64,3200]{1,0:T(8,128)(2,1)}, bf16[64,3200]{1,0:T(8,128)(2,1)}, u32[]{:S(2)}, u32[]{:S(2)}) collective-permute-start(bf16[64,3200]{1,0:T(8,128)(2,1)} %collective-permute-done.12.refs_2_), channel_id=1, source_target_pairs={{0,4},{8,0},{16,8},{24,16},{28,24},{20,28},{12,20},{4,12},{1,5},{9... | collective-permute-start | bytes 1228808 | tf_op jit(solution)/shard_map/ppermute | solution.py:38
  83.3 24.5 %copy-start.77 = (bf16[2,3,3072]{2,0,1:T(2,128)(2,1)}, bf16[2,3,3072]{2,0,1:T(2,128)(2,1)S(1)}, u32[]{:S(2)}) copy-start(bf16[2,3,3072]{2,0,1:T(2,128)(2,1)S(1)} %convert.21) | copy-start | bytes 110596
  87.4 10.4 %collective-permute-start.16 = (bf16[64,3200]{1,0:T(8,128)(2,1)}, bf16[64,3200]{1,0:T(8,128)(2,1)S(1)}, u32[]{:S(2)}, u32[]{:S(2)}) collective-permute-start(bf16[64,3200]{1,0:T(8,128)(2,1)} %collective-permute-done.15.refs_7_), channel_id=1, source_target_pairs={{0,8},{8,16},{16,24},{24,28},{28,20},{20,12},{12,4},{4,0},{1,9},{9... | collective-permute-start | bytes 1228808 | tf_op jit(solution)/shard_map/ppermute | solution.py:38
  88.1 10.4 %collective-permute-start.14 = (bf16[64,3200]{1,0:T(8,128)(2,1)}, bf16[64,3200]{1,0:T(8,128)(2,1)S(1)}, u32[]{:S(2)}, u32[]{:S(2)}) collective-permute-start(bf16[64,3200]{1,0:T(8,128)(2,1)} %collective-permute-done.13.refs_3_), channel_id=1, source_target_pairs={{0,4},{8,0},{16,8},{24,16},{28,24},{20,28},{12,20},{4,12},{1,5},{9... | collective-permute-start | bytes 1228808 | tf_op jit(solution)/shard_map/ppermute | solution.py:38
  97.8 5.8 %collective-permute-start.17 = (bf16[32,3200]{1,0:T(8,128)(2,1)S(1)}, bf16[32,3200]{1,0:T(8,128)(2,1)S(1)}, u32[]{:S(2)}, u32[]{:S(2)}) collective-permute-start(bf16[32,3200]{1,0:T(8,128)(2,1)S(1)} %split.26), channel_id=1, source_target_pairs={{0,8},{8,16},{16,24},{24,28},{28,20},{20,12},{12,4},{4,0},{1,9},{9... | collective-permute-start | bytes 614408 | tf_op jit(solution)/shard_map/ppermute | solution.py:38
  98.5 5.8 %collective-permute-start.18 = (bf16[32,3200]{1,0:T(8,128)(2,1)S(1)}, bf16[32,3200]{1,0:T(8,128)(2,1)S(1)}, u32[]{:S(2)}, u32[]{:S(2)}) collective-permute-start(bf16[32,3200]{1,0:T(8,128)(2,1)S(1)} %split.27), channel_id=1, source_target_pairs={{0,4},{8,0},{16,8},{24,16},{28,24},{20,28},{12,20},{4,12},{1,5},{9... | collective-permute-start | bytes 614408 | tf_op jit(solution)/shard_map/ppermute | solution.py:38
  107.7 22.6 %collective-permute-start.20 = (bf16[512,3072]{1,0:T(8,128)(2,1)}, bf16[512,3072]{1,0:T(8,128)(2,1)}, u32[]{:S(2)}, u32[]{:S(2)}) collective-permute-start(bf16[512,3072]{1,0:T(8,128)(2,1)} %get-tuple-element.50.rows_ref.normed_ref), channel_id=1, source_target_pairs={{0,1},{1,0},{2,3},{3,2},{4,5},{5,4},{6,7},{7,6},{8,9},{9,8},{10,11... | collective-permute-start | bytes 9437192 | tf_op jit(solution)/shard_map/ppermute | solution.py:88
  108.6 54.0 %collective-permute-start.21 = (bf16[512,1536]{1,0:T(8,128)(2,1)}, bf16[512,1536]{1,0:T(8,128)(2,1)}, u32[]{:S(2)}, u32[]{:S(2)}) collective-permute-start(bf16[512,1536]{1,0:T(8,128)(2,1)} %shard_map.134.refs_0_), channel_id=1, source_target_pairs={{0,2},{2,0},{1,3},{3,1},{4,6},{6,4},{5,7},{7,5},{8,10},{10,8},{9,1... | collective-permute-start | bytes 4718600 | tf_op jit(solution)/shard_map/ppermute | solution.py:88
  112.2 68.7 %all-to-all-start = ((bf16[8,2,192,384]{3,2,1,0:T(8,128)(2,1)}), bf16[8,2,192,384]{3,2,1,0:T(8,128)(2,1)}, u32[]{:S(2)}, u32[]{:S(2)}) async-start(bf16[8,2,192,384]{3,2,1,0:T(8,128)(2,1)} %pad_maximum_fusion.3), calls=%async_computation | async-start | bytes 4718592 | tf_op jit(solution)/shard_map/all_to_all | solution.py:708
  180.9 6.3 %collective-permute-start.22 = (bf16[8,2,192,384]{3,2,1,0:T(8,128)(2,1)}, bf16[8,2,192,384]{3,2,1,0:T(8,128)(2,1)S(1)}, u32[]{:S(2)}, u32[]{:S(2)}) collective-permute-start(bf16[8,2,192,384]{3,2,1,0:T(8,128)(2,1)} %all-to-all-done.own_ref), channel_id=1, source_target_pairs={{0,1},{1,0},{2,3},{3,2},{4,5},{5,4},{6,7},{7,6},{8,9},{9,8},{10,11... | collective-permute-start | bytes 7077896 | tf_op jit(solution)/shard_map/ppermute | solution.py:88
  196.8 7.6 %collective-permute-start.23 = (bf16[64,1536]{1,0:T(8,128)(2,1)S(1)}, bf16[64,1536]{1,0:T(8,128)(2,1)S(1)}, u32[]{:S(2)}, u32[]{:S(2)}) collective-permute-start(bf16[64,1536]{1,0:T(8,128)(2,1)S(1)} %get-tuple-element.109), channel_id=1, source_target_pairs={{0,8},{8,16},{16,24},{24,28},{28,20},{20,12},{12,4},{4,0},{1,9},{9... | collective-permute-start | bytes 589832 | tf_op jit(solution)/shard_map/ppermute | solution.py:38
  198.9 7.0 %collective-permute-start.27 = (bf16[64,1536]{1,0:T(8,128)(2,1)S(1)}, bf16[64,1536]{1,0:T(8,128)(2,1)S(1)}, u32[]{:S(2)}, u32[]{:S(2)}) collective-permute-start(bf16[64,1536]{1,0:T(8,128)(2,1)S(1)} %get-tuple-element.110), channel_id=1, source_target_pairs={{0,4},{8,0},{16,8},{24,16},{28,24},{20,28},{12,20},{4,12},{1,5},{9... | collective-permute-start | bytes 589832 | tf_op jit(solution)/shard_map/ppermute | solution.py:38
  206.8 14.5 %collective-permute-start.24 = (bf16[64,3072]{1,0:T(8,128)(2,1)}, bf16[64,3072]{1,0:T(8,128)(2,1)}, u32[]{:S(2)}, u32[]{:S(2)}) collective-permute-start(bf16[64,3072]{1,0:T(8,128)(2,1)} %pad_maximum_fusion.9), channel_id=1, source_target_pairs={{0,8},{8,16},{16,24},{24,28},{28,20},{20,12},{12,4},{4,0},{1,9},{9... | collective-permute-start | bytes 1179656 | tf_op jit(solution)/shard_map/ppermute | solution.py:38
  209.0 10.5 %collective-permute-start.28 = (bf16[64,3072]{1,0:T(8,128)(2,1)}, bf16[64,3072]{1,0:T(8,128)(2,1)}, u32[]{:S(2)}, u32[]{:S(2)}) collective-permute-start(bf16[64,3072]{1,0:T(8,128)(2,1)} %pad_maximum_fusion.10), channel_id=1, source_target_pairs={{0,4},{8,0},{16,8},{24,16},{28,24},{20,28},{12,20},{4,12},{1,5},{9... | collective-permute-start | bytes 1179656 | tf_op jit(solution)/shard_map/ppermute | solution.py:38
  220.7 12.5 %collective-permute-start.29 = (bf16[64,3072]{1,0:T(8,128)(2,1)S(1)}, bf16[64,3072]{1,0:T(8,128)(2,1)S(1)}, u32[]{:S(2)}, u32[]{:S(2)}) collective-permute-start(bf16[64,3072]{1,0:T(8,128)(2,1)S(1)} %add_convert_fusion.1), channel_id=1, source_target_pairs={{0,4},{8,0},{16,8},{24,16},{28,24},{20,28},{12,20},{4,12},{1,5},{9... | collective-permute-start | bytes 1179656 | tf_op jit(solution)/shard_map/ppermute | solution.py:38
  222.4 10.8 %collective-permute-start.25 = (bf16[64,3072]{1,0:T(8,128)(2,1)S(1)}, bf16[64,3072]{1,0:T(8,128)(2,1)S(1)}, u32[]{:S(2)}, u32[]{:S(2)}) collective-permute-start(bf16[64,3072]{1,0:T(8,128)(2,1)S(1)} %fusion.6), channel_id=1, source_target_pairs={{0,8},{8,16},{16,24},{24,28},{28,20},{20,12},{12,4},{4,0},{1,9},{9... | collective-permute-start | bytes 1179656 | tf_op jit(solution)/shard_map/ppermute | solution.py:38
  223.9 30.3 %copy-start.64 = (bf16[2,512,1536]{2,1,0:T(8,128)(2,1)S(1)}, bf16[2,512,1536]{2,1,0:T(8,128)(2,1)}, u32[]{:S(2)}) copy-start(bf16[2,512,1536]{2,1,0:T(8,128)(2,1)} %copy-done.63) | copy-start | bytes 9437188
  233.2 50.6 %copy-start.56 = (bf16[2,512,768]{2,1,0:T(8,128)(2,1)}, bf16[2,512,768]{2,1,0:T(8,128)(2,1)S(1)}, u32[]{:S(2)}) copy-start(bf16[2,512,768]{2,1,0:T(8,128)(2,1)S(1)} %shard_map.144.own_sign_ref) | copy-start | bytes 4718596
  233.4 8.7 %collective-permute-start.26 = (bf16[64,3072]{1,0:T(8,128)(2,1)S(1)}, bf16[64,3072]{1,0:T(8,128)(2,1)S(1)}, u32[]{:S(2)}, u32[]{:S(2)}) collective-permute-start(bf16[64,3072]{1,0:T(8,128)(2,1)S(1)} %get-tuple-element.99), channel_id=1, source_target_pairs={{0,8},{8,16},{16,24},{24,28},{28,20},{20,12},{12,4},{4,0},{1,9},{9... | collective-permute-start | bytes 1179656 | tf_op jit(solution)/shard_map/ppermute | solution.py:38
  234.9 8.4 %collective-permute-start.30 = (bf16[64,3072]{1,0:T(8,128)(2,1)S(1)}, bf16[64,3072]{1,0:T(8,128)(2,1)S(1)}, u32[]{:S(2)}, u32[]{:S(2)}) collective-permute-start(bf16[64,3072]{1,0:T(8,128)(2,1)S(1)} %get-tuple-element.100), channel_id=1, source_target_pairs={{0,4},{8,0},{16,8},{24,16},{28,24},{20,28},{12,20},{4,12},{1,5},{9... | collective-permute-start | bytes 1179656 | tf_op jit(solution)/shard_map/ppermute | solution.py:38
  237.0 7.7 %collective-permute-start.32 = (bf16[64,3072]{1,0:T(8,128)(2,1)S(1)}, bf16[64,3072]{1,0:T(8,128)(2,1)S(1)}, u32[]{:S(2)}, u32[]{:S(2)}) collective-permute-start(bf16[64,3072]{1,0:T(8,128)(2,1)S(1)} %pad_maximum_fusion.12), channel_id=1, source_target_pairs={{0,1},{1,0},{2,3},{3,2},{4,5},{5,4},{6,7},{7,6},{8,9},{9,8},{10,11... | collective-permute-start | bytes 1179656 | tf_op jit(solution)/shard_map/ppermute | solution.py:88
  237.1 17.1 %collective-permute-start.35 = (bf16[512,128]{1,0:T(8,128)(2,1)S(1)}, bf16[512,128]{1,0:T(8,128)(2,1)S(1)}, u32[]{:S(2)}, u32[]{:S(2)}) collective-permute-start(bf16[512,128]{1,0:T(8,128)(2,1)S(1)} %copy-done.47), channel_id=1, source_target_pairs={{0,1},{1,0},{2,3},{3,2},{4,5},{5,4},{6,7},{7,6},{8,9},{9,8},{10,11... | collective-permute-start | bytes 393224 | tf_op jit(solution)/shard_map/ppermute | solution.py:88
  243.5 7.8 %collective-permute-start.31 = (bf16[64,3072]{1,0:T(8,128)(2,1)S(1)}, bf16[64,3072]{1,0:T(8,128)(2,1)S(1)}, u32[]{:S(2)}, u32[]{:S(2)}) collective-permute-start(bf16[64,3072]{1,0:T(8,128)(2,1)S(1)} %fusion.9.own_ref), channel_id=1, source_target_pairs={{0,2},{2,0},{1,3},{3,1},{4,6},{6,4},{5,7},{7,5},{8,10},{10,8},{9,1... | collective-permute-start | bytes 1179656 | tf_op jit(solution)/shard_map/ppermute | solution.py:88
  244.6 35.3 %copy-start.89 = (f32[16,384]{1,0:T(8,128)}, f32[16,384]{1,0:T(8,128)S(1)}, u32[]{:S(2)}) copy-start(f32[16,384]{1,0:T(8,128)S(1)} %fusion.23) | copy-start | bytes 73732
  252.1 14.4 %collective-permute-start.33 = (bf16[64,3200]{1,0:T(8,128)(2,1)S(1)}, bf16[64,3200]{1,0:T(8,128)(2,1)S(1)}, u32[]{:S(2)}, u32[]{:S(2)}) collective-permute-start(bf16[64,3200]{1,0:T(8,128)(2,1)S(1)} %get-tuple-element.63.refs_1_), channel_id=1, source_target_pairs={{0,8},{8,16},{16,24},{24,28},{28,20},{20,12},{12,4},{4,0},{1,9},{9... | collective-permute-start | bytes 1228808 | tf_op jit(solution)/shard_map/ppermute | solution.py:38
  253.6 14.4 %collective-permute-start.34 = (bf16[64,3200]{1,0:T(8,128)(2,1)S(1)}, bf16[64,3200]{1,0:T(8,128)(2,1)S(1)}, u32[]{:S(2)}, u32[]{:S(2)}) collective-permute-start(bf16[64,3200]{1,0:T(8,128)(2,1)S(1)} %get-tuple-element.63.refs_1_), channel_id=1, source_target_pairs={{0,4},{8,0},{16,8},{24,16},{28,24},{20,28},{12,20},{4,12},{1,5},{9... | collective-permute-start | bytes 1228808 | tf_op jit(solution)/shard_map/ppermute | solution.py:38
  266.6 11.3 %collective-permute-start.38 = (bf16[64,3200]{1,0:T(8,128)(2,1)S(1)}, bf16[64,3200]{1,0:T(8,128)(2,1)S(1)}, u32[]{:S(2)}, u32[]{:S(2)}) collective-permute-start(bf16[64,3200]{1,0:T(8,128)(2,1)S(1)} %collective-permute-done.33.refs_0_), channel_id=1, source_target_pairs={{0,8},{8,16},{16,24},{24,28},{28,20},{20,12},{12,4},{4,0},{1,9},{9... | collective-permute-start | bytes 1228808 | tf_op jit(solution)/shard_map/ppermute | solution.py:38
  268.1 11.3 %collective-permute-start.36 = (bf16[64,3200]{1,0:T(8,128)(2,1)S(1)}, bf16[64,3200]{1,0:T(8,128)(2,1)S(1)}, u32[]{:S(2)}, u32[]{:S(2)}) collective-permute-start(bf16[64,3200]{1,0:T(8,128)(2,1)S(1)} %collective-permute-done.34.refs_2_), channel_id=1, source_target_pairs={{0,4},{8,0},{16,8},{24,16},{28,24},{20,28},{12,20},{4,12},{1,5},{9... | collective-permute-start | bytes 1228808 | tf_op jit(solution)/shard_map/ppermute | solution.py:38
  277.9 10.2 %collective-permute-start.39 = (bf16[64,3200]{1,0:T(8,128)(2,1)S(1)}, bf16[64,3200]{1,0:T(8,128)(2,1)S(1)}, u32[]{:S(2)}, u32[]{:S(2)}) collective-permute-start(bf16[64,3200]{1,0:T(8,128)(2,1)S(1)} %collective-permute-done.38.refs_7_), channel_id=1, source_target_pairs={{0,8},{8,16},{16,24},{24,28},{28,20},{20,12},{12,4},{4,0},{1,9},{9... | collective-permute-start | bytes 1228808 | tf_op jit(solution)/shard_map/ppermute | solution.py:38
  279.4 10.9 %collective-permute-start.37 = (bf16[64,3200]{1,0:T(8,128)(2,1)S(1)}, bf16[64,3200]{1,0:T(8,128)(2,1)S(1)}, u32[]{:S(2)}, u32[]{:S(2)}) collective-permute-start(bf16[64,3200]{1,0:T(8,128)(2,1)S(1)} %collective-permute-done.36.refs_3_), channel_id=1, source_target_pairs={{0,4},{8,0},{16,8},{24,16},{28,24},{20,28},{12,20},{4,12},{1,5},{9... | collective-permute-start | bytes 1228808 | tf_op jit(solution)/shard_map/ppermute | solution.py:38
  288.8 5.8 %collective-permute-start.40 = (bf16[32,3200]{1,0:T(8,128)(2,1)S(1)}, bf16[32,3200]{1,0:T(8,128)(2,1)S(1)}, u32[]{:S(2)}, u32[]{:S(2)}) collective-permute-start(bf16[32,3200]{1,0:T(8,128)(2,1)S(1)} %split.22), channel_id=1, source_target_pairs={{0,8},{8,16},{16,24},{24,28},{28,20},{20,12},{12,4},{4,0},{1,9},{9... | collective-permute-start | bytes 614408 | tf_op jit(solution)/shard_map/ppermute | solution.py:38
  291.1 5.8 %collective-permute-start.41 = (bf16[32,3200]{1,0:T(8,128)(2,1)S(1)}, bf16[32,3200]{1,0:T(8,128)(2,1)S(1)}, u32[]{:S(2)}, u32[]{:S(2)}) collective-permute-start(bf16[32,3200]{1,0:T(8,128)(2,1)S(1)} %split.23), channel_id=1, source_target_pairs={{0,4},{8,0},{16,8},{24,16},{28,24},{20,28},{12,20},{4,12},{1,5},{9... | collective-permute-start | bytes 614408 | tf_op jit(solution)/shard_map/ppermute | solution.py:38
  304.5 34.7 %copy-start.48 = (bf16[512,128]{1,0:T(8,128)(2,1)}, bf16[512,128]{1,0:T(8,128)(2,1)S(1)}, u32[]{:S(2)}) copy-start(bf16[512,128]{1,0:T(8,128)(2,1)S(1)} %get-tuple-element.81.tail_ref.own_tail_ref) | copy-start | bytes 393220
  304.5 19.5 %collective-permute-start.42 = (bf16[512,3072]{1,0:T(8,128)(2,1)S(1)}, bf16[512,3072]{1,0:T(8,128)(2,1)S(1)}, u32[]{:S(2)}, u32[]{:S(2)}) collective-permute-start(bf16[512,3072]{1,0:T(8,128)(2,1)S(1)} %get-tuple-element.75.normed_ref), channel_id=1, source_target_pairs={{0,1},{1,0},{2,3},{3,2},{4,5},{5,4},{6,7},{7,6},{8,9},{9,8},{10,11... | collective-permute-start | bytes 9437192 | tf_op jit(solution)/shard_map/ppermute | solution.py:88
  312.2 9.5 %collective-permute-start.48 = (bf16[64,1536]{1,0:T(8,128)(2,1)S(1)}, bf16[64,1536]{1,0:T(8,128)(2,1)S(1)}, u32[]{:S(2)}, u32[]{:S(2)}) collective-permute-start(bf16[64,1536]{1,0:T(8,128)(2,1)S(1)} %get-tuple-element.104), channel_id=1, source_target_pairs={{0,4},{8,0},{16,8},{24,16},{28,24},{20,28},{12,20},{4,12},{1,5},{9... | collective-permute-start | bytes 589832 | tf_op jit(solution)/shard_map/ppermute | solution.py:38
  312.9 8.9 %collective-permute-start.43 = (bf16[64,1536]{1,0:T(8,128)(2,1)S(1)}, bf16[64,1536]{1,0:T(8,128)(2,1)S(1)}, u32[]{:S(2)}, u32[]{:S(2)}) collective-permute-start(bf16[64,1536]{1,0:T(8,128)(2,1)S(1)} %get-tuple-element.103), channel_id=1, source_target_pairs={{0,8},{8,16},{16,24},{24,28},{28,20},{20,12},{12,4},{4,0},{1,9},{9... | collective-permute-start | bytes 589832 | tf_op jit(solution)/shard_map/ppermute | solution.py:38
  321.7 17.5 %collective-permute-start.46 = (bf16[512,128]{1,0:T(8,128)(2,1)S(1)}, bf16[512,128]{1,0:T(8,128)(2,1)S(1)}, u32[]{:S(2)}, u32[]{:S(2)}) collective-permute-start(bf16[512,128]{1,0:T(8,128)(2,1)S(1)} %get-tuple-element.81.tail_ref.own_tail_ref), channel_id=1, source_target_pairs={{0,1},{1,0},{2,3},{3,2},{4,5},{5,4},{6,7},{7,6},{8,9},{9,8},{10,11... | collective-permute-start | bytes 393224 | tf_op jit(solution)/shard_map/ppermute | solution.py:88
  321.9 11.5 %collective-permute-start.44 = (bf16[64,3072]{1,0:T(8,128)(2,1)S(1)}, bf16[64,3072]{1,0:T(8,128)(2,1)S(1)}, u32[]{:S(2)}, u32[]{:S(2)}) collective-permute-start(bf16[64,3072]{1,0:T(8,128)(2,1)S(1)} %pad_maximum_fusion.13), channel_id=1, source_target_pairs={{0,8},{8,16},{16,24},{24,28},{28,20},{20,12},{12,4},{4,0},{1,9},{9... | collective-permute-start | bytes 1179656 | tf_op jit(solution)/shard_map/ppermute | solution.py:38
  322.6 11.8 %collective-permute-start.49 = (bf16[64,3072]{1,0:T(8,128)(2,1)S(1)}, bf16[64,3072]{1,0:T(8,128)(2,1)S(1)}, u32[]{:S(2)}, u32[]{:S(2)}) collective-permute-start(bf16[64,3072]{1,0:T(8,128)(2,1)S(1)} %pad_maximum_fusion.14), channel_id=1, source_target_pairs={{0,4},{8,0},{16,8},{24,16},{28,24},{20,28},{12,20},{4,12},{1,5},{9... | collective-permute-start | bytes 1179656 | tf_op jit(solution)/shard_map/ppermute | solution.py:38
  337.2 14.4 %collective-permute-start.45 = (bf16[64,3072]{1,0:T(8,128)(2,1)}, bf16[64,3072]{1,0:T(8,128)(2,1)}, u32[]{:S(2)}, u32[]{:S(2)}) collective-permute-start(bf16[64,3072]{1,0:T(8,128)(2,1)} %fusion.1), channel_id=1, source_target_pairs={{0,8},{8,16},{16,24},{24,28},{28,20},{20,12},{12,4},{4,0},{1,9},{9... | collective-permute-start | bytes 1179656 | tf_op jit(solution)/shard_map/ppermute | solution.py:38
  337.8 13.8 %collective-permute-start.50 = (bf16[64,3072]{1,0:T(8,128)(2,1)}, bf16[64,3072]{1,0:T(8,128)(2,1)}, u32[]{:S(2)}, u32[]{:S(2)}) collective-permute-start(bf16[64,3072]{1,0:T(8,128)(2,1)} %add_convert_fusion), channel_id=1, source_target_pairs={{0,4},{8,0},{16,8},{24,16},{28,24},{20,28},{12,20},{4,12},{1,5},{9... | collective-permute-start | bytes 1179656 | tf_op jit(solution)/shard_map/ppermute | solution.py:38
  354.4 10.5 %collective-permute-start.47 = (bf16[64,3072]{1,0:T(8,128)(2,1)}, bf16[64,3072]{1,0:T(8,128)(2,1)}, u32[]{:S(2)}, u32[]{:S(2)}) collective-permute-start(bf16[64,3072]{1,0:T(8,128)(2,1)} %get-tuple-element.93), channel_id=1, source_target_pairs={{0,8},{8,16},{16,24},{24,28},{28,20},{20,12},{12,4},{4,0},{1,9},{9... | collective-permute-start | bytes 1179656 | tf_op jit(solution)/shard_map/ppermute | solution.py:38
  355.0 10.2 %collective-permute-start.51 = (bf16[64,3072]{1,0:T(8,128)(2,1)}, bf16[64,3072]{1,0:T(8,128)(2,1)}, u32[]{:S(2)}, u32[]{:S(2)}) collective-permute-start(bf16[64,3072]{1,0:T(8,128)(2,1)} %get-tuple-element.94), channel_id=1, source_target_pairs={{0,4},{8,0},{16,8},{24,16},{28,24},{20,28},{12,20},{4,12},{1,5},{9... | collective-permute-start | bytes 1179656 | tf_op jit(solution)/shard_map/ppermute | solution.py:38
  367.5 11.6 %collective-permute-start.52 = (bf16[64,1536]{1,0:T(8,128)(2,1)}, bf16[64,1536]{1,0:T(8,128)(2,1)}, u32[]{:S(2)}, u32[]{:S(2)}) collective-permute-start(bf16[64,1536]{1,0:T(8,128)(2,1)} %constant_dynamic-slice_fusion), channel_id=1, source_target_pairs={{0,2},{2,0},{1,3},{3,1},{4,6},{6,4},{5,7},{7,5},{8,10},{10,8},{9,1... | collective-permute-start | bytes 589832 | tf_op jit(solution)/shard_map/ppermute | solution.py:88
  369.3 9.7 %all-to-all-start.1 = ((f32[8,1,128]{2,1,0:T(1,128)}), f32[8,1,128]{2,1,0:T(1,128)S(1)}, u32[]{:S(2)}, u32[]{:S(2)}) async-start(f32[8,1,128]{2,1,0:T(1,128)} %bitcast.28), calls=%async_computation.1 | async-start | bytes 8192 | tf_op jit(solution)/shard_map/all_to_all | solution.py:767
  379.1 1.7 collective-permute-start.54
  380.2 4.6 %collective-permute-start.53 = (f32[64,1536]{1,0:T(8,128)S(1)}, f32[64,1536]{1,0:T(8,128)S(1)}, u32[]{:S(2)}, u32[]{:S(2)}) collective-permute-start(f32[64,1536]{1,0:T(8,128)S(1)} %multiply_add_fusion), channel_id=1, source_target_pairs={{0,1},{1,0},{2,3},{3,2},{4,5},{5,4},{6,7},{7,6},{8,9},{9,8},{10,11... | collective-permute-start | bytes 1179656 | tf_op jit(solution)/shard_map/ppermute | solution.py:88
  380.7 3.5 collective-permute-start.55
  (94 other events, 652.7 us)

commit v4 on v3

--- a/solution.py
+++ b/solution.py
@@ -654,6 +654,19 @@
 
         return job
 
+    exchanged = []
+
+    def estimate_exchange(token):
+        estimate = jnp.sum(sum(mlp_shares), axis=1)
+        attn_share = jnp.sum(sum(attn_shares), axis=1).reshape(2, queries)
+        estimate = estimate + jnp.pad(attn_share, ((0, 0), (0, half_tokens - queries))).reshape(tokens)
+        by_slot = estimate.reshape(2, ctx_size, half)
+        by_slot = jnp.where(first, by_slot, by_slot[::-1]).transpose(1, 0, 2).reshape(ctx_size, row_count)
+        by_owner = by_slot[owner_slot][:, None]
+        own_estimate = jnp.sum(lax.all_to_all(by_owner, "ctx", 0, 0, tiled=True), axis=0)
+        exchanged.append(own_estimate)
+        return exchanged
+
     def no_job(token):
         return []
 
@@ -737,7 +750,12 @@
         if step == 0:
             jobs = [no_job, unit_weights, unit_products(0)]
         else:
-            jobs = [lambda token: [raw_own], lambda token: [attended], head_tangent(step), unit_tangent(step)]
+            jobs = [
+                lambda token: [raw_own],
+                lambda token: [attended] + unit_tangent(step)(attended),
+                head_tangent(step),
+                estimate_exchange,
+            ]
         branch = ring_reduce(parts, cycle, BF16, jobs).astype(BF16)
         if step == STEPS - 1:
             break
@@ -747,9 +765,6 @@
             branch_other = sum_tp(branch) - branch.astype(F32)
         last_gate = gate
 
-    estimate = jnp.sum(sum(mlp_shares), axis=1)
-    attn_share = jnp.sum(sum(attn_shares), axis=1).reshape(2, queries)
-    estimate = estimate + jnp.pad(attn_share, ((0, 0), (0, half_tokens - queries))).reshape(tokens)
     def own_columns(array, index):
         return lax.dynamic_slice_in_dim(array, index * local_width, local_width, 1)
 
@@ -761,10 +776,7 @@
     lat_cols = own_columns(rows, tp_index) + step_size * (own_columns(gate, tp_index) * whole)
     latent_out = join_probe(lat_cols, 0)
 
-    by_slot = estimate.reshape(2, ctx_size, half)
-    by_slot = jnp.where(first, by_slot, by_slot[::-1]).transpose(1, 0, 2).reshape(ctx_size, row_count)
-    by_owner = by_slot[owner_slot][:, None]
-    own_estimate = jnp.sum(lax.all_to_all(by_owner, "ctx", 0, 0, tiled=True), axis=0)
+    own_estimate = exchanged[0]
     own_estimate = own_estimate + swap(own_estimate, "probe")
     own_estimate = sum_tp(own_estimate)[0]
     density_change = -step_size * own_estimate / (2 * math.sqrt(full_width))

time: 393 us -> 376 us (0.957)
  local copies, waits for them, and re-layouts: 64.7 us -> 51.1 us
  waiting for transfers between devices: 57.6 us -> 61.9 us
    unnamed x205 -> x149, local copies, waits for them, and re-layouts: 36.2 us -> 23.7 us
    ppermute x16, waiting for transfers between devices: 8.79 us -> 15.1 us  [swap(): return lax.ppermute(x, axis, [(0, 1), (1, 0)])]
    convert_element_type x6, other arithmetic: 6.87 us -> 2.74 us  [ring_reduce(): up, down = (up.astype(wire), down.astype(wire))]
  transfers between devices with their start and end apart: 58 -> 58, of which waited for: 20 -> 20; matrix products, arithmetic and copies ran while one was open for 23% -> 23% of each run, Pallas kernels for 32% -> 33%
where the time goes in v4:
time: 376 us; the launch traced here: 369 us
  Pallas kernels  135 us (36%)
  waiting for transfers between devices  61.9 us (16%)
  starting transfers between devices  60.7 us (16%)
  local copies, waits for them, and re-layouts  51.1 us (14%)
  other arithmetic  37.5 us (10%)
  matrix products  18.6 us (5%)
  between operations  4.17 us (1%)
    pallas_call x4, Pallas kernels, sign_products(): pl.pallas_call(kernel, grid=(blocks,), out_shape=jax.ShapeDtypeStruct((st...  51.5 us
    ppermute x40, starting transfers between devices, ring_shift(): return lax.ppermute(x, 'ctx', pairs)  43.2 us
    ppermute x40, waiting for transfers between devices, ring_shift(): return lax.ppermute(x, 'ctx', pairs)  40.5 us
    pallas_call x2, Pallas kernels, attention_tangent(): pl.pallas_call(kernel, grid=(heads,), out_shape=jax.ShapeDtypeStruct((2 *...  23.8 us
    unnamed x149, local copies, waits for them, and re-layouts  23.7 us
    pallas_call x4, Pallas kernels, project(): pl.pallas_call(kernel, grid=(total_columns // columns,), out_shape=jax.Sh...  22.3 us
    dot_general x8, matrix products, dot(): return jnp.dot(a, b, preferred_element_type=F32)  18.6 us
    ppermute x16, waiting for transfers between devices, swap(): return lax.ppermute(x, axis, [(0, 1), (1, 0)])  15.1 us
  transfers between devices with their start and end apart: 58, of which 20 were waited for; matrix products, arithmetic and copies ran while one was open for 23% of the time, Pallas kernels for 33%

profile of v4, /device:TPU:0, one launch (start us, length us, event | category | flops | bytes accessed | tf_op | source)
XLA Modules:
  0.0 368.9 jit_solution(5234949764543721770)
XLA Ops:
  2.1 3.0 collective-permute-start.7
  5.3 1.8 constant_dynamic-slice_fusion.4.rows_ref
  7.0 1.9 collective-permute-start
  12.7 1.7 collective-permute-done.7.refs_2_
  14.3 1.7 collective-permute-start.8
  16.4 6.2 %dynamic-slice_bitcast_fusion.2 = (bf16[3072,384]{1,0:T(8,128)(2,1)}, bf16[3072,384]{1,0:T(8,128)(2,1)}, bf16[3072,384]{1,0:T(8,128)(2,1)}) fusion(bf16[3072,3,1536]{2,0,1:T(8,128)(2,1)} %param.16, s32[]{:T(128)S(6)} %select_n.133, s32[]{:T(128)S(6)} %add.239, s32[]{:T(128)S(6)} %add.240), kind=kLoop, calls=%fused_computation.9 | loop fusion | bytes 14155788 | tf_op jit(solution)/shard_map/squeeze | solution.py:601
  24.6 2.0 shard_map.131.own_ref
  26.6 1.7 collective-permute-start.2
  31.5 6.2 %collective-permute-done.9.refs_4_ = bf16[128,1536]{1,0:T(8,128)(2,1)S(1)} collective-permute-done((bf16[128,1536]{1,0:T(8,128)(2,1)}, bf16[128,1536]{1,0:T(8,128)(2,1)S(1)}, u32[]{:S(2)}, u32[]{:S(2)}) %collective-permute-start.9) | collective-permute-done | bytes 393248 | tf_op jit(solution)/shard_map/ppermute | solution.py:38
  42.1 2.3 shard_map.132.refs_1_
  44.5 2.2 collective-permute-done.6
  49.8 6.3 %pad_maximum_fusion.1.weight_ref = bf16[3072,1152]{1,0:T(8,128)(2,1)} fusion(bf16[3072,384]{1,0:T(8,128)(2,1)} %get-tuple-element.92, bf16[3072,384]{1,0:T(8,128)(2,1)} %get-tuple-element.91, bf16[3072,384]{1,0:T(8,128)(2,1)} %get-tuple-element.90), kind=kLoop, calls=%fused_computation.3 | loop fusion | flops 21233664 | bytes 14155776 | tf_op jit(solution)/shard_map/concatenate | solution.py:601
  56.1 3.3 constant_dynamic-slice_fusion.3
  59.4 4.3 %copy.43 = bf16[384,3072]{0,1:T(8,128)(2,1)} copy(bf16[384,3072]{1,0:T(8,128)(2,1)} %constant_dynamic-slice_fusion.3) | data formatting | bytes 4718592
  65.6 3.4 shard_map.133.refs_0_
  69.7 3.4 shard_map.134.refs_0_
  75.2 8.1 %pad_maximum_fusion.weight_ref = bf16[3072,1536]{1,0:T(8,128)(2,1)} fusion(bf16[3072,384]{1,0:T(8,128)(2,1)S(1)} %bitcast.91, bf16[3072,1152]{1,0:T(8,128)(2,1)} %pad_maximum_fusion.1.weight_ref), kind=kLoop, calls=%fused_computation.2 | loop fusion | flops 18874368 | bytes 18874368 | tf_op jit(solution)/shard_map/concatenate | solution.py:611
  89.6 1.6 pad_maximum_fusion.3
  91.8 6.0 %collective-permute-done.16.refs_6_ = bf16[64,3200]{1,0:T(8,128)(2,1)S(1)} collective-permute-done((bf16[64,3200]{1,0:T(8,128)(2,1)}, bf16[64,3200]{1,0:T(8,128)(2,1)S(1)}, u32[]{:S(2)}, u32[]{:S(2)}) %collective-permute-start.16) | collective-permute-done | bytes 409632 | tf_op jit(solution)/shard_map/ppermute | solution.py:38
  100.7 2.9 collective-permute-done.17
  104.4 3.2 shard_map.135
  112.2 6.1 %all-to-all-start = ((bf16[8,2,192,384]{3,2,1,0:T(8,128)(2,1)}), bf16[8,2,192,384]{3,2,1,0:T(8,128)(2,1)}, u32[]{:S(2)}, u32[]{:S(2)}) async-start(bf16[8,2,192,384]{3,2,1,0:T(8,128)(2,1)} %pad_maximum_fusion.3), calls=%async_computation | async-start | bytes 4718592 | tf_op jit(solution)/shard_map/all_to_all | solution.py:721
  119.4 3.0 copy-done.2
  122.4 7.9 %shard_map.136.q_ref.k_ref.v_ref = f32[512,1152]{1,0:T(8,128)S(1)} custom-call(bf16[512,3072]{1,0:T(8,128)(2,1)} %get-tuple-element.50.rows_ref.normed_ref, bf16[3072,1152]{1,0:T(8,128)(2,1)S(1)} %copy-done.2), custom_call_target="tpu_custom_call" | custom-call | flops 5435817984 | bytes 12582912 | tf_op jit(solution)/shard_map/pallas_call | solution.py:245
  130.4 8.9 %shard_map.137.k_twin_ref.v_twin_ref.q_twin_ref = f32[512,1152]{1,0:T(8,128)S(1)} custom-call(bf16[512,3072]{1,0:T(8,128)(2,1)} %collective-permute-done.20.rows_ref, bf16[3072,1152]{1,0:T(8,128)(2,1)S(1)} %copy-done.2), custom_call_target="tpu_custom_call" | custom-call | flops 5435817984 | bytes 12582912 | tf_op jit(solution)/shard_map/pallas_call | solution.py:245
  139.3 2.9 shard_map.138
  144.3 16.6 %shard_map.139.qs_ref.ks_ref.vs_ref.back_ref = bf16[2,512,1536]{2,1,0:T(8,128)(2,1)S(1)} custom-call(s32[2]{0:T(128)S(1)} %pad_add_fusion.starts_ref, bf16[4,2,3072]{2,1,0:T(2,128)(2,1)S(1)} %pad_maximum_fusion.15.scale_ref, bf16[3072,1536]{1,0:T(8,128)(2,1)S(1)} %bitcast.85, bf16[512,1536]{1,0:T(8,128)(2,1)} %shard_map.133.refs_0_, ...), custom_call_target="tpu_custom_call" | custom-call | flops 14495514624 | bytes 15728640 | tf_op jit(solution)/shard_map/pallas_call | solution.py:218
  160.9 1.7 copy-done.32
  162.6 16.6 %shard_map.140.qs_twin_ref.ks_twin_ref.vs_twin_ref.back_twin_ref = bf16[2,512,1536]{2,1,0:T(8,128)(2,1)S(1)} custom-call(s32[2]{0:T(128)S(1)} %pad_add_fusion.starts_ref, bf16[4,2,3072]{2,1,0:T(2,128)(2,1)S(1)} %pad_maximum_fusion.15.scale_ref, bf16[3072,1536]{1,0:T(8,128)(2,1)S(1)} %bitcast.85, bf16[512,1536]{1,0:T(8,128)(2,1)} %shard_map.134.refs_0_, ...), custom_call_target="tpu_custom_call" | custom-call | flops 14495514624 | bytes 15728640 | tf_op jit(solution)/shard_map/pallas_call | solution.py:218
  179.2 1.7 copy-done.34
  181.7 4.0 %fusion.21 = f32[16,1152]{1,0:T(8,128)S(1)} fusion(bf16[3072,1152]{1,0:T(8,128)(2,1)} %pad_maximum_fusion.1.weight_ref, bf16[1,3072]{1,0:T(2,128)(2,1)S(1)} %get-tuple-element.124, bf16[1,3072]{1,0:T(2,128)(2,1)S(1)} %get-tuple-element.129, bf16[1,3072]{1,0:T(2,128)(2,1)S(1)} %get-tuple-element.123, bf16[1,3072]{1,0:T(2,128)(2,1)S(1)} %get-tuple-element.130), kind=kOutput, calls=%fused_computation.110 | convolution fusion | flops 113885184 | bytes 7176192 | tf_op jit(solution)/shard_map/dot_general | solution.py:24
  188.8 2.3 shard_map.141.up_ref.weight_ref
  191.1 5.5 %shard_map.143 = (f32[512,384]{1,0:T(8,128)S(1)}, bf16[256,384]{1,0:T(8,128)(2,1)S(1)}, bf16[256,3072]{1,0:T(8,128)(2,1)S(1)}) custom-call(bf16[512,3072]{1,0:T(8,128)(2,1)} %get-tuple-element.50.rows_ref.normed_ref, bf16[3072,384]{1,0:T(8,128)(2,1)S(1)} %shard_map.141.up_ref.weight_ref, bf16[384,3072]{1,0:T(8,128)(2,1)S(1)} %shard_map.142.down_ref), custom_call_target="tpu_custom_call" | custom-call | flops 2415919104 | bytes 11010048 | tf_op jit(solution)/shard_map/pallas_call | solution.py:279
  196.8 2.1 collective-permute-start.23
  200.7 2.7 convolution_add_fusion.1
  209.5 2.5 copy.38
  212.0 2.9 pad_maximum_fusion.2.weight_ref
  214.9 4.5 %collective-permute-done.28 = bf16[64,3072]{1,0:T(8,128)(2,1)} collective-permute-done((bf16[64,3072]{1,0:T(8,128)(2,1)}, bf16[64,3072]{1,0:T(8,128)(2,1)}, u32[]{:S(2)}, u32[]{:S(2)}) %collective-permute-start.28) | collective-permute-done | bytes 393248 | tf_op jit(solution)/shard_map/ppermute | solution.py:38
  222.3 1.5 collective-permute-start.25
  223.9 9.1 %shard_map.144.own_sign_ref = bf16[2,512,768]{2,1,0:T(8,128)(2,1)S(1)} custom-call(s32[2]{0:T(128)S(1)} %pad_add_fusion.starts_ref, bf16[2,2,3072]{2,1,0:T(2,128)(2,1)S(1)} %pad_maximum_fusion.16.scale_ref, bf16[3072,768]{1,0:T(8,128)(2,1)S(1)} %pad_maximum_fusion.2.weight_ref, bf16[512,1536]{1,0:T(8,128)(2,1)} %shard_map.133.refs_0_, ...), custom_call_target="tpu_custom_call" | custom-call | flops 7247757312 | bytes 9437184 | tf_op jit(solution)/shard_map/pallas_call | solution.py:218
  237.4 4.6 %collective-permute-done.26 = bf16[64,3072]{1,0:T(8,128)(2,1)S(1)} collective-permute-done((bf16[64,3072]{1,0:T(8,128)(2,1)S(1)}, bf16[64,3072]{1,0:T(8,128)(2,1)S(1)}, u32[]{:S(2)}, u32[]{:S(2)}) %collective-permute-start.26) | collective-permute-done | bytes 393248 | tf_op jit(solution)/shard_map/ppermute | solution.py:38
  245.5 6.7 %collective-permute-done.31.other_ref = bf16[64,3072]{1,0:T(8,128)(2,1)S(1)} collective-permute-done((bf16[64,3072]{1,0:T(8,128)(2,1)S(1)}, bf16[64,3072]{1,0:T(8,128)(2,1)S(1)}, u32[]{:S(2)}, u32[]{:S(2)}) %collective-permute-start.31) | collective-permute-done | bytes 393248 | tf_op jit(solution)/shard_map/ppermute | solution.py:88
  255.1 1.9 copy-done.35
  257.0 12.0 %shard_map.146 = f32[512,128]{1,0:T(8,128)S(1)} custom-call(f32[512,1152]{1,0:T(8,128)S(1)} %copy-done.9, f32[512,1152]{1,0:T(8,128)S(1)} %copy-done.9, f32[512,1152]{1,0:T(8,128)S(1)} %copy-done.9, f32[512,1152]{1,0:T(8,128)S(1)} %copy-done.11, f32[512,1152]{1,0:T(8,128)S(1)} %copy-done.11, f32[512,1152]{1,0:T(8,128)S(1)} %copy-done.11, ...), custom_call_target="tpu_custom_call" | custom-call | flops 14092861440 | bytes 13631488 | tf_op jit(solution)/shard_map/pallas_call | solution.py:522
  271.1 9.1 %shard_map.147.twin_sign_ref = bf16[2,512,768]{2,1,0:T(8,128)(2,1)S(1)} custom-call(s32[2]{0:T(128)S(1)} %pad_add_fusion.starts_ref, bf16[2,2,3072]{2,1,0:T(2,128)(2,1)S(1)} %pad_maximum_fusion.16.scale_ref, bf16[3072,768]{1,0:T(8,128)(2,1)S(1)} %pad_maximum_fusion.2.weight_ref, bf16[512,1536]{1,0:T(8,128)(2,1)} %shard_map.134.refs_0_, ...), custom_call_target="tpu_custom_call" | custom-call | flops 7247757312 | bytes 9437184 | tf_op jit(solution)/shard_map/pallas_call | solution.py:218
  282.4 3.7 %shard_map.148.twin_ref = f32[512,384]{1,0:T(8,128)S(1)} custom-call(bf16[512,3072]{1,0:T(8,128)(2,1)} %collective-permute-done.20.rows_ref, bf16[3072,384]{1,0:T(8,128)(2,1)S(1)} %copy-done.7), custom_call_target="tpu_custom_call" | custom-call | flops 1811939328 | bytes 6291456 | tf_op jit(solution)/shard_map/pallas_call | solution.py:245
  286.2 1.8 shard_map.149
  288.0 2.5 collective-permute-done.39.refs_6_
  293.7 2.6 collective-permute-done.40
  296.3 1.5 collective-permute-done.41
  299.1 2.8 shard_map.152
  302.6 1.7 collective-permute-start.43
  304.3 4.2 %fusion.30.q_ref.k_ref.v_ref = f32[512,1152]{1,0:T(8,128)S(1)} fusion(bf16[512,3072]{1,0:T(8,128)(2,1)S(1)} %get-tuple-element.75.normed_ref, bf16[3072,1152]{1,0:T(8,128)(2,1)S(1)} %bitcast.79), kind=kOutput, calls=%fused_computation.117 | convolution fusion | flops 3623878656 | bytes 12582912 | tf_op jit(solution)/shard_map/dot_general | solution.py:24
  312.1 4.2 %fusion.31.k_twin_ref.v_twin_ref.q_twin_ref = f32[512,1152]{1,0:T(8,128)S(1)} fusion(bf16[512,3072]{1,0:T(8,128)(2,1)S(1)} %collective-permute-done.42.rows_ref, bf16[3072,1152]{1,0:T(8,128)(2,1)S(1)} %bitcast.79), kind=kOutput, calls=%fused_computation.118 | convolution fusion | flops 3623878656 | bytes 12582912 | tf_op jit(solution)/shard_map/dot_general | solution.py:24
  316.4 2.9 shard_map.151
  319.3 1.8 shard_map.153.twin_ref
  321.1 1.8 shard_map.154
  325.0 1.8 collective-permute-start.46
  327.5 11.8 %shard_map.155 = f32[512,128]{1,0:T(8,128)S(1)} custom-call(f32[512,1152]{1,0:T(8,128)S(1)} %fusion.30.q_ref.k_ref.v_ref, f32[512,1152]{1,0:T(8,128)S(1)} %fusion.30.q_ref.k_ref.v_ref, f32[512,1152]{1,0:T(8,128)S(1)} %fusion.30.q_ref.k_ref.v_ref, f32[512,1152]{1,0:T(8,128)S(1)} %fusion.31.k_twin_ref.v_twin_ref.q_twin_ref, ...), custom_call_target="tpu_custom_call" | custom-call | flops 14092861440 | bytes 13631488 | tf_op jit(solution)/shard_map/pallas_call | solution.py:522
  343.4 3.3 all-to-all-start.1
  346.8 6.4 %all-to-all-done.1 = f32[8,1,128]{2,1,0:T(1,128)S(1)} async-done(((f32[8,1,128]{2,1,0:T(1,128)}), f32[8,1,128]{2,1,0:T(1,128)S(1)}, u32[]{:S(2)}, u32[]{:S(2)}) %all-to-all-start.1) | async-done | bytes 4128 | tf_op jit(solution)/shard_map/all_to_all | solution.py:666
  354.0 1.6 fusion.4
  356.9 5.3 %collective-permute-done.52 = bf16[64,1536]{1,0:T(8,128)(2,1)} collective-permute-done((bf16[64,1536]{1,0:T(8,128)(2,1)}, bf16[64,1536]{1,0:T(8,128)(2,1)}, u32[]{:S(2)}, u32[]{:S(2)}) %collective-permute-start.52) | collective-permute-done | bytes 196640 | tf_op jit(solution)/shard_map/ppermute | solution.py:88
  364.0 3.0 collective-permute-done.55
  (339 shorter events, 89.9 us)
Async XLA Ops:
  0.6 88.8 %copy-start = (bf16[3072,384]{1,0:T(8,128)(2,1)S(1)}, bf16[3072,384]{1,0:T(8,128)(2,1)}, u32[]{:S(2)}) copy-start(bf16[3072,384]{1,0:T(8,128)(2,1)} %param.19) | copy-start | bytes 7077892
  2.1 12.2 %collective-permute-start.7 = (bf16[128,1536]{1,0:T(8,128)(2,1)S(1)}, bf16[128,1536]{1,0:T(8,128)(2,1)S(1)}, u32[]{:S(2)}, u32[]{:S(2)}) collective-permute-start(bf16[128,1536]{1,0:T(8,128)(2,1)S(1)} %bitcast.86), channel_id=1, source_target_pairs={{0,4},{8,0},{16,8},{24,16},{28,24},{20,28},{12,20},{4,12},{1,5},{9... | collective-permute-start | bytes 1179656 | tf_op jit(solution)/shard_map/ppermute | solution.py:38
  5.2 10.9 %collective-permute-start.3 = (bf16[128,1536]{1,0:T(8,128)(2,1)S(1)}, bf16[128,1536]{1,0:T(8,128)(2,1)}, u32[]{:S(2)}, u32[]{:S(2)}) collective-permute-start(bf16[128,1536]{1,0:T(8,128)(2,1)S(1)} %bitcast.87), channel_id=1, source_target_pairs={{0,8},{8,16},{16,24},{24,28},{28,20},{20,12},{12,4},{4,0},{1,9},{9... | collective-permute-start | bytes 1179656 | tf_op jit(solution)/shard_map/ppermute | solution.py:38
  7.0 23.2 %collective-permute-start = (f32[64,1536]{1,0:T(8,128)}, f32[64,1536]{1,0:T(8,128)}, u32[]{:S(2)}, u32[]{:S(2)}) collective-permute-start(f32[64,1536]{1,0:T(8,128)} %constant_dynamic-slice_fusion.4.rows_ref), channel_id=1, source_target_pairs={{0,2},{2,0},{1,3},{3,1},{4,6},{6,4},{5,7},{7,5},{8,10},{10,8},{9,1... | collective-permute-start | bytes 1179656 | tf_op jit(solution)/shard_map/ppermute | solution.py:88
  9.7 14.2 %collective-permute-start.1 = (bf16[64,1536]{1,0:T(8,128)(2,1)}, bf16[64,1536]{1,0:T(8,128)(2,1)S(1)}, u32[]{:S(2)}, u32[]{:S(2)}) collective-permute-start(bf16[64,1536]{1,0:T(8,128)(2,1)} %get-tuple-element.117), channel_id=1, source_target_pairs={{0,1},{1,0},{2,3},{3,2},{4,5},{5,4},{6,7},{7,6},{8,9},{9,8},{10,11... | collective-permute-start | bytes 589832 | tf_op jit(solution)/shard_map/ppermute | solution.py:88
  14.3 13.9 %collective-permute-start.8 = (bf16[128,1536]{1,0:T(8,128)(2,1)S(1)}, bf16[128,1536]{1,0:T(8,128)(2,1)}, u32[]{:S(2)}, u32[]{:S(2)}) collective-permute-start(bf16[128,1536]{1,0:T(8,128)(2,1)S(1)} %collective-permute-done.7.refs_2_), channel_id=1, source_target_pairs={{0,4},{8,0},{16,8},{24,16},{28,24},{20,28},{12,20},{4,12},{1,5},{9... | collective-permute-start | bytes 1179656 | tf_op jit(solution)/shard_map/ppermute | solution.py:38
  16.0 13.8 %collective-permute-start.4 = (bf16[128,1536]{1,0:T(8,128)(2,1)}, bf16[128,1536]{1,0:T(8,128)(2,1)}, u32[]{:S(2)}, u32[]{:S(2)}) collective-permute-start(bf16[128,1536]{1,0:T(8,128)(2,1)} %collective-permute-done.3.refs_0_), channel_id=1, source_target_pairs={{0,8},{8,16},{16,24},{24,28},{28,20},{20,12},{12,4},{4,0},{1,9},{9... | collective-permute-start | bytes 1179656 | tf_op jit(solution)/shard_map/ppermute | solution.py:38
  26.6 15.5 %collective-permute-start.2 = (f32[64,128]{1,0:T(8,128)}, f32[64,128]{1,0:T(8,128)}, u32[]{:S(2)}, u32[]{:S(2)}) collective-permute-start(f32[64,128]{1,0:T(8,128)} %shard_map.131.own_ref), channel_id=1, source_target_pairs={{0,2},{2,0},{1,3},{3,1},{4,6},{6,4},{5,7},{7,5},{8,10},{10,8},{9,1... | collective-permute-start | bytes 98312 | tf_op jit(solution)/shard_map/ppermute | solution.py:88
  28.3 9.5 %collective-permute-start.9 = (bf16[128,1536]{1,0:T(8,128)(2,1)}, bf16[128,1536]{1,0:T(8,128)(2,1)S(1)}, u32[]{:S(2)}, u32[]{:S(2)}) collective-permute-start(bf16[128,1536]{1,0:T(8,128)(2,1)} %collective-permute-done.8.refs_3_), channel_id=1, source_target_pairs={{0,4},{8,0},{16,8},{24,16},{28,24},{20,28},{12,20},{4,12},{1,5},{9... | collective-permute-start | bytes 1179656 | tf_op jit(solution)/shard_map/ppermute | solution.py:38
  29.8 10.1 %collective-permute-start.5 = (bf16[128,1536]{1,0:T(8,128)(2,1)}, bf16[128,1536]{1,0:T(8,128)(2,1)S(1)}, u32[]{:S(2)}, u32[]{:S(2)}) collective-permute-start(bf16[128,1536]{1,0:T(8,128)(2,1)} %collective-permute-done.4.refs_7_), channel_id=1, source_target_pairs={{0,8},{8,16},{16,24},{24,28},{28,20},{20,12},{12,4},{4,0},{1,9},{9... | collective-permute-start | bytes 1179656 | tf_op jit(solution)/shard_map/ppermute | solution.py:38
  38.4 6.0 %collective-permute-start.10 = (bf16[128,768]{1,0:T(8,128)(2,1)}, bf16[128,768]{1,0:T(8,128)(2,1)}, u32[]{:S(2)}, u32[]{:S(2)}) collective-permute-start(bf16[128,768]{1,0:T(8,128)(2,1)} %split.25), channel_id=1, source_target_pairs={{0,4},{8,0},{16,8},{24,16},{28,24},{20,28},{12,20},{4,12},{1,5},{9... | collective-permute-start | bytes 589832 | tf_op jit(solution)/shard_map/ppermute | solution.py:38
  40.7 6.0 %collective-permute-start.6 = (bf16[128,768]{1,0:T(8,128)(2,1)}, bf16[128,768]{1,0:T(8,128)(2,1)}, u32[]{:S(2)}, u32[]{:S(2)}) collective-permute-start(bf16[128,768]{1,0:T(8,128)(2,1)} %split.24), channel_id=1, source_target_pairs={{0,8},{8,16},{16,24},{24,28},{28,20},{20,12},{12,4},{4,0},{1,9},{9... | collective-permute-start | bytes 589832 | tf_op jit(solution)/shard_map/ppermute | solution.py:38
  47.7 25.4 %collective-permute-start.11 = (bf16[64,3200]{1,0:T(8,128)(2,1)}, bf16[64,3200]{1,0:T(8,128)(2,1)}, u32[]{:S(2)}, u32[]{:S(2)}) collective-permute-start(bf16[64,3200]{1,0:T(8,128)(2,1)} %shard_map.132.refs_1_), channel_id=1, source_target_pairs={{0,8},{8,16},{16,24},{24,28},{28,20},{20,12},{12,4},{4,0},{1,9},{9... | collective-permute-start | bytes 1228808 | tf_op jit(solution)/shard_map/ppermute | solution.py:38
  48.3 25.6 %collective-permute-start.12 = (bf16[64,3200]{1,0:T(8,128)(2,1)}, bf16[64,3200]{1,0:T(8,128)(2,1)}, u32[]{:S(2)}, u32[]{:S(2)}) collective-permute-start(bf16[64,3200]{1,0:T(8,128)(2,1)} %shard_map.132.refs_1_), channel_id=1, source_target_pairs={{0,4},{8,0},{16,8},{24,16},{28,24},{20,28},{12,20},{4,12},{1,5},{9... | collective-permute-start | bytes 1228808 | tf_op jit(solution)/shard_map/ppermute | solution.py:38
  69.1 35.3 %collective-permute-start.19 = (bf16[512,1536]{1,0:T(8,128)(2,1)}, bf16[512,1536]{1,0:T(8,128)(2,1)}, u32[]{:S(2)}, u32[]{:S(2)}) collective-permute-start(bf16[512,1536]{1,0:T(8,128)(2,1)} %shard_map.133.refs_0_), channel_id=1, source_target_pairs={{0,2},{2,0},{1,3},{3,1},{4,6},{6,4},{5,7},{7,5},{8,10},{10,8},{9,1... | collective-permute-start | bytes 4718600 | tf_op jit(solution)/shard_map/ppermute | solution.py:88
  73.1 14.3 %collective-permute-start.15 = (bf16[64,3200]{1,0:T(8,128)(2,1)}, bf16[64,3200]{1,0:T(8,128)(2,1)}, u32[]{:S(2)}, u32[]{:S(2)}) collective-permute-start(bf16[64,3200]{1,0:T(8,128)(2,1)} %collective-permute-done.11.refs_0_), channel_id=1, source_target_pairs={{0,8},{8,16},{16,24},{24,28},{28,20},{20,12},{12,4},{4,0},{1,9},{9... | collective-permute-start | bytes 1228808 | tf_op jit(solution)/shard_map/ppermute | solution.py:38
  73.8 14.2 %collective-permute-start.13 = (bf16[64,3200]{1,0:T(8,128)(2,1)}, bf16[64,3200]{1,0:T(8,128)(2,1)}, u32[]{:S(2)}, u32[]{:S(2)}) collective-permute-start(bf16[64,3200]{1,0:T(8,128)(2,1)} %collective-permute-done.12.refs_2_), channel_id=1, source_target_pairs={{0,4},{8,0},{16,8},{24,16},{28,24},{20,28},{12,20},{4,12},{1,5},{9... | collective-permute-start | bytes 1228808 | tf_op jit(solution)/shard_map/ppermute | solution.py:38
  83.3 24.4 %copy-start.49 = (bf16[2,3,3072]{2,0,1:T(2,128)(2,1)}, bf16[2,3,3072]{2,0,1:T(2,128)(2,1)S(1)}, u32[]{:S(2)}) copy-start(bf16[2,3,3072]{2,0,1:T(2,128)(2,1)S(1)} %convert.21) | copy-start | bytes 110596
  87.4 10.4 %collective-permute-start.16 = (bf16[64,3200]{1,0:T(8,128)(2,1)}, bf16[64,3200]{1,0:T(8,128)(2,1)S(1)}, u32[]{:S(2)}, u32[]{:S(2)}) collective-permute-start(bf16[64,3200]{1,0:T(8,128)(2,1)} %collective-permute-done.15.refs_7_), channel_id=1, source_target_pairs={{0,8},{8,16},{16,24},{24,28},{28,20},{20,12},{12,4},{4,0},{1,9},{9... | collective-permute-start | bytes 1228808 | tf_op jit(solution)/shard_map/ppermute | solution.py:38
  88.1 10.4 %collective-permute-start.14 = (bf16[64,3200]{1,0:T(8,128)(2,1)}, bf16[64,3200]{1,0:T(8,128)(2,1)S(1)}, u32[]{:S(2)}, u32[]{:S(2)}) collective-permute-start(bf16[64,3200]{1,0:T(8,128)(2,1)} %collective-permute-done.13.refs_3_), channel_id=1, source_target_pairs={{0,4},{8,0},{16,8},{24,16},{28,24},{20,28},{12,20},{4,12},{1,5},{9... | collective-permute-start | bytes 1228808 | tf_op jit(solution)/shard_map/ppermute | solution.py:38
  97.8 5.8 %collective-permute-start.17 = (bf16[32,3200]{1,0:T(8,128)(2,1)S(1)}, bf16[32,3200]{1,0:T(8,128)(2,1)S(1)}, u32[]{:S(2)}, u32[]{:S(2)}) collective-permute-start(bf16[32,3200]{1,0:T(8,128)(2,1)S(1)} %split.26), channel_id=1, source_target_pairs={{0,8},{8,16},{16,24},{24,28},{28,20},{20,12},{12,4},{4,0},{1,9},{9... | collective-permute-start | bytes 614408 | tf_op jit(solution)/shard_map/ppermute | solution.py:38
  98.5 5.8 %collective-permute-start.18 = (bf16[32,3200]{1,0:T(8,128)(2,1)S(1)}, bf16[32,3200]{1,0:T(8,128)(2,1)S(1)}, u32[]{:S(2)}, u32[]{:S(2)}) collective-permute-start(bf16[32,3200]{1,0:T(8,128)(2,1)S(1)} %split.27), channel_id=1, source_target_pairs={{0,4},{8,0},{16,8},{24,16},{28,24},{20,28},{12,20},{4,12},{1,5},{9... | collective-permute-start | bytes 614408 | tf_op jit(solution)/shard_map/ppermute | solution.py:38
  107.6 22.7 %collective-permute-start.20 = (bf16[512,3072]{1,0:T(8,128)(2,1)}, bf16[512,3072]{1,0:T(8,128)(2,1)}, u32[]{:S(2)}, u32[]{:S(2)}) collective-permute-start(bf16[512,3072]{1,0:T(8,128)(2,1)} %get-tuple-element.50.rows_ref.normed_ref), channel_id=1, source_target_pairs={{0,1},{1,0},{2,3},{3,2},{4,5},{5,4},{6,7},{7,6},{8,9},{9,8},{10,11... | collective-permute-start | bytes 9437192 | tf_op jit(solution)/shard_map/ppermute | solution.py:88
  108.5 54.1 %collective-permute-start.21 = (bf16[512,1536]{1,0:T(8,128)(2,1)}, bf16[512,1536]{1,0:T(8,128)(2,1)}, u32[]{:S(2)}, u32[]{:S(2)}) collective-permute-start(bf16[512,1536]{1,0:T(8,128)(2,1)} %shard_map.134.refs_0_), channel_id=1, source_target_pairs={{0,2},{2,0},{1,3},{3,1},{4,6},{6,4},{5,7},{7,5},{8,10},{10,8},{9,1... | collective-permute-start | bytes 4718600 | tf_op jit(solution)/shard_map/ppermute | solution.py:88
  112.2 68.7 %all-to-all-start = ((bf16[8,2,192,384]{3,2,1,0:T(8,128)(2,1)}), bf16[8,2,192,384]{3,2,1,0:T(8,128)(2,1)}, u32[]{:S(2)}, u32[]{:S(2)}) async-start(bf16[8,2,192,384]{3,2,1,0:T(8,128)(2,1)} %pad_maximum_fusion.3), calls=%async_computation | async-start | bytes 4718592 | tf_op jit(solution)/shard_map/all_to_all | solution.py:721
  162.6 18.4 %copy-start.50 = (bf16[2,3,3072]{2,0,1:T(2,128)(2,1)S(1)}, bf16[2,3,3072]{2,0,1:T(2,128)(2,1)}, u32[]{:S(2)}) copy-start(bf16[2,3,3072]{2,0,1:T(2,128)(2,1)} %copy-done.49) | copy-start | bytes 110596
  162.6 18.4 %copy-start.60 = (bf16[2,1,3072]{2,0,1:T(2,128)(2,1)S(1)}, bf16[2,1,3072]{2,0,1:T(2,128)(2,1)}, u32[]{:S(2)}) copy-start(bf16[2,1,3072]{2,0,1:T(2,128)(2,1)} %add_convert_fusion.7) | copy-start | bytes 36868
  180.9 6.4 %collective-permute-start.22 = (bf16[8,2,192,384]{3,2,1,0:T(8,128)(2,1)}, bf16[8,2,192,384]{3,2,1,0:T(8,128)(2,1)S(1)}, u32[]{:S(2)}, u32[]{:S(2)}) collective-permute-start(bf16[8,2,192,384]{3,2,1,0:T(8,128)(2,1)} %all-to-all-done.own_ref), channel_id=1, source_target_pairs={{0,1},{1,0},{2,3},{3,2},{4,5},{5,4},{6,7},{7,6},{8,9},{9,8},{10,11... | collective-permute-start | bytes 7077896 | tf_op jit(solution)/shard_map/ppermute | solution.py:88
  196.8 7.6 %collective-permute-start.23 = (bf16[64,1536]{1,0:T(8,128)(2,1)S(1)}, bf16[64,1536]{1,0:T(8,128)(2,1)S(1)}, u32[]{:S(2)}, u32[]{:S(2)}) collective-permute-start(bf16[64,1536]{1,0:T(8,128)(2,1)S(1)} %get-tuple-element.109), channel_id=1, source_target_pairs={{0,8},{8,16},{16,24},{24,28},{28,20},{20,12},{12,4},{4,0},{1,9},{9... | collective-permute-start | bytes 589832 | tf_op jit(solution)/shard_map/ppermute | solution.py:38
  198.8 7.0 %collective-permute-start.27 = (bf16[64,1536]{1,0:T(8,128)(2,1)S(1)}, bf16[64,1536]{1,0:T(8,128)(2,1)S(1)}, u32[]{:S(2)}, u32[]{:S(2)}) collective-permute-start(bf16[64,1536]{1,0:T(8,128)(2,1)S(1)} %get-tuple-element.110), channel_id=1, source_target_pairs={{0,4},{8,0},{16,8},{24,16},{28,24},{20,28},{12,20},{4,12},{1,5},{9... | collective-permute-start | bytes 589832 | tf_op jit(solution)/shard_map/ppermute | solution.py:38
  206.8 14.5 %collective-permute-start.24 = (bf16[64,3072]{1,0:T(8,128)(2,1)}, bf16[64,3072]{1,0:T(8,128)(2,1)}, u32[]{:S(2)}, u32[]{:S(2)}) collective-permute-start(bf16[64,3072]{1,0:T(8,128)(2,1)} %pad_maximum_fusion.9), channel_id=1, source_target_pairs={{0,8},{8,16},{16,24},{24,28},{28,20},{20,12},{12,4},{4,0},{1,9},{9... | collective-permute-start | bytes 1179656 | tf_op jit(solution)/shard_map/ppermute | solution.py:38
  209.0 10.5 %collective-permute-start.28 = (bf16[64,3072]{1,0:T(8,128)(2,1)}, bf16[64,3072]{1,0:T(8,128)(2,1)}, u32[]{:S(2)}, u32[]{:S(2)}) collective-permute-start(bf16[64,3072]{1,0:T(8,128)(2,1)} %pad_maximum_fusion.10), channel_id=1, source_target_pairs={{0,4},{8,0},{16,8},{24,16},{28,24},{20,28},{12,20},{4,12},{1,5},{9... | collective-permute-start | bytes 1179656 | tf_op jit(solution)/shard_map/ppermute | solution.py:38
  220.7 12.4 %collective-permute-start.29 = (bf16[64,3072]{1,0:T(8,128)(2,1)S(1)}, bf16[64,3072]{1,0:T(8,128)(2,1)S(1)}, u32[]{:S(2)}, u32[]{:S(2)}) collective-permute-start(bf16[64,3072]{1,0:T(8,128)(2,1)S(1)} %add_convert_fusion.1), channel_id=1, source_target_pairs={{0,4},{8,0},{16,8},{24,16},{28,24},{20,28},{12,20},{4,12},{1,5},{9... | collective-permute-start | bytes 1179656 | tf_op jit(solution)/shard_map/ppermute | solution.py:38
  222.3 10.7 %collective-permute-start.25 = (bf16[64,3072]{1,0:T(8,128)(2,1)S(1)}, bf16[64,3072]{1,0:T(8,128)(2,1)S(1)}, u32[]{:S(2)}, u32[]{:S(2)}) collective-permute-start(bf16[64,3072]{1,0:T(8,128)(2,1)S(1)} %fusion.6), channel_id=1, source_target_pairs={{0,8},{8,16},{16,24},{24,28},{28,20},{20,12},{12,4},{4,0},{1,9},{9... | collective-permute-start | bytes 1179656 | tf_op jit(solution)/shard_map/ppermute | solution.py:38
  233.0 22.1 %copy-start.33 = (bf16[2,512,1536]{2,1,0:T(8,128)(2,1)S(1)}, bf16[2,512,1536]{2,1,0:T(8,128)(2,1)}, u32[]{:S(2)}) copy-start(bf16[2,512,1536]{2,1,0:T(8,128)(2,1)} %copy-done.32) | copy-start | bytes 9437188
  233.2 8.7 %collective-permute-start.26 = (bf16[64,3072]{1,0:T(8,128)(2,1)S(1)}, bf16[64,3072]{1,0:T(8,128)(2,1)S(1)}, u32[]{:S(2)}, u32[]{:S(2)}) collective-permute-start(bf16[64,3072]{1,0:T(8,128)(2,1)S(1)} %get-tuple-element.99), channel_id=1, source_target_pairs={{0,8},{8,16},{16,24},{24,28},{28,20},{20,12},{12,4},{4,0},{1,9},{9... | collective-permute-start | bytes 1179656 | tf_op jit(solution)/shard_map/ppermute | solution.py:38
  234.7 8.4 %collective-permute-start.30 = (bf16[64,3072]{1,0:T(8,128)(2,1)S(1)}, bf16[64,3072]{1,0:T(8,128)(2,1)S(1)}, u32[]{:S(2)}, u32[]{:S(2)}) collective-permute-start(bf16[64,3072]{1,0:T(8,128)(2,1)S(1)} %get-tuple-element.100), channel_id=1, source_target_pairs={{0,4},{8,0},{16,8},{24,16},{28,24},{20,28},{12,20},{4,12},{1,5},{9... | collective-permute-start | bytes 1179656 | tf_op jit(solution)/shard_map/ppermute | solution.py:38
  236.8 8.8 %collective-permute-start.32 = (bf16[64,3072]{1,0:T(8,128)(2,1)S(1)}, bf16[64,3072]{1,0:T(8,128)(2,1)S(1)}, u32[]{:S(2)}, u32[]{:S(2)}) collective-permute-start(bf16[64,3072]{1,0:T(8,128)(2,1)S(1)} %pad_maximum_fusion.12), channel_id=1, source_target_pairs={{0,1},{1,0},{2,3},{3,2},{4,5},{5,4},{6,7},{7,6},{8,9},{9,8},{10,11... | collective-permute-start | bytes 1179656 | tf_op jit(solution)/shard_map/ppermute | solution.py:88
  236.9 18.2 %collective-permute-start.35 = (bf16[512,128]{1,0:T(8,128)(2,1)S(1)}, bf16[512,128]{1,0:T(8,128)(2,1)S(1)}, u32[]{:S(2)}, u32[]{:S(2)}) collective-permute-start(bf16[512,128]{1,0:T(8,128)(2,1)S(1)} %copy-done.29), channel_id=1, source_target_pairs={{0,1},{1,0},{2,3},{3,2},{4,5},{5,4},{6,7},{7,6},{8,9},{9,8},{10,11... | collective-permute-start | bytes 393224 | tf_op jit(solution)/shard_map/ppermute | solution.py:88
  244.4 7.8 %collective-permute-start.31 = (bf16[64,3072]{1,0:T(8,128)(2,1)S(1)}, bf16[64,3072]{1,0:T(8,128)(2,1)S(1)}, u32[]{:S(2)}, u32[]{:S(2)}) collective-permute-start(bf16[64,3072]{1,0:T(8,128)(2,1)S(1)} %fusion.9.own_ref), channel_id=1, source_target_pairs={{0,2},{2,0},{1,3},{3,1},{4,6},{6,4},{5,7},{7,5},{8,10},{10,8},{9,1... | collective-permute-start | bytes 1179656 | tf_op jit(solution)/shard_map/ppermute | solution.py:88
  253.0 16.0 %collective-permute-start.33 = (bf16[64,3200]{1,0:T(8,128)(2,1)S(1)}, bf16[64,3200]{1,0:T(8,128)(2,1)S(1)}, u32[]{:S(2)}, u32[]{:S(2)}) collective-permute-start(bf16[64,3200]{1,0:T(8,128)(2,1)S(1)} %get-tuple-element.63.refs_1_), channel_id=1, source_target_pairs={{0,8},{8,16},{16,24},{24,28},{28,20},{20,12},{12,4},{4,0},{1,9},{9... | collective-permute-start | bytes 1228808 | tf_op jit(solution)/shard_map/ppermute | solution.py:38
  254.5 16.0 %collective-permute-start.34 = (bf16[64,3200]{1,0:T(8,128)(2,1)S(1)}, bf16[64,3200]{1,0:T(8,128)(2,1)S(1)}, u32[]{:S(2)}, u32[]{:S(2)}) collective-permute-start(bf16[64,3200]{1,0:T(8,128)(2,1)S(1)} %get-tuple-element.63.refs_1_), channel_id=1, source_target_pairs={{0,4},{8,0},{16,8},{24,16},{28,24},{20,28},{12,20},{4,12},{1,5},{9... | collective-permute-start | bytes 1228808 | tf_op jit(solution)/shard_map/ppermute | solution.py:38
  269.0 11.2 %collective-permute-start.38 = (bf16[64,3200]{1,0:T(8,128)(2,1)S(1)}, bf16[64,3200]{1,0:T(8,128)(2,1)S(1)}, u32[]{:S(2)}, u32[]{:S(2)}) collective-permute-start(bf16[64,3200]{1,0:T(8,128)(2,1)S(1)} %collective-permute-done.33.refs_0_), channel_id=1, source_target_pairs={{0,8},{8,16},{16,24},{24,28},{28,20},{20,12},{12,4},{4,0},{1,9},{9... | collective-permute-start | bytes 1228808 | tf_op jit(solution)/shard_map/ppermute | solution.py:38
  270.6 11.2 %collective-permute-start.36 = (bf16[64,3200]{1,0:T(8,128)(2,1)S(1)}, bf16[64,3200]{1,0:T(8,128)(2,1)S(1)}, u32[]{:S(2)}, u32[]{:S(2)}) collective-permute-start(bf16[64,3200]{1,0:T(8,128)(2,1)S(1)} %collective-permute-done.34.refs_2_), channel_id=1, source_target_pairs={{0,4},{8,0},{16,8},{24,16},{28,24},{20,28},{12,20},{4,12},{1,5},{9... | collective-permute-start | bytes 1228808 | tf_op jit(solution)/shard_map/ppermute | solution.py:38
  280.3 10.2 %collective-permute-start.39 = (bf16[64,3200]{1,0:T(8,128)(2,1)S(1)}, bf16[64,3200]{1,0:T(8,128)(2,1)S(1)}, u32[]{:S(2)}, u32[]{:S(2)}) collective-permute-start(bf16[64,3200]{1,0:T(8,128)(2,1)S(1)} %collective-permute-done.38.refs_7_), channel_id=1, source_target_pairs={{0,8},{8,16},{16,24},{24,28},{28,20},{20,12},{12,4},{4,0},{1,9},{9... | collective-permute-start | bytes 1228808 | tf_op jit(solution)/shard_map/ppermute | solution.py:38
  281.8 10.2 %collective-permute-start.37 = (bf16[64,3200]{1,0:T(8,128)(2,1)S(1)}, bf16[64,3200]{1,0:T(8,128)(2,1)S(1)}, u32[]{:S(2)}, u32[]{:S(2)}) collective-permute-start(bf16[64,3200]{1,0:T(8,128)(2,1)S(1)} %collective-permute-done.36.refs_3_), channel_id=1, source_target_pairs={{0,4},{8,0},{16,8},{24,16},{28,24},{20,28},{12,20},{4,12},{1,5},{9... | collective-permute-start | bytes 1228808 | tf_op jit(solution)/shard_map/ppermute | solution.py:38
  290.5 5.8 %collective-permute-start.40 = (bf16[32,3200]{1,0:T(8,128)(2,1)S(1)}, bf16[32,3200]{1,0:T(8,128)(2,1)S(1)}, u32[]{:S(2)}, u32[]{:S(2)}) collective-permute-start(bf16[32,3200]{1,0:T(8,128)(2,1)S(1)} %split.22), channel_id=1, source_target_pairs={{0,8},{8,16},{16,24},{24,28},{28,20},{20,12},{12,4},{4,0},{1,9},{9... | collective-permute-start | bytes 614408 | tf_op jit(solution)/shard_map/ppermute | solution.py:38
  292.1 5.8 %collective-permute-start.41 = (bf16[32,3200]{1,0:T(8,128)(2,1)S(1)}, bf16[32,3200]{1,0:T(8,128)(2,1)S(1)}, u32[]{:S(2)}, u32[]{:S(2)}) collective-permute-start(bf16[32,3200]{1,0:T(8,128)(2,1)S(1)} %split.23), channel_id=1, source_target_pairs={{0,4},{8,0},{16,8},{24,16},{28,24},{20,28},{12,20},{4,12},{1,5},{9... | collective-permute-start | bytes 614408 | tf_op jit(solution)/shard_map/ppermute | solution.py:38
  298.4 13.7 %collective-permute-start.42 = (bf16[512,3072]{1,0:T(8,128)(2,1)S(1)}, bf16[512,3072]{1,0:T(8,128)(2,1)S(1)}, u32[]{:S(2)}, u32[]{:S(2)}) collective-permute-start(bf16[512,3072]{1,0:T(8,128)(2,1)S(1)} %get-tuple-element.75.normed_ref), channel_id=1, source_target_pairs={{0,1},{1,0},{2,3},{3,2},{4,5},{5,4},{6,7},{7,6},{8,9},{9,8},{10,11... | collective-permute-start | bytes 9437192 | tf_op jit(solution)/shard_map/ppermute | solution.py:88
  302.0 7.3 %collective-permute-start.48 = (bf16[64,1536]{1,0:T(8,128)(2,1)S(1)}, bf16[64,1536]{1,0:T(8,128)(2,1)S(1)}, u32[]{:S(2)}, u32[]{:S(2)}) collective-permute-start(bf16[64,1536]{1,0:T(8,128)(2,1)S(1)} %get-tuple-element.104), channel_id=1, source_target_pairs={{0,4},{8,0},{16,8},{24,16},{28,24},{20,28},{12,20},{4,12},{1,5},{9... | collective-permute-start | bytes 589832 | tf_op jit(solution)/shard_map/ppermute | solution.py:38
  302.6 7.2 %collective-permute-start.43 = (bf16[64,1536]{1,0:T(8,128)(2,1)S(1)}, bf16[64,1536]{1,0:T(8,128)(2,1)S(1)}, u32[]{:S(2)}, u32[]{:S(2)}) collective-permute-start(bf16[64,1536]{1,0:T(8,128)(2,1)S(1)} %get-tuple-element.103), channel_id=1, source_target_pairs={{0,8},{8,16},{16,24},{24,28},{28,20},{20,12},{12,4},{4,0},{1,9},{9... | collective-permute-start | bytes 589832 | tf_op jit(solution)/shard_map/ppermute | solution.py:38
  308.5 12.6 %collective-permute-start.45 = (bf16[512,128]{1,0:T(8,128)(2,1)S(1)}, bf16[512,128]{1,0:T(8,128)(2,1)S(1)}, u32[]{:S(2)}, u32[]{:S(2)}) collective-permute-start(bf16[512,128]{1,0:T(8,128)(2,1)S(1)} %get-tuple-element.81.own_tail_ref.tail_ref), channel_id=1, source_target_pairs={{0,1},{1,0},{2,3},{3,2},{4,5},{5,4},{6,7},{7,6},{8,9},{9,8},{10,11... | collective-permute-start | bytes 393224 | tf_op jit(solution)/shard_map/ppermute | solution.py:88
  310.0 13.9 %collective-permute-start.44 = (bf16[64,3072]{1,0:T(8,128)(2,1)S(1)}, bf16[64,3072]{1,0:T(8,128)(2,1)S(1)}, u32[]{:S(2)}, u32[]{:S(2)}) collective-permute-start(bf16[64,3072]{1,0:T(8,128)(2,1)S(1)} %pad_maximum_fusion.13), channel_id=1, source_target_pairs={{0,8},{8,16},{16,24},{24,28},{28,20},{20,12},{12,4},{4,0},{1,9},{9... | collective-permute-start | bytes 1179656 | tf_op jit(solution)/shard_map/ppermute | solution.py:38
  311.5 15.2 %collective-permute-start.49 = (bf16[64,3072]{1,0:T(8,128)(2,1)S(1)}, bf16[64,3072]{1,0:T(8,128)(2,1)S(1)}, u32[]{:S(2)}, u32[]{:S(2)}) collective-permute-start(bf16[64,3072]{1,0:T(8,128)(2,1)S(1)} %pad_maximum_fusion.14), channel_id=1, source_target_pairs={{0,4},{8,0},{16,8},{24,16},{28,24},{20,28},{12,20},{4,12},{1,5},{9... | collective-permute-start | bytes 1179656 | tf_op jit(solution)/shard_map/ppermute | solution.py:38
  325.0 14.4 %collective-permute-start.46 = (bf16[64,3072]{1,0:T(8,128)(2,1)S(1)}, bf16[64,3072]{1,0:T(8,128)(2,1)S(1)}, u32[]{:S(2)}, u32[]{:S(2)}) collective-permute-start(bf16[64,3072]{1,0:T(8,128)(2,1)S(1)} %fusion.1), channel_id=1, source_target_pairs={{0,8},{8,16},{16,24},{24,28},{28,20},{20,12},{12,4},{4,0},{1,9},{9... | collective-permute-start | bytes 1179656 | tf_op jit(solution)/shard_map/ppermute | solution.py:38
  326.9 12.5 %collective-permute-start.50 = (bf16[64,3072]{1,0:T(8,128)(2,1)S(1)}, bf16[64,3072]{1,0:T(8,128)(2,1)S(1)}, u32[]{:S(2)}, u32[]{:S(2)}) collective-permute-start(bf16[64,3072]{1,0:T(8,128)(2,1)S(1)} %add_convert_fusion), channel_id=1, source_target_pairs={{0,4},{8,0},{16,8},{24,16},{28,24},{20,28},{12,20},{4,12},{1,5},{9... | collective-permute-start | bytes 1179656 | tf_op jit(solution)/shard_map/ppermute | solution.py:38
  339.5 22.7 %copy-start.26 = (f32[64,3072]{1,0:T(8,128)S(1)}, f32[64,3072]{1,0:T(8,128)}, u32[]{:S(2)}) copy-start(f32[64,3072]{1,0:T(8,128)} %copy-done.25) | copy-start | bytes 2359300
  339.6 13.6 %collective-permute-start.47 = (bf16[64,3072]{1,0:T(8,128)(2,1)S(1)}, bf16[64,3072]{1,0:T(8,128)(2,1)S(1)}, u32[]{:S(2)}, u32[]{:S(2)}) collective-permute-start(bf16[64,3072]{1,0:T(8,128)(2,1)S(1)} %get-tuple-element.93), channel_id=1, source_target_pairs={{0,8},{8,16},{16,24},{24,28},{28,20},{20,12},{12,4},{4,0},{1,9},{9... | collective-permute-start | bytes 1179656 | tf_op jit(solution)/shard_map/ppermute | solution.py:38
  341.1 12.9 %collective-permute-start.51 = (bf16[64,3072]{1,0:T(8,128)(2,1)S(1)}, bf16[64,3072]{1,0:T(8,128)(2,1)}, u32[]{:S(2)}, u32[]{:S(2)}) collective-permute-start(bf16[64,3072]{1,0:T(8,128)(2,1)S(1)} %get-tuple-element.94), channel_id=1, source_target_pairs={{0,4},{8,0},{16,8},{24,16},{28,24},{20,28},{12,20},{4,12},{1,5},{9... | collective-permute-start | bytes 1179656 | tf_op jit(solution)/shard_map/ppermute | solution.py:38
  343.4 9.7 %all-to-all-start.1 = ((f32[8,1,128]{2,1,0:T(1,128)}), f32[8,1,128]{2,1,0:T(1,128)S(1)}, u32[]{:S(2)}, u32[]{:S(2)}) async-start(f32[8,1,128]{2,1,0:T(1,128)} %bitcast.28), calls=%async_computation.1 | async-start | bytes 8192 | tf_op jit(solution)/shard_map/all_to_all | solution.py:666
  356.3 6.0 %collective-permute-start.52 = (bf16[64,1536]{1,0:T(8,128)(2,1)}, bf16[64,1536]{1,0:T(8,128)(2,1)}, u32[]{:S(2)}, u32[]{:S(2)}) collective-permute-start(bf16[64,1536]{1,0:T(8,128)(2,1)} %constant_dynamic-slice_fusion), channel_id=1, source_target_pairs={{0,2},{2,0},{1,3},{3,1},{4,6},{6,4},{5,7},{7,5},{8,10},{10,8},{9,1... | collective-permute-start | bytes 589832 | tf_op jit(solution)/shard_map/ppermute | solution.py:88
  356.8 6.5 %collective-permute-start.54 = (f32[1,128]{1,0:T(1,128)S(1)}, f32[1,128]{1,0:T(1,128)S(1)}, u32[]{:S(2)}, u32[]{:S(2)}) collective-permute-start(f32[1,128]{1,0:T(1,128)S(1)} %bitcast.99), channel_id=1, source_target_pairs={{0,1},{1,0},{2,3},{3,2},{4,5},{5,4},{6,7},{7,6},{8,9},{9,8},{10,11... | collective-permute-start | bytes 1544 | tf_op jit(solution)/shard_map/ppermute | solution.py:88
  363.3 4.2 %collective-permute-start.53 = (f32[64,1536]{1,0:T(8,128)S(1)}, f32[64,1536]{1,0:T(8,128)S(1)}, u32[]{:S(2)}, u32[]{:S(2)}) collective-permute-start(f32[64,1536]{1,0:T(8,128)S(1)} %multiply_add_fusion), channel_id=1, source_target_pairs={{0,1},{1,0},{2,3},{3,2},{4,5},{5,4},{6,7},{7,6},{8,9},{9,8},{10,11... | collective-permute-start | bytes 1179656 | tf_op jit(solution)/shard_map/ppermute | solution.py:88
  363.4 3.6 collective-permute-start.55
  (66 other events, 479.8 us)
